TPU v7x, 256 devices: a whole 4x4x8 slice. The times are simulated.
256 devices in a mesh: arc: 8 (over z_lo, core), par: 32 (over z_hi, x, y).
Axes of the slice: x: 4, y: 4, z: 8 (z_hi: 2, z_lo: 4; z = z_hi * 4 + z_lo), core: 2. Of those that a mesh axis runs over, the one named last changes fastest.
Arguments:
- design: bfloat16 [16, 1024, 40960], P('arc', None, 'par'), may hold values from -0.1875 to 0.1875
- cov_factor: float32 [16, 1024, 1024], P('arc', 'par'), may hold values from -1 to 3, as said below
- active_blocks: int32 [16, 80], P('arc'), may hold values from 0 to 159, all different within a row
- panel_index: int32 [1], replicated, may hold values from 0 to 79
- reg_diag: float32 [40960], replicated, may hold values from 0.5 to 4
Outputs:
- solved: float32 [512, 40960], P(None, ('par', 'arc'))
Inputs may be any that keep to these rules, and one draw needn't show every extreme that they name: Each cov_factor[a] is lower triangular with a positive diagonal.
All inputs are finite; a program needn't handle non-finite values.
Results may differ from a plain program's by a relative error of at most 0.0032.
Values may be sent and summed in bfloat16 or wider, within the bound.
A program may use at most 192 MiB of HBM per device.

v0:
```python
import jax
import jax.numpy as jnp
from jax import lax
from jax.sharding import Mesh
from jax.sharding import PartitionSpec as P

PANEL = 512
BLK = 256
PAR = ("par_0", "par_1", "par_2")
PAR_ARC = ("par_0", "par_1", "par_2", "arc")


def in_blocks(shard, dim, count):
    before, after = (shard.shape[:dim], shard.shape[dim + 1 :])
    return jnp.moveaxis(shard.reshape(*before, count, -1, *after), dim, 0)


def sum_at_owner(shard, axis, dim):
    tiles = in_blocks(shard, dim, lax.axis_size(axis))
    arrived = lax.all_to_all(tiles, axis, split_axis=0, concat_axis=0, tiled=True)
    return arrived.astype(jnp.float32).sum(axis=0)


def sum_in_two_steps(shard, axes, dim):
    far, near = axes
    own = sum_at_owner(in_blocks(shard, dim, lax.axis_size(far)), near, dim + 1)
    return jnp.sum(
        lax.all_to_all(own.astype(jnp.bfloat16), far, 0, 0, tiled=True).astype(jnp.float32), axis=0
    )


def rows_for(lines, count):
    spare = -len(lines) % count
    return jnp.pad(lines, [(0, spare)] + [(0, 0)] * (lines.ndim - 1))


def from_everyone(shard, axis):
    copies = jnp.broadcast_to(shard, (lax.axis_size(axis), *shard.shape))
    return lax.all_to_all(copies, axis, split_axis=0, concat_axis=0, tiled=True)


def joined_along(tiles, dim):
    lengths = list(tiles.shape[1:])
    lengths[dim] *= tiles.shape[0]
    return jnp.moveaxis(tiles, 0, dim).reshape(lengths)


def whole_of(shard, axes, dim):
    far, near = axes
    first = from_everyone(shard, far)
    tiles = jnp.swapaxes(from_everyone(first, near), 0, 1)
    return joined_along(tiles.reshape(-1, *shard.shape), dim)


def sum_by_parts(shard, axes):
    lines = shard.reshape(-1, shard.shape[-1])
    own = sum_in_two_steps(
        rows_for(lines, lax.axis_size(axes[0]) * lax.axis_size(axes[1])), axes, 0
    )
    whole = whole_of(own.astype(jnp.bfloat16), axes, 0)
    return whole[: len(lines)].reshape(shard.shape).astype(jnp.float32)


def summed_on_arrival(shard, axis, dim):
    tiles = in_blocks(shard, dim, lax.axis_size(axis))
    arrived = lax.all_to_all(tiles, axis, split_axis=0, concat_axis=0, tiled=True)
    return arrived.sum(axis=0)


def whiten(factor, rhs):
    size = factor.shape[0]
    step = min(128, size)
    pieces = []
    for index in range(size // step):
        low = index * step
        accum = rhs[low : low + step]
        if index > 0:
            done = jnp.concatenate(pieces, axis=0)
            accum = accum - jnp.dot(
                factor[low : low + step, :low],
                done,
                precision=lax.Precision.HIGHEST,
                preferred_element_type=jnp.float32,
            )
        pieces.append(
            lax.linalg.triangular_solve(
                factor[low : low + step, low : low + step], accum, left_side=True, lower=True
            )
        )
    return jnp.concatenate(pieces, axis=0)


def on_device(design, cov_factor, active_blocks, panel_index, reg_diag):
    arcs, observed, columns = design.shape
    local_blocks = columns // BLK
    par_id = lax.axis_index(PAR)
    arc_id = lax.axis_index("arc")
    factor = lax.all_gather(cov_factor, PAR, axis=1, tiled=True)
    block_ids = par_id * local_blocks + jnp.arange(local_blocks, dtype=jnp.int32)
    hits = jnp.any(active_blocks[:, :, None] == block_ids[None, None, :], axis=1)
    col_mask = jnp.repeat(hits, BLK, axis=1).astype(jnp.bfloat16)
    masked = design * col_mask[:, None, :]
    whitened = jnp.stack(
        [
            whiten(factor[arc], masked[arc].astype(jnp.float32)).astype(jnp.bfloat16)
            for arc in range(arcs)
        ]
    )
    start = panel_index[0] * PANEL
    offset = start - par_id * columns
    padded = jnp.pad(whitened, ((0, 0), (0, 0), (PANEL, PANEL)))
    window = lax.dynamic_slice_in_dim(
        padded, jnp.clip(offset + PANEL, 0, columns + PANEL), PANEL, 2
    )
    panel = sum_by_parts(
        window.astype(jnp.float32).astype(jnp.bfloat16), ("par_0", ("par_1", "par_2"))
    ).astype(jnp.bfloat16)
    gram = jnp.einsum("aop,aoc->pc", panel, whitened, preferred_element_type=jnp.float32)
    block = jnp.einsum("aop,aoq->pq", panel, panel, preferred_element_type=jnp.float32)
    share = columns // lax.axis_size("arc")
    gram = summed_on_arrival(gram, "arc", 1)
    block = lax.psum(block, "arc")
    reg_panel = lax.dynamic_slice_in_dim(reg_diag, start, PANEL)
    lower11 = jnp.linalg.cholesky(block + jnp.diag(reg_panel))
    global_cols = par_id * columns + arc_id * share + jnp.arange(share, dtype=jnp.int32)
    rows_at = start + jnp.arange(PANEL, dtype=jnp.int32)
    shifted = gram + jnp.where(
        global_cols[None, :] == rows_at[:, None], reg_panel[:, None], jnp.float32(0.0)
    )
    return whiten(lower11, shifted)


def solution(mesh):
    split = Mesh(
        mesh.devices.reshape(mesh.shape["arc"], 2, 4, 4), ("arc", "par_0", "par_1", "par_2")
    )
    return jax.shard_map(
        on_device,
        mesh=split,
        in_specs=(P("arc", None, PAR), P("arc", PAR, None), P("arc", None), P(), P()),
        out_specs=P(None, PAR_ARC),
        check_vma=False,
    )
```

profile of v0, /device:TPU:1, one launch (start us, length us, event | category | flops | bytes accessed | tf_op | source)
XLA Modules:
  0.0 815.6 jit_solution(5755372639396352478)
XLA Ops:
  24.3 141.0 %all-gather.2.cloned.1.call-done = f32[2,1024,1024]{2,1,0:T(8,128)} async-done(((f32[2,32,1024]{2,1,0:T(8,128)}), f32[2,1024,1024]{2,1,0:T(8,128)}) %all-gather.2.cloned.1.call-update) | async-done | bytes 8388624 | tf_op jit(solution)/shard_map/all_gather | solution.py:98
  173.1 9.8 %custom-call.62 = f32[1,128,128]{1,2,0:T(8,128)S(1)} custom-call(f32[1,128,128]{2,1,0:T(8,128)S(1)} %get-tuple-element.28), custom_call_target="InvertDiagBlocksLowerTriangular" | custom-call | tf_op jit(solution)/shard_map/triangular_solve/custom-call.3 | solution.py:86
  189.2 9.8 %custom-call.54 = f32[1,128,128]{1,2,0:T(8,128)S(1)} custom-call(f32[1,128,128]{2,1,0:T(8,128)S(1)} %get-tuple-element.107), custom_call_target="InvertDiagBlocksLowerTriangular" | custom-call | tf_op jit(solution)/shard_map/triangular_solve/custom-call.3 | solution.py:86
  206.2 9.9 %custom-call.63 = f32[1,128,128]{1,2,0:T(8,128)S(1)} custom-call(f32[1,128,128]{2,1,0:T(8,128)S(1)} %get-tuple-element.27), custom_call_target="InvertDiagBlocksLowerTriangular" | custom-call | tf_op jit(solution)/shard_map/triangular_solve/custom-call.3 | solution.py:86
  221.0 11.3 %custom-call.64 = f32[1,128,128]{1,2,0:T(8,128)} custom-call(f32[1,128,128]{2,1,0:T(8,128)} %get-tuple-element.26), custom_call_target="InvertDiagBlocksLowerTriangular" | custom-call | tf_op jit(solution)/shard_map/triangular_solve/custom-call.3 | solution.py:86
  240.0 11.5 %custom-call.65 = f32[1,128,128]{1,2,0:T(8,128)} custom-call(f32[1,128,128]{2,1,0:T(8,128)} %get-tuple-element.25), custom_call_target="InvertDiagBlocksLowerTriangular" | custom-call | tf_op jit(solution)/shard_map/triangular_solve/custom-call.3 | solution.py:86
  260.3 11.3 %custom-call.66 = f32[1,128,128]{1,2,0:T(8,128)} custom-call(f32[1,128,128]{2,1,0:T(8,128)} %get-tuple-element.24), custom_call_target="InvertDiagBlocksLowerTriangular" | custom-call | tf_op jit(solution)/shard_map/triangular_solve/custom-call.3 | solution.py:86
  287.8 10.6 %custom-call.67 = f32[1,128,128]{1,2,0:T(8,128)S(1)} custom-call(f32[1,128,128]{2,1,0:T(8,128)} %get-tuple-element.23), custom_call_target="InvertDiagBlocksLowerTriangular" | custom-call | tf_op jit(solution)/shard_map/triangular_solve/custom-call.3 | solution.py:86
  309.7 10.8 %custom-call.68 = f32[1,128,128]{1,2,0:T(8,128)S(1)} custom-call(f32[1,128,128]{2,1,0:T(8,128)} %get-tuple-element.22), custom_call_target="InvertDiagBlocksLowerTriangular" | custom-call | tf_op jit(solution)/shard_map/triangular_solve/custom-call.3 | solution.py:86
  322.9 10.8 %fusion.30 = f32[128,1280]{0,1:T(8,128)} fusion(f32[896,1280]{1,0:T(8,128)} %constant_dynamic-update-slice_fusion.29, f32[1,1024,1280]{1,2,0:T(8,128)} %get-tuple-element.12, f32[1024,1024]{1,0:T(8,128)} %copy-done.1), kind=kOutput, calls=%fused_computation.32 | convolution fusion | flops 1761771520 | bytes 6356992 | tf_op jit(solution)/shard_map/dot_general | solution.py:79
  333.7 11.3 %custom-call.69 = f32[1,128,128]{1,2,0:T(8,128)} custom-call(f32[1,128,128]{2,1,0:T(8,128)} %get-tuple-element.21), custom_call_target="InvertDiagBlocksLowerTriangular" | custom-call | tf_op jit(solution)/shard_map/triangular_solve/custom-call.3 | solution.py:86
  345.0 10.8 %custom-call.55 = f32[1,128,128]{1,2,0:T(8,128)S(1)} custom-call(f32[1,128,128]{2,1,0:T(8,128)} %get-tuple-element.108), custom_call_target="InvertDiagBlocksLowerTriangular" | custom-call | tf_op jit(solution)/shard_map/triangular_solve/custom-call.3 | solution.py:86
  360.7 10.6 %custom-call.56 = f32[1,128,128]{1,2,0:T(8,128)S(1)} custom-call(f32[1,128,128]{2,1,0:T(8,128)} %get-tuple-element.109), custom_call_target="InvertDiagBlocksLowerTriangular" | custom-call | tf_op jit(solution)/shard_map/triangular_solve/custom-call.3 | solution.py:86
  377.3 11.7 %custom-call.57 = f32[1,128,128]{1,2,0:T(8,128)} custom-call(f32[1,128,128]{2,1,0:T(8,128)} %get-tuple-element.110), custom_call_target="InvertDiagBlocksLowerTriangular" | custom-call | tf_op jit(solution)/shard_map/triangular_solve/custom-call.3 | solution.py:86
  396.7 9.8 %custom-call.58 = f32[1,128,128]{1,2,0:T(8,128)S(1)} custom-call(f32[1,128,128]{2,1,0:T(8,128)S(1)} %get-tuple-element.111), custom_call_target="InvertDiagBlocksLowerTriangular" | custom-call | tf_op jit(solution)/shard_map/triangular_solve/custom-call.3 | solution.py:86
  421.5 9.8 %custom-call.59 = f32[1,128,128]{1,2,0:T(8,128)S(1)} custom-call(f32[1,128,128]{2,1,0:T(8,128)S(1)} %get-tuple-element.112), custom_call_target="InvertDiagBlocksLowerTriangular" | custom-call | tf_op jit(solution)/shard_map/triangular_solve/custom-call.3 | solution.py:86
  441.9 10.0 %custom-call.60 = f32[1,128,128]{1,2,0:T(8,128)S(1)} custom-call(f32[1,128,128]{2,1,0:T(8,128)S(1)} %get-tuple-element.113), custom_call_target="InvertDiagBlocksLowerTriangular" | custom-call | tf_op jit(solution)/shard_map/triangular_solve/custom-call.3 | solution.py:86
  453.5 10.8 %fusion.35 = f32[128,1280]{0,1:T(8,128)} fusion(f32[896,1280]{1,0:T(8,128)} %constant_dynamic-update-slice_fusion.11, f32[1,1024,1280]{1,2,0:T(8,128)} %get-tuple-element.11, f32[1024,1024]{1,0:T(8,128)} %copy-done), kind=kOutput, calls=%fused_computation.42 | convolution fusion | flops 1761771520 | bytes 6356992 | tf_op jit(solution)/shard_map/dot_general | solution.py:79
  464.3 10.2 %custom-call.61 = f32[1,128,128]{1,2,0:T(8,128)S(1)} custom-call(f32[1,128,128]{2,1,0:T(8,128)S(1)} %get-tuple-element.114), custom_call_target="InvertDiagBlocksLowerTriangular" | custom-call | tf_op jit(solution)/shard_map/triangular_solve/custom-call.3 | solution.py:86
  483.9 31.3 %all_to_all.25 = bf16[16,2,64,512]{3,2,1,0:T(8,128)(2,1)S(1)} all-to-all(bf16[16,2,64,512]{3,2,1,0:T(8,128)(2,1)S(1)} %copy.23), channel_id=1, replica_groups=mesh['arc'=8,'par_0'=2,'par_1'=4,'par_2'=4] {'par_1','par_2'}, dimensions={0} | all-to-all | bytes 4194304 | tf_op jit(solution)/shard_map/all_to_all | solution.py:20
  548.1 15.2 %all-to-all-done.3 = bf16[16,2,64,512]{3,2,1,0:T(8,128)(2,1)S(1)} async-done(((bf16[16,2,64,512]{3,2,1,0:T(8,128)(2,1)}), bf16[16,2,64,512]{3,2,1,0:T(8,128)(2,1)S(1)}, u32[]{:S(2)}, u32[]{:S(2)}) %all-to-all-start.3) | async-done | bytes 2097184 | tf_op jit(solution)/shard_map/all_to_all | solution.py:39
  572.6 13.4 %all-to-all-start.4 = ((f32[8,512,160]{1,2,0:T(8,128)}), f32[8,512,160]{1,2,0:T(8,128)S(1)}, u32[]{:S(2)}, u32[]{:S(2)}) async-start(f32[8,512,160]{1,2,0:T(8,128)} %convolution_bitcast_fusion.12), calls=%async_computation.4 | async-start | bytes 5242880 | tf_op jit(solution)/shard_map/all_to_all | solution.py:66
  586.8 73.7 %all-reduce.4.cloned.1.call-done = f32[512,512]{1,0:T(8,128)} async-done(((f32[512,512]{1,0:T(8,128)}), f32[512,512]{1,0:T(8,128)}) %all-reduce.4.cloned.1.call-update) | async-done | bytes 1048592 | tf_op jit(solution)/shard_map/psum | solution.py:122
  668.2 11.7 %cholesky.103 = f32[128,128]{1,0:T(8,128)S(1)} custom-call(f32[128,128]{1,0:T(8,128)S(1)} %cholesky.263), custom_call_target="Cholesky" | custom-call | tf_op jit(solution)/shard_map/jit(cholesky)/cholesky | solution.py:124
  694.1 11.7 %cholesky.215 = f32[128,128]{1,0:T(8,128)S(1)} custom-call(f32[128,128]{1,0:T(8,128)S(1)} %cholesky.267), custom_call_target="Cholesky" | custom-call | tf_op jit(solution)/shard_map/jit(cholesky)/cholesky | solution.py:124
  706.4 10.0 %custom-call.34 = f32[1,128,128]{1,2,0:T(8,128)S(1)} custom-call(f32[1,128,128]{2,1,0:T(8,128)S(1)} %get-tuple-element.73), custom_call_target="InvertDiagBlocksLowerTriangular" | custom-call | tf_op jit(solution)/shard_map/jit(cholesky)/cholesky | solution.py:124
  718.8 11.7 %cholesky.236 = f32[128,128]{1,0:T(8,128)S(1)} custom-call(f32[128,128]{1,0:T(8,128)S(1)} %cholesky.272), custom_call_target="Cholesky" | custom-call | tf_op jit(solution)/shard_map/jit(cholesky)/cholesky | solution.py:124
  743.2 11.7 %cholesky.253 = f32[128,128]{1,0:T(8,128)S(1)} custom-call(f32[128,128]{1,0:T(8,128)S(1)} %convolution_subtract_fusion.5), custom_call_target="Cholesky" | custom-call | tf_op jit(solution)/shard_map/jit(cholesky)/cholesky | solution.py:124
  763.4 9.8 %custom-call.70 = f32[1,128,128]{1,2,0:T(8,128)S(1)} custom-call(f32[1,128,128]{2,1,0:T(8,128)S(1)} %get-tuple-element.32), custom_call_target="InvertDiagBlocksLowerTriangular" | custom-call | tf_op jit(solution)/shard_map/triangular_solve/custom-call.8 | solution.py:86
  773.2 9.8 %custom-call.71 = f32[1,128,128]{1,2,0:T(8,128)S(1)} custom-call(f32[1,128,128]{2,1,0:T(8,128)S(1)} %get-tuple-element.31), custom_call_target="InvertDiagBlocksLowerTriangular" | custom-call | tf_op jit(solution)/shard_map/triangular_solve/custom-call.8 | solution.py:86
  783.0 9.8 %custom-call.72 = f32[1,128,128]{1,2,0:T(8,128)S(1)} custom-call(f32[1,128,128]{2,1,0:T(8,128)S(1)} %get-tuple-element.30), custom_call_target="InvertDiagBlocksLowerTriangular" | custom-call | tf_op jit(solution)/shard_map/triangular_solve/custom-call.8 | solution.py:86
  792.8 9.8 %custom-call.73 = f32[1,128,128]{1,2,0:T(8,128)S(1)} custom-call(f32[1,128,128]{2,1,0:T(8,128)S(1)} %get-tuple-element.29), custom_call_target="InvertDiagBlocksLowerTriangular" | custom-call | tf_op jit(solution)/shard_map/triangular_solve/custom-call.8 | solution.py:86
  (127 shorter events, 236.5 us)
Async XLA Ops:
  6.5 158.8 %all-gather.2.cloned.1.call-start = ((), (), s32[]{:S(2)}) async-start(), calls=%async_computation.5 | async-start | bytes 8650752 | tf_op jit(solution)/shard_map/all_gather | solution.py:98
  7.9 7.9 copy-start.8
  169.7 2.1 copy-start
  169.7 3.4 copy-start.1
  322.0 33.8 %copy-start.5 = (f32[128,1280]{0,1:T(8,128)S(1)}, f32[128,1280]{0,1:T(8,128)}, u32[]{:S(2)}) copy-start(f32[128,1280]{0,1:T(8,128)} %fusion.39) | copy-start | bytes 1966084
  412.3 19.0 %copy-start.2 = (bf16[1,1024,1280]{2,1,0:T(8,128)(2,1)S(1)}, bf16[1,1024,1280]{2,1,0:T(8,128)(2,1)}, u32[]{:S(2)}) copy-start(bf16[1,1024,1280]{2,1,0:T(8,128)(2,1)} %get-tuple-element.99) | copy-start | bytes 7864324
  452.6 21.9 %copy-start.6 = (f32[128,1280]{0,1:T(8,128)S(1)}, f32[128,1280]{0,1:T(8,128)}, u32[]{:S(2)}) copy-start(f32[128,1280]{0,1:T(8,128)} %fusion.30) | copy-start | bytes 1966084
  452.6 21.9 %copy-start.7 = (f32[1,128,128]{1,2,0:T(8,128)S(1)}, f32[1,128,128]{1,2,0:T(8,128)}, u32[]{:S(2)}) copy-start(f32[1,128,128]{1,2,0:T(8,128)} %custom-call.69) | copy-start | bytes 196612
  536.3 27.0 %all-to-all-start.3 = ((bf16[16,2,64,512]{3,2,1,0:T(8,128)(2,1)}), bf16[16,2,64,512]{3,2,1,0:T(8,128)(2,1)S(1)}, u32[]{:S(2)}, u32[]{:S(2)}) async-start(bf16[16,2,64,512]{3,2,1,0:T(8,128)(2,1)} %broadcast_in_dim.49), calls=%async_computation.3 | async-start | bytes 4194304 | tf_op jit(solution)/shard_map/all_to_all | solution.py:39
  540.0 120.4 %all-reduce.4.cloned.1.call-start = ((), (), s32[]{:S(2)}) async-start(), calls=%async_computation.6 | async-start | bytes 2097152 | tf_op jit(solution)/shard_map/psum | solution.py:122
  572.6 230.0 %all-to-all-start.4 = ((f32[8,512,160]{1,2,0:T(8,128)}), f32[8,512,160]{1,2,0:T(8,128)S(1)}, u32[]{:S(2)}, u32[]{:S(2)}) async-start(f32[8,512,160]{1,2,0:T(8,128)} %convolution_bitcast_fusion.12), calls=%async_computation.4 | async-start | bytes 5242880 | tf_op jit(solution)/shard_map/all_to_all | solution.py:66
  667.2 1.0 copy-start.4
  762.4 1.0 copy-start.3
Sparse Core Ops, SparseCore 0:
  10.9 154.3 all-gather.1
  565.7 94.7 all-reduce.3
where the time goes:
time: 826 us; the launch traced here: 816 us
  other arithmetic  311 us (38%)
  waiting for transfers between devices  231 us (28%)
  matrix products  138 us (17%)
  blocking collectives  50.5 us (6%)
  local copies, waits for them, and re-layouts  50.2 us (6%)
  between operations  17.6 us (2%)
  starting transfers between devices  17.2 us (2%)
    another operation x22, other arithmetic, whiten(): lax.linalg.triangular_solve(factor[low:low + step, low:low + step], accum...  210 us
    all_gather x1, waiting for transfers between devices, on_device(): factor = lax.all_gather(cov_factor, PAR, axis=1, tiled=True)  141 us
    dot_general x17, matrix products, whiten(): jnp.dot(factor[low:low + step, :low], done, precision=lax.Precision.HIGHE...  91.9 us
    another operation x15, other arithmetic, on_device(): lower11 = jnp.linalg.cholesky(block + jnp.diag(reg_panel))  81.2 us
    psum x1, waiting for transfers between devices, on_device(): block = lax.psum(block, 'arc')  73.7 us
    all_to_all x1, blocking collectives, sum_at_owner(): lax.all_to_all(tiles, axis, split_axis=0, concat_axis=0, tiled=True)  31.3 us
    another operation x20, matrix products, whiten(): lax.linalg.triangular_solve(factor[low:low + step, low:low + step], accum...  29.5 us
    unnamed x33, local copies, waits for them, and re-layouts  28.6 us
  transfers between devices with their start and end apart: 4, of which 3 were waited for; matrix products, arithmetic and copies ran while one was open for 21% of the time, Pallas kernels for 0%

commit v1 on v0

v1 whole, which is shorter than its diff:
```python
import functools
import jax
import jax.numpy as jnp
from jax import lax
from jax.experimental import pallas as pl
from jax.experimental.pallas import tpu as pltpu
from jax.sharding import Mesh
from jax.sharding import PartitionSpec as P

OBS_STEP = 256
BF = jnp.bfloat16
F32 = jnp.float32
KERNEL_VMEM = 56 * 1024 * 1024


def halves(value):
    high = value.astype(BF)
    return high, (value - high.astype(F32)).astype(BF)


def dot_by(a, b, dims):
    return lax.dot_general(a, b, (dims, ((), ())), preferred_element_type=F32)


def dot3(a, b, dims=((1,), (0,))):
    (ah, al), (bh, bl) = a, b
    return dot_by(ah, bh, dims) + (dot_by(ah, bl, dims) + dot_by(al, bh, dims))


def lanes(shape):
    return lax.broadcasted_iota(jnp.int32, shape, 1)


def rows_of(shape):
    return lax.broadcasted_iota(jnp.int32, shape, 0)


def invert_tiles(tiles):
    lane = lanes((8, 128))
    low = lane < 64
    base = jnp.where(low, 0, 64)
    packed, inverse = [], []
    for tile in tiles:
        packed.append(
            [jnp.where(low, tile[8 * g : 8 * g + 8], tile[64 + 8 * g : 72 + 8 * g]) for g in range(8)]
        )
        inverse.append(
            [
                jnp.where(lane - base == rows_of((8, 128)) + 8 * g, 1.0, 0.0).astype(F32)
                for g in range(8)
            ]
        )
    for j in range(64):
        at, sub = j // 8, j % 8
        index = base + j
        for pack, inv in zip(packed, inverse):
            coef = [jnp.take_along_axis(pack[g], index, axis=1) for g in range(at, 8)]
            pivot = inv[at][sub : sub + 1] / coef[0][sub : sub + 1]
            pivot = jnp.broadcast_to(pivot, (8, 128))
            row = rows_of((8, 128))
            inv[at] = jnp.where(
                row == sub, pivot, jnp.where(row > sub, inv[at] - coef[0] * pivot, inv[at])
            )
            for g in range(at + 1, 8):
                inv[g] = inv[g] - coef[g - at] * pivot
    return [jnp.concatenate(inv, axis=0) for inv in inverse]


def solve_kernel(arcs, factor_ref, rhs_ref, y_ref, qh_ref, ql_ref, inv, fh, fl, wh, wl, yh, yl):
    size = factor_ref.shape[1]
    tiles = size // 128

    @pl.loop(0, arcs * tiles // 4)
    def _(step):
        found = []
        for part in range(4):
            at = step * 4 + part
            arc, tile = at // tiles, lax.rem(at, tiles)
            spot = pl.ds(pl.multiple_of(tile * 128, 128), 128)
            found.append((arc, spot))
        values = [factor_ref[arc, spot, spot] for arc, spot in found]
        low = lanes((64, 128)) < 64
        for (arc, spot), value, done in zip(found, values, invert_tiles(values)):
            first = jnp.where(low, done, 0.0)
            second = jnp.where(low, 0.0, done)
            whole = jnp.concatenate([first, second], axis=0)
            cross = jnp.where(low, value[64:], 0.0)
            left = dot3(halves(cross), halves(whole))
            left = jnp.concatenate([jnp.zeros_like(left), left], axis=0)
            corner = dot3(halves(second), halves(left))
            inv[arc, spot, :] = jnp.concatenate([first, second - corner], axis=0)

    blocks = size // OBS_STEP
    for arc in range(arcs):
        for b in range(blocks):
            r = b * OBS_STEP
            one, two = inv[arc, r : r + 128, :], inv[arc, r + 128 : r + 256, :]
            cross = factor_ref[arc, r + 128 : r + 256, r : r + 128]
            corner = -dot3(halves(two), halves(dot3(halves(cross), halves(one))))
            zero = jnp.zeros((128, 128), BF)
            for (ref, a, c, d) in zip((wh, wl), halves(one), halves(corner), halves(two)):
                ref[arc, r : r + 128, 0:128] = a
                ref[arc, r : r + 128, 128:256] = zero
                ref[arc, r + 128 : r + 256, 0:128] = c
                ref[arc, r + 128 : r + 256, 128:256] = d
            if b:
                high, less = halves(factor_ref[arc, r : r + 256, 0:r])
                fh[arc, r : r + 256, 0:r] = high
                fl[arc, r : r + 256, 0:r] = less

    for b in range(blocks):
        r = b * OBS_STEP
        here = slice(r, r + OBS_STEP)
        for arc in range(arcs):
            value = rhs_ref[arc, here, :].astype(F32)
            if b:
                value = value - dot3(
                    (fh[arc, here, 0:r], fl[arc, here, 0:r]), (yh[arc, 0:r, :], yl[arc, 0:r, :])
                )
            value = dot3((wh[arc, here, :], wl[arc, here, :]), halves(value))
            high, less = halves(value)
            yh[arc, here, :] = high
            yl[arc, here, :] = less
            y_ref[arc, here, :] = high
    flip = ((0,), (0,))
    for b in reversed(range(blocks)):
        r = b * OBS_STEP
        here, after = slice(r, r + OBS_STEP), slice(r + OBS_STEP, size)
        for arc in range(arcs):
            value = yh[arc, here, :].astype(F32) + yl[arc, here, :].astype(F32)
            if b + 1 < blocks:
                value = value - dot3(
                    (fh[arc, after, here], fl[arc, after, here]),
                    (qh_ref[arc, after, :], ql_ref[arc, after, :]),
                    flip,
                )
            value = dot3((wh[arc, here, :], wl[arc, here, :]), halves(value), flip)
            qh_ref[arc, here, :], ql_ref[arc, here, :] = halves(value)


def solve_twice(factor, rhs):
    arcs, size, width = rhs.shape
    vm = pltpu.VMEM
    out = jax.ShapeDtypeStruct(rhs.shape, BF)
    return pl.pallas_call(
        functools.partial(solve_kernel, arcs),
        out_shape=(out, out, out),
        in_specs=[pl.BlockSpec(memory_space=vm)] * 2,
        out_specs=(pl.BlockSpec(memory_space=vm),) * 3,
        scratch_shapes=[
            vm((arcs, size, 128), F32),
            vm((arcs, size, size), BF),
            vm((arcs, size, size), BF),
            vm((arcs, size, OBS_STEP), BF),
            vm((arcs, size, OBS_STEP), BF),
            vm((arcs, size, width), BF),
            vm((arcs, size, width), BF),
        ],
        compiler_params=pltpu.CompilerParams(vmem_limit_bytes=KERNEL_VMEM),
    )(factor, rhs)


def split_rows(u):
    high, less = halves(u)
    return jnp.concatenate([high, high, less], axis=0), jnp.concatenate([high, less, high], axis=0)


def eliminate(panel, first):
    row = rows_of((8, 128))
    scale = [jnp.zeros((8, 128), F32) for _ in range(4)]
    for group in range(4):
        cols = []
        for t in range(8):
            lane = first + group * 8 + t
            cols.append(
                [
                    jnp.broadcast_to(panel[g][0][:, lane : lane + 1], (8, 128)) if g >= group else None
                    for g in range(4)
                ]
            )
        for t in range(8):
            pivot = lax.rsqrt(jnp.broadcast_to(cols[t][group][t : t + 1], (8, 128)))
            scale[group] = jnp.where(row == t, pivot, scale[group])
            inv = pivot * pivot
            mult = [None if g < group else cols[t][g] * inv for g in range(4)]
            mult[group] = jnp.where(row > t, mult[group], 0.0)
            for t2 in range(t + 1, 8):
                top = jnp.broadcast_to(cols[t2][group][t : t + 1], (8, 128))
                for g in range(group, 4):
                    cols[t2][g] = cols[t2][g] - mult[g] * top
            for c in range(len(panel[0])):
                top = jnp.broadcast_to(panel[group][c][t : t + 1], (8, 128))
                for g in range(group, 4):
                    panel[g][c] = panel[g][c] - mult[g] * top
    return jnp.concatenate(
        [jnp.concatenate([piece * scale[g] for piece in panel[g]], axis=1) for g in range(4)], axis=0
    )


def factor_and_solve(work):
    size, width = work.shape
    flip = ((0,), (0,))
    for k in range(size // 128):
        c0 = k * 128
        for q in range(4):
            r = c0 + q * 32
            panel = [
                [work[r + 8 * g : r + 8 * g + 8, c : c + 128] for c in range(c0, width, 128)]
                for g in range(4)
            ]
            done = eliminate(panel, q * 32)
            work[r : r + 32, c0:width] = done
            if q < 3:
                a, b = split_rows(done)
                less = dot_by(a[:, 0:128], b, flip)
                work[r + 32 : c0 + 128, c0:width] -= less[q * 32 + 32 : 128]
        if c0 + 128 < size:
            a, b = split_rows(work[c0 : c0 + 128, c0:width])
            for i in range(c0 + 128, size, 128):
                work[i : i + 128, i:width] -= dot_by(
                    a[:, i - c0 : i - c0 + 128], b[:, i - c0 :], flip
                )


def last_kernel(block_ref, reg_ref, rhs_ref, out_ref, work):
    size, share = rhs_ref.shape
    work[:, size:] = jnp.zeros((size, work.shape[1] - size), F32)
    for i in range(0, size, 128):
        work[i : i + 128, 0:size] = block_ref[i : i + 128, :]
        square = (128, 128)
        work[i : i + 128, i : i + 128] += jnp.where(
            lanes(square) == rows_of(square), reg_ref[:, i : i + 128], 0.0
        )
    work[:, size : size + share] = rhs_ref[...]
    factor_and_solve(work)
    out_ref[...] = work[:, size : size + share]


def last_solve(block, reg_panel, rhs):
    size, share = rhs.shape
    vm = pltpu.VMEM
    return pl.pallas_call(
        last_kernel,
        out_shape=jax.ShapeDtypeStruct(rhs.shape, F32),
        in_specs=[pl.BlockSpec(memory_space=vm)] * 3,
        out_specs=pl.BlockSpec(memory_space=vm),
        scratch_shapes=[vm((size, size + -(-share // 128) * 128), F32)],
        compiler_params=pltpu.CompilerParams(vmem_limit_bytes=KERNEL_VMEM),
    )(block, reg_panel[None], rhs)


PANEL = 512
BLK = 256
PAR = ("par_0", "par_1", "par_2")
PAR_ARC = ("par_0", "par_1", "par_2", "arc")


def in_blocks(shard, dim, count):
    before, after = (shard.shape[:dim], shard.shape[dim + 1 :])
    return jnp.moveaxis(shard.reshape(*before, count, -1, *after), dim, 0)


def sum_at_owner(shard, axis, dim):
    tiles = in_blocks(shard, dim, lax.axis_size(axis))
    arrived = lax.all_to_all(tiles, axis, split_axis=0, concat_axis=0, tiled=True)
    return arrived.astype(F32).sum(axis=0)


def sum_in_two_steps(shard, axes, dim):
    far, near = axes
    own = sum_at_owner(in_blocks(shard, dim, lax.axis_size(far)), near, dim + 1)
    return jnp.sum(
        lax.all_to_all(own.astype(BF), far, 0, 0, tiled=True).astype(F32), axis=0
    )


def from_everyone(shard, axis):
    copies = jnp.broadcast_to(shard, (lax.axis_size(axis), *shard.shape))
    return lax.all_to_all(copies, axis, split_axis=0, concat_axis=0, tiled=True)


def joined_along(tiles, dim):
    lengths = list(tiles.shape[1:])
    lengths[dim] *= tiles.shape[0]
    return jnp.moveaxis(tiles, 0, dim).reshape(lengths)


def whole_of(shard, axes, dim):
    far, near = axes
    first = from_everyone(shard, far)
    tiles = jnp.swapaxes(from_everyone(first, near), 0, 1)
    return joined_along(tiles.reshape(-1, *shard.shape), dim)


def sum_by_parts(shard, axes):
    lines = shard.reshape(-1, shard.shape[-1])
    own = sum_in_two_steps(lines, axes, 0)
    return whole_of(own.astype(BF), axes, 0).reshape(shard.shape)


def on_device(design, cov_factor, active_blocks, panel_index, reg_diag):
    arcs, observed, columns = design.shape
    local_blocks = columns // BLK
    par_id = lax.axis_index(PAR)
    arc_id = lax.axis_index("arc")
    factor = lax.all_gather(cov_factor, PAR, axis=1, tiled=True)
    block_ids = par_id * local_blocks + jnp.arange(local_blocks, dtype=jnp.int32)
    hits = jnp.any(active_blocks[:, :, None] == block_ids[None, None, :], axis=1)
    col_mask = jnp.repeat(hits, BLK, axis=1).astype(BF)
    masked = design * col_mask[:, None, :]
    start = panel_index[0] * PANEL
    offset = start - par_id * columns
    padded = jnp.pad(masked, ((0, 0), (0, 0), (PANEL, PANEL)))
    window = lax.dynamic_slice_in_dim(
        padded, jnp.clip(offset + PANEL, 0, columns + PANEL), PANEL, 2
    )
    raw = sum_by_parts(window, ("par_0", ("par_1", "par_2")))
    panel, solved_high, solved_low = solve_twice(factor, raw)
    gram = jnp.einsum(
        "haop,aoc->pc",
        jnp.stack([solved_high, solved_low]),
        masked,
        preferred_element_type=F32,
    )
    block = jnp.einsum("aop,aoq->pq", panel, panel, preferred_element_type=F32)
    share = columns // lax.axis_size("arc")
    tiles = in_blocks(gram.astype(BF), 1, lax.axis_size("arc"))
    arrived = lax.all_to_all(tiles, "arc", split_axis=0, concat_axis=0, tiled=True)
    block = lax.psum(block, "arc")
    gram = arrived.astype(F32).sum(axis=0)
    reg_panel = lax.dynamic_slice_in_dim(reg_diag, start, PANEL)
    global_cols = par_id * columns + arc_id * share + jnp.arange(share, dtype=jnp.int32)
    rows_at = start + jnp.arange(PANEL, dtype=jnp.int32)
    shifted = gram + jnp.where(
        global_cols[None, :] == rows_at[:, None], reg_panel[:, None], jnp.float32(0.0)
    )
    return last_solve(block, reg_panel, shifted)


def solution(mesh):
    split = Mesh(
        mesh.devices.reshape(mesh.shape["arc"], 2, 4, 4), ("arc", "par_0", "par_1", "par_2")
    )
    return jax.shard_map(
        on_device,
        mesh=split,
        in_specs=(P("arc", None, PAR), P("arc", PAR, None), P("arc", None), P(), P()),
        out_specs=P(None, PAR_ARC),
        check_vma=False,
    )
```

time: 826 us -> 346 us (0.42); the launches traced: 816 us -> 345 us
  other arithmetic: 311 us -> 8.14 us
  matrix products: 138 us -> 6.51 us
  waiting for transfers between devices: 231 us -> 159 us
  blocking collectives: 50.5 us -> 95.9 us
  Pallas kernels: 0 us -> 44.1 us
  local copies, waits for them, and re-layouts: 50.2 us -> 9.95 us
  starting transfers between devices: 17.2 us -> 6.53 us
    another operation x37 -> x0, other arithmetic: 291 us -> none  [the longest x22 210 us: whiten(): lax.linalg.triangular_solve(factor[low:low + step, low:low + step], accum...]
    dot_general x19 -> x2, matrix products: 101 us -> 6.51 us  [the longest x1 4.26 us: on_device(): jnp.einsum('haop,aoc->pc', jnp.stack([solved_high, solved_low]), masked,...]
    all_gather x1, waiting for transfers between devices: 141 us -> 85.3 us  [on_device(): factor = lax.all_gather(cov_factor, PAR, axis=1, tiled=True)]
    pallas_call x0 -> x2, Pallas kernels: none -> 44.1 us  [the longest x1 25.9 us: solve_twice(): pl.pallas_call(functools.partial(solve_kernel, arcs), out_shape=(out, out...]
    another operation x26 -> x0, matrix products: 37.3 us -> none  [the longest x20 29.5 us: whiten(): lax.linalg.triangular_solve(factor[low:low + step, low:low + step], accum...]
    psum x1, waiting for transfers between devices: 73.7 us -> 37.6 us  [on_device(): block = lax.psum(block, 'arc')]
    all_to_all x1 -> x2, blocking collectives: 9.61 us -> 42.1 us  [from_everyone(): return lax.all_to_all(copies, axis, split_axis=0, concat_axis=0, tiled=True)]
    unnamed x33 -> x12, local copies, waits for them, and re-layouts: 28.6 us -> 1.36 us
  transfers between devices with their start and end apart: 4 -> 3, of which waited for: 3 -> 3; matrix products, arithmetic and copies ran while one was open for 21% -> 3% of each run, Pallas kernels for 0% -> 0%
where the time goes in v1:
time: 346 us; the launch traced here: 345 us
  waiting for transfers between devices  159 us (46%)
  blocking collectives  95.9 us (28%)
  Pallas kernels  44.1 us (13%)
  between operations  14.2 us (4%)
  local copies, waits for them, and re-layouts  9.95 us (3%)
  other arithmetic  8.14 us (2%)
  starting transfers between devices  6.53 us (2%)
  matrix products  6.51 us (2%)
    all_gather x1, waiting for transfers between devices, on_device(): factor = lax.all_gather(cov_factor, PAR, axis=1, tiled=True)  85.3 us
    all_to_all x2, blocking collectives, from_everyone(): return lax.all_to_all(copies, axis, split_axis=0, concat_axis=0, tiled=True)  42.1 us
    psum x1, waiting for transfers between devices, on_device(): block = lax.psum(block, 'arc')  37.6 us
    all_to_all x1, blocking collectives, sum_at_owner(): lax.all_to_all(tiles, axis, split_axis=0, concat_axis=0, tiled=True)  37.3 us
    all_to_all x1, waiting for transfers between devices, on_device(): lax.all_to_all(tiles, 'arc', split_axis=0, concat_axis=0, tiled=True)  35.7 us
    pallas_call x1, Pallas kernels, solve_twice(): pl.pallas_call(functools.partial(solve_kernel, arcs), out_shape=(out, out...  25.9 us
    pallas_call x1, Pallas kernels, last_solve(): pl.pallas_call(last_kernel, out_shape=jax.ShapeDtypeStruct(rhs.shape, F32...  18.2 us
    all_to_all x1, blocking collectives, sum_in_two_steps(): lax.all_to_all(own.astype(BF), far, 0, 0, tiled=True).astype(F32)  16.5 us
  transfers between devices with their start and end apart: 3, of which 3 were waited for; matrix products, arithmetic and copies ran while one was open for 3% of the time, Pallas kernels for 0%

profile of v1, /device:TPU:1, one launch (start us, length us, event | category | flops | bytes accessed | tf_op | source)
XLA Modules:
  0.0 344.6 jit_solution(14823371539023678841)
XLA Ops:
  6.5 0.7 all-gather.2.cloned.1.call-update
  7.9 0.9 compare_reduce_fusion
  8.8 0.1 broadcast_bitcast_fusion
  8.9 2.8 broadcast_multiply_fusion
  11.7 0.0 copy-start
  11.7 1.1 pad_dynamic-slice_fusion
  12.8 1.3 copy-done
  14.1 0.2 copy.24
  14.3 37.3 %all_to_all.25 = bf16[16,2,64,512]{3,2,1,0:T(8,128)(2,1)S(1)} all-to-all(bf16[16,2,64,512]{3,2,1,0:T(8,128)(2,1)S(1)} %copy.24), channel_id=1, replica_groups=mesh['arc'=8,'par_0'=2,'par_1'=4,'par_2'=4] {'par_1','par_2'}, dimensions={0} | all-to-all | bytes 4194304 | tf_op jit(solution)/shard_map/all_to_all | solution.py:265
  51.6 0.3 reduce_sum.42
  51.9 16.5 %all_to_all.26 = bf16[2,64,512]{2,1,0:T(8,128)(2,1)S(1)} all-to-all(bf16[2,64,512]{2,1,0:T(8,128)(2,1)S(1)} %reduce_sum.42), channel_id=1, replica_groups=mesh['arc'=8,'par_0'=2,'par_1'=4,'par_2'=4] {'par_0'}, dimensions={0} | all-to-all | bytes 262144 | tf_op jit(solution)/shard_map/all_to_all | solution.py:273
  68.4 14.8 %all_to_all.27 = bf16[2,64,512]{2,1,0:T(8,128)(2,1)S(1)} all-to-all(bf16[2,64,512]{2,1,0:T(8,128)(2,1)S(1)} %broadcast_in_dim.31), channel_id=1, replica_groups=mesh['arc'=8,'par_0'=2,'par_1'=4,'par_2'=4] {'par_0'}, dimensions={0} | all-to-all | bytes 262144 | tf_op jit(solution)/shard_map/all_to_all | solution.py:279
  83.2 0.2 broadcast_in_dim.32
  83.5 27.3 %all_to_all.28 = bf16[16,2,64,512]{3,2,1,0:T(8,128)(2,1)S(1)} all-to-all(bf16[16,2,64,512]{3,2,1,0:T(8,128)(2,1)S(1)} %broadcast_in_dim.32), channel_id=1, replica_groups=mesh['arc'=8,'par_0'=2,'par_1'=4,'par_2'=4] {'par_1','par_2'}, dimensions={0} | all-to-all | bytes 4194304 | tf_op jit(solution)/shard_map/all_to_all | solution.py:279
  110.8 1.5 copy.25
  112.4 85.3 %all-gather.2.cloned.1.call-done.factor_ref = f32[2,1024,1024]{2,1,0:T(8,128)} async-done(((f32[2,32,1024]{2,1,0:T(8,128)}), f32[2,1024,1024]{2,1,0:T(8,128)}) %all-gather.2.cloned.1.call-update) | async-done | bytes 8388624 | tf_op jit(solution)/shard_map/all_gather | solution.py:306
  197.6 25.9 %shard_map.55 = (bf16[2,1024,512]{2,1,0:T(8,128)(2,1)}, bf16[2,1024,512]{2,1,0:T(8,128)(2,1)}, bf16[2,1024,512]{2,1,0:T(8,128)(2,1)}) custom-call(f32[2,1024,1024]{2,1,0:T(8,128)} %all-gather.2.cloned.1.call-done.factor_ref, bf16[2,1024,512]{2,1,0:T(8,128)(2,1)} %bitcast.27), custom_call_target="tpu_custom_call" | custom-call | tf_op jit(solution)/shard_map/pallas_call | solution.py:145
  223.5 2.9 convert_reduce_fusion
  226.5 4.3 %fusion = bf16[512,1280]{1,0:T(8,128)(2,1)} fusion(bf16[2,1024,512]{2,1,0:T(8,128)(2,1)S(1)} %convert_reduce_fusion, bf16[2,1024,1280]{2,1,0:T(8,128)(2,1)S(1)} %bitcast.26), kind=kOutput, calls=%fused_computation.3 | convolution fusion | flops 2684354560 | bytes 8650752 | tf_op jit(solution)/shard_map/haop,aoc->pc/dot_general | solution.py:319
  230.7 2.6 copy.28
  233.3 6.5 %all-to-all-start.4 = ((bf16[8,512,160]{1,2,0:T(8,128)(2,1)}), bf16[8,512,160]{1,2,0:T(8,128)(2,1)S(1)}, u32[]{:S(2)}, u32[]{:S(2)}) async-start(bf16[8,512,160]{1,2,0:T(8,128)(2,1)} %bitcast.30), calls=%async_computation.4 | async-start | bytes 2621440 | tf_op jit(solution)/shard_map/all_to_all | solution.py:328
  239.9 0.0 copy-done.1
  239.9 2.2 convolution_bitcast_fusion.1
  242.1 0.0 all-reduce.3.cloned.1.call-update
  242.2 0.8 dynamic_slice.7
  242.9 35.7 %all-to-all-done.4 = bf16[8,512,160]{1,2,0:T(8,128)(2,1)S(1)} async-done(((bf16[8,512,160]{1,2,0:T(8,128)(2,1)}), bf16[8,512,160]{1,2,0:T(8,128)(2,1)S(1)}, u32[]{:S(2)}, u32[]{:S(2)}) %all-to-all-start.4) | async-done | bytes 1310752 | tf_op jit(solution)/shard_map/all_to_all | solution.py:328
  278.7 0.2 convert_reduce_fusion.1
  278.9 0.2 copy.29
  279.1 1.0 select_add_fusion.rhs_ref
  280.1 37.6 %all-reduce.3.cloned.1.call-done.block_ref = f32[512,512]{1,0:T(8,128)} async-done(((f32[512,512]{1,0:T(8,128)}), f32[512,512]{1,0:T(8,128)}) %all-reduce.3.cloned.1.call-update) | async-done | bytes 1048592 | tf_op jit(solution)/shard_map/psum | solution.py:329
  317.6 18.2 %shard_map.56 = f32[512,160]{1,0:T(8,128)} custom-call(f32[512,512]{1,0:T(8,128)} %all-reduce.3.cloned.1.call-done.block_ref, f32[1,512]{1,0:T(1,128)} %bitcast.34, f32[512,160]{1,0:T(8,128)} %select_add_fusion.rhs_ref), custom_call_target="tpu_custom_call" | custom-call | tf_op jit(solution)/shard_map/pallas_call | solution.py:242
  335.8 1.9 copy.30
  (17 shorter events, 0.1 us)
Async XLA Ops:
  6.5 191.1 %all-gather.2.cloned.1.call-start = ((), (), s32[]{:S(2)}) async-start(), calls=%async_computation.5 | async-start | bytes 8650752 | tf_op jit(solution)/shard_map/all_gather | solution.py:306
  11.7 2.4 copy-start
  110.8 115.6 %slice-start = ((s8[5242880]{0:T(1024)(128)(4,1)}), s8[1048576]{0:T(1024)(128)(4,1)S(1)}, s32[]{:S(2)}) async-start(s8[5242880]{0:T(1024)(128)(4,1)} %bitcast.25), calls=%async_computation.7 | async-start | bytes 2097152
  197.6 28.8 %slice-start.1 = ((s8[5242880]{0:T(1024)(128)(4,1)}), s8[4194304]{0:T(1024)(128)(4,1)S(1)}, s32[]{:S(2)}) async-start(s8[5242880]{0:T(1024)(128)(4,1)} %bitcast.25), calls=%async_computation.8 | async-start | bytes 8388608
  230.7 9.1 %copy-start.1 = (bf16[2,1024,512]{2,1,0:T(8,128)(2,1)S(1)}, bf16[2,1024,512]{2,1,0:T(8,128)(2,1)}, u32[]{:S(2)}) copy-start(bf16[2,1024,512]{2,1,0:T(8,128)(2,1)} %get-tuple-element.8) | copy-start | bytes 6291460
  233.3 45.3 %all-to-all-start.4 = ((bf16[8,512,160]{1,2,0:T(8,128)(2,1)}), bf16[8,512,160]{1,2,0:T(8,128)(2,1)S(1)}, u32[]{:S(2)}, u32[]{:S(2)}) async-start(bf16[8,512,160]{1,2,0:T(8,128)(2,1)} %bitcast.30), calls=%async_computation.4 | async-start | bytes 2621440 | tf_op jit(solution)/shard_map/all_to_all | solution.py:328
  239.9 77.8 %all-reduce.3.cloned.1.call-start = ((), (), s32[]{:S(2)}) async-start(), calls=%async_computation.6 | async-start | bytes 2097152 | tf_op jit(solution)/shard_map/psum | solution.py:329
  242.9 74.7 %copy-start.2 = (f32[512]{0:T(512)}, f32[512]{0:T(512)S(1)}, u32[]{:S(2)}) copy-start(f32[512]{0:T(512)S(1)} %dynamic_slice.7) | copy-start | bytes 6148
Sparse Core Ops, SparseCore 0:
  10.9 186.6 all-gather.1
  243.3 74.2 all-reduce.2

commit v2 on v1

--- a/solution.py
+++ b/solution.py
@@ -66,8 +66,21 @@
     return [jnp.concatenate(inv, axis=0) for inv in inverse]
 
 
+def spot_of(arc, row_slab, piece):
+    big = row_slab // 16
+    pair = row_slab + big * (31 - 2 * row_slab)
+    near, far = lax.rem(pair, 4) if not isinstance(pair, int) else pair % 4, pair // 4
+    place = (1 - arc) * (4 * far + near) + arc * (4 * near + far)
+    return place, piece + big * (far + 1)
+
+
+def tile_of(ref, arc, row, column):
+    pieces = [ref[(arc, *spot_of(arc, 4 * row + i, column))] for i in range(4)]
+    return jnp.concatenate(pieces, axis=0)
+
+
 def solve_kernel(arcs, factor_ref, rhs_ref, y_ref, qh_ref, ql_ref, inv, fh, fl, wh, wl, yh, yl):
-    size = factor_ref.shape[1]
+    size = rhs_ref.shape[1]
     tiles = size // 128
 
     @pl.loop(0, arcs * tiles // 4)
@@ -77,10 +90,10 @@
             at = step * 4 + part
             arc, tile = at // tiles, lax.rem(at, tiles)
             spot = pl.ds(pl.multiple_of(tile * 128, 128), 128)
-            found.append((arc, spot))
-        values = [factor_ref[arc, spot, spot] for arc, spot in found]
+            found.append((arc, spot, tile))
+        values = [tile_of(factor_ref, arc, tile, tile) for arc, spot, tile in found]
         low = lanes((64, 128)) < 64
-        for (arc, spot), value, done in zip(found, values, invert_tiles(values)):
+        for (arc, spot, _), value, done in zip(found, values, invert_tiles(values)):
             first = jnp.where(low, done, 0.0)
             second = jnp.where(low, 0.0, done)
             whole = jnp.concatenate([first, second], axis=0)
@@ -95,7 +108,7 @@
         for b in range(blocks):
             r = b * OBS_STEP
             one, two = inv[arc, r : r + 128, :], inv[arc, r + 128 : r + 256, :]
-            cross = factor_ref[arc, r + 128 : r + 256, r : r + 128]
+            cross = tile_of(factor_ref, arc, 2 * b + 1, 2 * b)
             corner = -dot3(halves(two), halves(dot3(halves(cross), halves(one))))
             zero = jnp.zeros((128, 128), BF)
             for (ref, a, c, d) in zip((wh, wl), halves(one), halves(corner), halves(two)):
@@ -103,10 +116,11 @@
                 ref[arc, r : r + 128, 128:256] = zero
                 ref[arc, r + 128 : r + 256, 0:128] = c
                 ref[arc, r + 128 : r + 256, 128:256] = d
-            if b:
-                high, less = halves(factor_ref[arc, r : r + 256, 0:r])
-                fh[arc, r : r + 256, 0:r] = high
-                fl[arc, r : r + 256, 0:r] = less
+            for row in (2 * b, 2 * b + 1):
+                for column in range(2 * b):
+                    high, less = halves(tile_of(factor_ref, arc, row, column))
+                    fh[arc, row * 128 : row * 128 + 128, column * 128 : column * 128 + 128] = high
+                    fl[arc, row * 128 : row * 128 + 128, column * 128 : column * 128 + 128] = less
 
     for b in range(blocks):
         r = b * OBS_STEP
@@ -197,11 +211,12 @@
     )
 
 
-def factor_and_solve(work):
-    size, width = work.shape
+def factor_and_invert(work):
+    size = work.shape[0]
     flip = ((0,), (0,))
     for k in range(size // 128):
         c0 = k * 128
+        width = size + 128 + c0
         for q in range(4):
             r = c0 + q * 32
             panel = [
@@ -222,80 +237,324 @@
                 )
 
 
-def last_kernel(block_ref, reg_ref, rhs_ref, out_ref, work):
-    size, share = rhs_ref.shape
-    work[:, size:] = jnp.zeros((size, work.shape[1] - size), F32)
-    for i in range(0, size, 128):
-        work[i : i + 128, 0:size] = block_ref[i : i + 128, :]
-        square = (128, 128)
-        work[i : i + 128, i : i + 128] += jnp.where(
-            lanes(square) == rows_of(square), reg_ref[:, i : i + 128], 0.0
-        )
-    work[:, size : size + share] = rhs_ref[...]
-    factor_and_solve(work)
-    out_ref[...] = work[:, size : size + share]
-
-
-def last_solve(block, reg_panel, rhs):
-    size, share = rhs.shape
+def tile_list(size):
+    return [(i, j) for i in range(size // 128) for j in range(i, size // 128)]
+
+
+def factor_kernel(block_ref, reg_ref, out_ref, work):
+    size = out_ref.shape[0]
+    square = (128, 128)
+    eye = lanes(square) == rows_of(square)
+    work[:, size:] = jnp.zeros((size, size), F32)
+    for at, (i, j) in enumerate(tile_list(size)):
+        value = block_ref[at * 128 : at * 128 + 128, :]
+        if i == j:
+            value = value + jnp.where(eye, reg_ref[:, i * 128 : i * 128 + 128], 0.0)
+            work[i * 128 : i * 128 + 128, size + i * 128 : size + i * 128 + 128] = jnp.where(eye, 1.0, 0.0)
+        work[i * 128 : i * 128 + 128, j * 128 : j * 128 + 128] = value
+    factor_and_invert(work)
+    out_ref[...] = work[:, size:]
+
+
+def factor_inverse(block, reg_panel):
+    size = reg_panel.shape[0]
     vm = pltpu.VMEM
     return pl.pallas_call(
-        last_kernel,
-        out_shape=jax.ShapeDtypeStruct(rhs.shape, F32),
-        in_specs=[pl.BlockSpec(memory_space=vm)] * 3,
+        factor_kernel,
+        out_shape=jax.ShapeDtypeStruct((size, size), F32),
+        in_specs=[pl.BlockSpec(memory_space=vm)] * 2,
         out_specs=pl.BlockSpec(memory_space=vm),
-        scratch_shapes=[vm((size, size + -(-share // 128) * 128), F32)],
+        scratch_shapes=[vm((size, 2 * size), F32)],
         compiler_params=pltpu.CompilerParams(vmem_limit_bytes=KERNEL_VMEM),
-    )(block, reg_panel[None], rhs)
+        cost_estimate=pl.CostEstimate(flops=30_000_000_000, bytes_accessed=60_000_000, transcendentals=0),
+    )(block, reg_panel[None])
+
+
+def apply_kernel(shift_ref, arrived_ref, inverse_ref, reg_ref, out_ref):
+    total = arrived_ref[0].astype(F32)
+    for part in range(1, arrived_ref.shape[0]):
+        total = total + arrived_ref[part].astype(F32)
+    on = rows_of(total.shape) + shift_ref[0] == lanes(total.shape)
+    total = total + jnp.where(on, reg_ref[...], 0.0)
+    out_ref[...] = dot3(halves(inverse_ref[...]), halves(total), ((1,), (1,)))
+
+
+def apply_inverse(shift, arrived, inverse, reg_panel):
+    _, share, size = arrived.shape
+    vm = pltpu.VMEM
+    return pl.pallas_call(
+        apply_kernel,
+        out_shape=jax.ShapeDtypeStruct((size, share), F32),
+        in_specs=[pl.BlockSpec(memory_space=pltpu.SMEM)] + [pl.BlockSpec(memory_space=vm)] * 3,
+        out_specs=pl.BlockSpec(memory_space=vm),
+        compiler_params=pltpu.CompilerParams(vmem_limit_bytes=KERNEL_VMEM),
+    )(shift, arrived, inverse, reg_panel[None])
+
+
+MESH = pl.DeviceIdType.MESH
+
+
+def remote(src, dst, send, recv, device):
+    return pltpu.make_async_remote_copy(
+        src_ref=src, dst_ref=dst, send_sem=send, recv_sem=recv, device_id=device, device_id_type=MESH
+    )
+
+
+def meet(devices):
+    barrier = pltpu.get_barrier_semaphore()
+    for device in devices:
+        pl.semaphore_signal(barrier, inc=1, device_id=device, device_id_type=MESH)
+    pl.semaphore_wait(barrier, len(devices))
+
+
+def ring_pair(slot, me, axis, send, recv):
+    mine = slot(me)
+    return [
+        remote(mine, mine, send.at[d], recv.at[d], {axis: lax.rem(me + step, 4)})
+        for d, step in enumerate((1, 3))
+    ]
+
+
+def ring_far(first, second, me, axis, send, recv):
+    left, right = lax.rem(me + 3, 4), lax.rem(me + 1, 4)
+    one, two = first(left), second(right)
+    return [
+        remote(one, one, send.at[2], recv.at[2], {axis: right}),
+        remote(two, two, send.at[3], recv.at[3], {axis: left}),
+    ]
+
+
+def spread_kernel(
+    cov_ref, win_ref, fac_ref, rhs_ref, slabs, got1, got2, gotz, sum1, sum2,
+    ls, lr, m1s, m1r, m2s, m2r, mzs, mzr, gls, glr, gms, gmr,
+):
+    z, x, y = (lax.axis_index(name) for name in ("par_0", "par_1", "par_2"))
+    arcs = cov_ref.shape[0]
+    turned = lambda v: v + z * (3 - 2 * v)
+    outer = [(x, "par_1"), (y, "par_2")]
+    inner = [(y, "par_2"), (x, "par_1")]
+    partner = {"par_0": 1 - z, "par_1": 3 - x, "par_2": 3 - y}
+    ring = [{"par_1": lax.rem(x + k, 4)} for k in (1, 2, 3)] + [
+        {"par_2": lax.rem(y + k, 4)} for k in (1, 2, 3)
+    ]
+    meet(ring + [{"par_0": 1 - z}, partner])
+
+    small = turned(x) + 1
+    held = small + z * (9 - 2 * small)
+
+    def piece(c):
+        spot = pl.ds(pl.multiple_of(c * 128, 128), 128)
+        return remote(cov_ref.at[:, :, spot], slabs.at[z, :, :, spot], ls.at[c], lr.at[c], partner)
+
+    pl.loop(0, held)(lambda c: piece(c).start())
+    scatter1 = [
+        remote(
+            win_ref.at[arc, pl.ds(pl.multiple_of(lax.rem(outer[arc][0] + k, 4) * 256, 256), 256)],
+            got1.at[arc, k - 1], m1s.at[arc, k - 1], m1r.at[arc, k - 1],
+            {outer[arc][1]: lax.rem(outer[arc][0] + k, 4)},
+        )
+        for k in (1, 3, 2) for arc in range(arcs)
+    ]
+    for copy in scatter1:
+        copy.start()
+    slabs[z] = cov_ref[...]
+    pl.loop(0, 9 - held)(lambda c: piece(c).wait_recv())
+
+    @pl.loop(0, small)
+    def _(c):
+        spot = pl.ds(pl.multiple_of(c * 128, 128), 128)
+        for arc in range(arcs):
+            place = 4 * turned(outer[arc][0]) + turned(inner[arc][0])
+            fac_ref[arc, place, c] = slabs[0, arc, :, spot]
+
+    @pl.loop(0, 9 - small)
+    def _(c):
+        spot = pl.ds(pl.multiple_of(c * 128, 128), 128)
+        for arc in range(arcs):
+            place = 4 * turned(outer[arc][0]) + turned(inner[arc][0])
+            fac_ref[arc, place, small + c] = slabs[1, arc, :, spot]
+
+    def l_unit(arc, cut=slice(0, 9)):
+        size = cut.stop - cut.start
+        return lambda r: fac_ref.at[
+            arc, 4 * turned(outer[arc][0]) + turned(r), pl.ds(cut.start, size)
+        ]
+
+    def l_group(arc, low=0, size=4):
+        return lambda r: fac_ref.at[arc, pl.ds(4 * turned(r) + low, size)]
+
+    def m_rows(arc, unit, base, low, size):
+        return lambda r: rhs_ref.at[arc, pl.ds(pl.multiple_of(base + r * unit + low, 32), size)]
+
+    def m_unit(arc, low=0, size=64):
+        return m_rows(arc, 64, outer[arc][0] * 256, low, size)
+
+    def m_group(arc, low=0, size=256):
+        return m_rows(arc, 256, 0, low, size)
+
+    def begin(copies):
+        for copy in copies:
+            copy.start()
+        return copies
+
+    def arrive(copies):
+        for copy in copies:
+            copy.wait_recv()
+        return copies
+
+    two = range(arcs)
+    sent = list(scatter1)
+    near = lambda slot, ax, stage, s, r: [
+        copy for arc in two
+        for copy in ring_pair(slot(arc), *ax[arc], s.at[arc, stage], r.at[arc, stage])
+    ]
+    far = lambda first, second, ax, stage, s, r: [
+        copy for arc in two
+        for copy in ring_far(first(arc), second(arc), *ax[arc], s.at[arc, stage], r.at[arc, stage])
+    ]
+    l1 = begin(near(l_unit, inner, 0, gls, glr))
+    arrive(scatter1)
+    scatter2 = []
+    for arc in two:
+        own = win_ref[arc, pl.ds(pl.multiple_of(outer[arc][0] * 256, 256), 256), :]
+        sum1[arc] = (own + got1[arc, 0]) + (got1[arc, 1] + got1[arc, 2])
+        i, axis = inner[arc]
+        for k in (1, 3, 2):
+            to = lax.rem(i + k, 4)
+            scatter2 += begin([
+                remote(
+                    sum1.at[arc, pl.ds(pl.multiple_of(to * 64, 64), 64)],
+                    got2.at[arc, k - 1], m2s.at[arc, k - 1], m2r.at[arc, k - 1], {axis: to},
+                )
+            ])
+    arrive(l1)
+    l2 = begin(far(lambda a: l_unit(a, slice(0, 5)), lambda a: l_unit(a, slice(5, 9)), inner, 0, gls, glr))
+    arrive(scatter2)
+    across = []
+    for arc in two:
+        own = sum1[arc, pl.ds(pl.multiple_of(inner[arc][0] * 64, 64), 64), :]
+        sum2[arc] = (own + got2[arc, 0]) + (got2[arc, 1] + got2[arc, 2])
+        across += begin([remote(sum2.at[arc], gotz.at[arc], mzs.at[arc], mzr.at[arc], {"par_0": 1 - z})])
+    arrive(l2)
+    l3 = begin(near(l_group, outer, 1, gls, glr))
+    arrive(across)
+    for arc in two:
+        spot = pl.ds(pl.multiple_of(outer[arc][0] * 256 + inner[arc][0] * 64, 64), 64)
+        rhs_ref[arc, spot, :] = sum2[arc] + gotz[arc]
+    g1 = begin(near(m_unit, inner, 0, gms, gmr))
+    arrive(g1)
+    g2 = begin(far(lambda a: m_unit(a, 0, 32), lambda a: m_unit(a, 32, 32), inner, 0, gms, gmr))
+    arrive(g2)
+    g3 = begin(near(m_group, outer, 1, gms, gmr))
+    arrive(l3)
+    l4 = begin(far(lambda a: l_group(a, 0, 2), lambda a: l_group(a, 2, 2), outer, 1, gls, glr))
+    arrive(g3)
+    g4 = begin(far(lambda a: m_group(a, 0, 128), lambda a: m_group(a, 128, 128), outer, 1, gms, gmr))
+    arrive(l4)
+    arrive(g4)
+    pl.loop(0, held)(lambda c: piece(c).wait_send())
+    for copy in sent + scatter2 + across + l1 + l2 + l3 + l4 + g1 + g2 + g3 + g4:
+        copy.wait_send()
+
+
+def spread(cov, window):
+    arcs, lines, size = cov.shape
+    _, observed, width = window.shape
+    vm, dma = pltpu.VMEM, pltpu.SemaphoreType.DMA
+    return pl.pallas_call(
+        spread_kernel,
+        out_shape=(
+            jax.ShapeDtypeStruct((arcs, 16, 9, lines, 128), F32),
+            jax.ShapeDtypeStruct(window.shape, BF),
+        ),
+        in_specs=[pl.BlockSpec(memory_space=vm)] * 2,
+        out_specs=(pl.BlockSpec(memory_space=vm),) * 2,
+        scratch_shapes=[
+            vm((2, arcs, lines, size), F32),
+            vm((arcs, 3, 256, width), BF),
+            vm((arcs, 3, 64, width), BF),
+            vm((arcs, 64, width), BF),
+            vm((arcs, 256, width), BF),
+            vm((arcs, 64, width), BF),
+            dma((8,)), dma((8,)),
+            dma((arcs, 3)), dma((arcs, 3)), dma((arcs, 3)), dma((arcs, 3)),
+            dma((arcs,)), dma((arcs,)),
+            dma((arcs, 2, 4)), dma((arcs, 2, 4)), dma((arcs, 2, 4)), dma((arcs, 2, 4)),
+        ],
+        compiler_params=pltpu.CompilerParams(
+            vmem_limit_bytes=KERNEL_VMEM, collective_id=0, has_side_effects=True
+        ),
+    )(cov, window)
+
+
+def total_kernel(part_ref, out_ref, kept, mate, got, ps, pr, rs, rr, gs, gr, fs, fr):
+    me = lax.axis_index("arc")
+    core, chip = lax.rem(me, 2), me // 2
+    other = {"arc": chip * 2 + 1 - core}
+    chips = [lax.rem(chip + k, 4) for k in (1, 2, 3)]
+    peers = [{"arc": c * 2 + core} for c in chips]
+    meet(peers + [other])
+    half = part_ref.shape[0] // 2
+    quarter = half // 4
+    rows = lambda base, n: pl.ds(pl.multiple_of(base, 32), n)
+    swap = remote(part_ref.at[rows((1 - core) * half, half)], mate, ps, pr, other)
+    swap.start()
+    swap.wait_recv()
+    kept[...] = part_ref[rows(core * half, half), :] + mate[...]
+    scatter = [
+        remote(kept.at[rows(c * quarter, quarter)], got.at[k], rs.at[k], rr.at[k], peer)
+        for k, (c, peer) in enumerate(zip(chips, peers))
+    ]
+    for copy in scatter:
+        copy.start()
+    for copy in scatter:
+        copy.wait_recv()
+    mine = rows(core * half + chip * quarter, quarter)
+    out_ref[mine, :] = (kept[rows(chip * quarter, quarter), :] + got[0]) + (got[1] + got[2])
+    gather = [
+        remote(out_ref.at[mine], out_ref.at[mine], gs.at[k], gr.at[k], peer)
+        for k, peer in enumerate(peers)
+    ]
+    forward = [remote(out_ref.at[mine], out_ref.at[mine], fs.at[0], fr.at[0], other)]
+    for copy in gather + forward:
+        copy.start()
+    for k in range(3):
+        gather[k].wait_recv()
+        came = rows(core * half + lax.rem(chip + 3 - k, 4) * quarter, quarter)
+        copy = remote(out_ref.at[came], out_ref.at[came], fs.at[k + 1], fr.at[k + 1], other)
+        copy.start()
+        forward.append(copy)
+    for copy in forward:
+        copy.wait_recv()
+    for copy in [swap] + scatter + gather + forward:
+        copy.wait_send()
+
+
+def total_over_arc(part):
+    lines, width = part.shape
+    vm, dma = pltpu.VMEM, pltpu.SemaphoreType.DMA
+    return pl.pallas_call(
+        total_kernel,
+        out_shape=jax.ShapeDtypeStruct(part.shape, F32),
+        in_specs=[pl.BlockSpec(memory_space=vm)],
+        out_specs=pl.BlockSpec(memory_space=vm),
+        scratch_shapes=[
+            vm((lines // 2, width), F32),
+            vm((lines // 2, width), F32),
+            vm((3, lines // 8, width), F32),
+            dma, dma, dma((3,)), dma((3,)), dma((3,)), dma((3,)), dma((4,)), dma((4,)),
+        ],
+        compiler_params=pltpu.CompilerParams(
+            vmem_limit_bytes=KERNEL_VMEM, collective_id=1, has_side_effects=True
+        ),
+        cost_estimate=pl.CostEstimate(flops=20_000_000_000, bytes_accessed=40_000_000, transcendentals=0),
+    )(part)
 
 
 PANEL = 512
 BLK = 256
 PAR = ("par_0", "par_1", "par_2")
 PAR_ARC = ("par_0", "par_1", "par_2", "arc")
-
-
-def in_blocks(shard, dim, count):
-    before, after = (shard.shape[:dim], shard.shape[dim + 1 :])
-    return jnp.moveaxis(shard.reshape(*before, count, -1, *after), dim, 0)
-
-
-def sum_at_owner(shard, axis, dim):
-    tiles = in_blocks(shard, dim, lax.axis_size(axis))
-    arrived = lax.all_to_all(tiles, axis, split_axis=0, concat_axis=0, tiled=True)
-    return arrived.astype(F32).sum(axis=0)
-
-
-def sum_in_two_steps(shard, axes, dim):
-    far, near = axes
-    own = sum_at_owner(in_blocks(shard, dim, lax.axis_size(far)), near, dim + 1)
-    return jnp.sum(
-        lax.all_to_all(own.astype(BF), far, 0, 0, tiled=True).astype(F32), axis=0
-    )
-
-
-def from_everyone(shard, axis):
-    copies = jnp.broadcast_to(shard, (lax.axis_size(axis), *shard.shape))
-    return lax.all_to_all(copies, axis, split_axis=0, concat_axis=0, tiled=True)
-
-
-def joined_along(tiles, dim):
-    lengths = list(tiles.shape[1:])
-    lengths[dim] *= tiles.shape[0]
-    return jnp.moveaxis(tiles, 0, dim).reshape(lengths)
-
-
-def whole_of(shard, axes, dim):
-    far, near = axes
-    first = from_everyone(shard, far)
-    tiles = jnp.swapaxes(from_everyone(first, near), 0, 1)
-    return joined_along(tiles.reshape(-1, *shard.shape), dim)
-
-
-def sum_by_parts(shard, axes):
-    lines = shard.reshape(-1, shard.shape[-1])
-    own = sum_in_two_steps(lines, axes, 0)
-    return whole_of(own.astype(BF), axes, 0).reshape(shard.shape)
 
 
 def on_device(design, cov_factor, active_blocks, panel_index, reg_diag):
@@ -303,38 +562,38 @@
     local_blocks = columns // BLK
     par_id = lax.axis_index(PAR)
     arc_id = lax.axis_index("arc")
-    factor = lax.all_gather(cov_factor, PAR, axis=1, tiled=True)
+    start = panel_index[0] * PANEL
     block_ids = par_id * local_blocks + jnp.arange(local_blocks, dtype=jnp.int32)
     hits = jnp.any(active_blocks[:, :, None] == block_ids[None, None, :], axis=1)
+    wanted = []
+    for part in range(PANEL // BLK):
+        local = start // BLK + part - par_id * local_blocks
+        kept = jnp.clip(local, 0, local_blocks - 1)
+        on = (local == kept) & lax.dynamic_slice_in_dim(hits, kept, 1, 1)
+        piece = lax.dynamic_slice_in_dim(design, kept * BLK, BLK, 2)
+        wanted.append(jnp.where(on[:, :, None], piece, jnp.zeros((), BF)))
+    factor, raw = spread(cov_factor, jnp.concatenate(wanted, axis=2))
+    panel, solved_high, solved_low = solve_twice(factor, raw)
     col_mask = jnp.repeat(hits, BLK, axis=1).astype(BF)
     masked = design * col_mask[:, None, :]
-    start = panel_index[0] * PANEL
-    offset = start - par_id * columns
-    padded = jnp.pad(masked, ((0, 0), (0, 0), (PANEL, PANEL)))
-    window = lax.dynamic_slice_in_dim(
-        padded, jnp.clip(offset + PANEL, 0, columns + PANEL), PANEL, 2
-    )
-    raw = sum_by_parts(window, ("par_0", ("par_1", "par_2")))
-    panel, solved_high, solved_low = solve_twice(factor, raw)
     gram = jnp.einsum(
-        "haop,aoc->pc",
+        "haop,aoc->cp",
         jnp.stack([solved_high, solved_low]),
         masked,
         preferred_element_type=F32,
     )
+    devices = lax.axis_size("arc")
+    share = columns // devices
+    tiles = gram.astype(BF).reshape(devices, share, PANEL)
+    arrived = lax.all_to_all(tiles, "arc", split_axis=0, concat_axis=0, tiled=True)
     block = jnp.einsum("aop,aoq->pq", panel, panel, preferred_element_type=F32)
-    share = columns // lax.axis_size("arc")
-    tiles = in_blocks(gram.astype(BF), 1, lax.axis_size("arc"))
-    arrived = lax.all_to_all(tiles, "arc", split_axis=0, concat_axis=0, tiled=True)
-    block = lax.psum(block, "arc")
-    gram = arrived.astype(F32).sum(axis=0)
+    upper = jnp.concatenate(
+        [block[i * 128 : i * 128 + 128, j * 128 : j * 128 + 128] for i, j in tile_list(PANEL)], axis=0
+    )
     reg_panel = lax.dynamic_slice_in_dim(reg_diag, start, PANEL)
-    global_cols = par_id * columns + arc_id * share + jnp.arange(share, dtype=jnp.int32)
-    rows_at = start + jnp.arange(PANEL, dtype=jnp.int32)
-    shifted = gram + jnp.where(
-        global_cols[None, :] == rows_at[:, None], reg_panel[:, None], jnp.float32(0.0)
-    )
-    return last_solve(block, reg_panel, shifted)
+    inverse = factor_inverse(total_over_arc(upper), reg_panel)
+    shift = (par_id * columns + arc_id * share - start).astype(jnp.int32)[None]
+    return apply_inverse(shift, arrived, inverse, reg_panel)
 
 
 def solution(mesh):

time: 346 us -> 194 us (0.56)
  waiting for transfers between devices: 159 us -> 0.01 us
  Pallas kernels: 44.1 us -> 167 us
  blocking collectives: 95.9 us -> 0 us
  between operations: 14.2 us -> 0.89 us
  local copies, waits for them, and re-layouts: 9.95 us -> 5.42 us
    pallas_call x1 -> x4, Pallas kernels: 18.2 us -> 141 us  [the longest x1 75.5 us: spread(): pl.pallas_call(spread_kernel, out_shape=(jax.ShapeDtypeStruct((arcs, 16,...]
    all_to_all x4 -> x0, blocking collectives: 95.9 us -> none  [the longest x2 42.1 us: from_everyone(): return lax.all_to_all(copies, axis, split_axis=0, concat_axis=0, tiled=True)]
    all_gather x1 -> x0, waiting for transfers between devices: 85.3 us -> none  [on_device(): factor = lax.all_gather(cov_factor, PAR, axis=1, tiled=True)]
    psum x1 -> x0, waiting for transfers between devices: 37.6 us -> none  [on_device(): block = lax.psum(block, 'arc')]
    all_to_all x1, waiting for transfers between devices: 35.7 us -> 0.01 us  [on_device(): lax.all_to_all(tiles, 'arc', split_axis=0, concat_axis=0, tiled=True)]
  transfers between devices with their start and end apart: 3 -> 1, of which waited for: 3 -> 0; matrix products, arithmetic and copies ran while one was open for 3% -> 1% of each run, Pallas kernels for 0% -> 32%
where the time goes in v2:
time: 194 us
  Pallas kernels  167 us (86%)
  other arithmetic  8.03 us (4%)
  starting transfers between devices  7.62 us (4%)
  matrix products  5.52 us (3%)
  local copies, waits for them, and re-layouts  5.42 us (3%)
    pallas_call x1, Pallas kernels, spread(): pl.pallas_call(spread_kernel, out_shape=(jax.ShapeDtypeStruct((arcs, 16,...  75.5 us
    pallas_call x1, Pallas kernels, total_over_arc(): pl.pallas_call(total_kernel, out_shape=jax.ShapeDtypeStruct(part.shape, F...  44 us
    pallas_call x1, Pallas kernels, solve_twice(): pl.pallas_call(functools.partial(solve_kernel, arcs), out_shape=(out, out...  25.6 us
    pallas_call x1, Pallas kernels, factor_inverse(): pl.pallas_call(factor_kernel, out_shape=jax.ShapeDtypeStruct((size, size)...  18.1 us
    all_to_all x1, starting transfers between devices, on_device(): lax.all_to_all(tiles, 'arc', split_axis=0, concat_axis=0, tiled=True)  7.62 us
    dot_general x1, matrix products, on_device(): jnp.einsum('haop,aoc->cp', jnp.stack([solved_high, solved_low]), masked,...  4.24 us
  transfers between devices with their start and end apart: 1, of which 0 were waited for; matrix products, arithmetic and copies ran while one was open for 1% of the time, Pallas kernels for 32%

profile of v2, /device:TPU:1, one launch (start us, length us, event | category | flops | bytes accessed | tf_op | source)
XLA Modules:
  0.0 194.0 jit_solution(4621910737239583898)
XLA Ops:
  0.7 0.9 compare_reduce_fusion
  1.6 0.1 broadcast_bitcast_fusion
  1.7 0.2 and_reduce_fusion.1
  1.9 2.4 %dynamic-slice_select_fusion.1 = (bf16[2,1024,256]{2,1,0:T(8,128)(2,1)S(1)}, bf16[2,1024,256]{2,1,0:T(8,128)(2,1)S(1)}) fusion(bf16[2,1024,1280]{2,1,0:T(8,128)(2,1)} %param.5, s32[]{:T(128)S(6)} %select_n.25, pred[2]{0:T(512)(128)(4,1)S(1)} %get-tuple-element.15, s32[]{:T(128)S(6)} %select_n.27, pred[2]{0:T(512)(128)(4,1)S(1)} %get-tuple-element.16), kind=kLoop, calls=%fused_computation.9 | loop fusion | flops 1048576 | bytes 4194316 | tf_op jit(solution)/shard_map/jit(_where)/select_n | solution.py:574
  4.4 1.5 pad_maximum_fusion.win_ref
  5.9 0.0 slice-start
  5.9 75.5 %shard_map.55 = (f32[2,16,9,32,128]{4,3,2,1,0:T(8,128)}, bf16[2,1024,512]{2,1,0:T(8,128)(2,1)}) custom-call(f32[2,32,1024]{2,1,0:T(8,128)} %cov_ref.1, bf16[2,1024,512]{2,1,0:T(8,128)(2,1)} %pad_maximum_fusion.win_ref), custom_call_target="tpu_custom_call" | custom-call | tf_op jit(solution)/shard_map/pallas_call | solution.py:464
  81.5 0.0 slice-start.1
  81.5 25.6 %shard_map.56 = (bf16[2,1024,512]{2,1,0:T(8,128)(2,1)}, bf16[2,1024,512]{2,1,0:T(8,128)(2,1)}, bf16[2,1024,512]{2,1,0:T(8,128)(2,1)}) custom-call(f32[2,16,9,32,128]{4,3,2,1,0:T(8,128)} %get-tuple-element.10.factor_ref, bf16[2,1024,512]{2,1,0:T(8,128)(2,1)} %get-tuple-element.11.rhs_ref), custom_call_target="tpu_custom_call" | custom-call | tf_op jit(solution)/shard_map/pallas_call | solution.py:159
  107.1 2.9 %convert_reduce_fusion = bf16[2,1024,512]{2,1,0:T(8,128)(2,1)S(1)} fusion(bf16[1,2,1024,512]{3,2,1,0:T(8,128)(2,1)} %bitcast.19, bf16[1,2,1024,512]{3,2,1,0:T(8,128)(2,1)} %bitcast.18), kind=kLoop, calls=%fused_computation | loop fusion | flops 9437184 | bytes 6291456 | tf_op jit(solution)/shard_map/haop,aoc->cp/reduce_sum | solution.py:579
  110.0 0.0 slice-done
  110.1 0.0 slice-done.1
  110.1 4.2 %fusion.5 = bf16[1280,512]{1,0:T(8,128)(2,1)} fusion(bf16[2,1024,512]{2,1,0:T(8,128)(2,1)S(1)} %convert_reduce_fusion, bf16[2,1024,1280]{2,1,0:T(8,128)(2,1)S(1)} %bitcast.22, bf16[2,1280]{1,0:T(2,128)(2,1)S(1)} %bitcast.25), kind=kOutput, calls=%fused_computation.4 | convolution fusion | flops 2686976000 | bytes 8655872 | tf_op jit(solution)/shard_map/haop,aoc->cp/dot_general | solution.py:579
  114.3 0.0 copy-start
  114.3 7.6 %all-to-all-start = ((bf16[8,160,512]{2,1,0:T(8,128)(2,1)}), bf16[8,160,512]{2,1,0:T(8,128)(2,1)S(1)}, u32[]{:S(2)}, u32[]{:S(2)}) async-start(bf16[8,160,512]{2,1,0:T(8,128)(2,1)} %bitcast.20), calls=%async_computation | async-start | bytes 2621440 | tf_op jit(solution)/shard_map/all_to_all | solution.py:588
  121.9 0.0 copy-done
  121.9 1.3 convolution_bitcast_fusion
  123.4 0.0 copy-start.2
  123.4 0.9 copy-done.2
  124.3 44.0 %shard_map.57.block_ref = f32[1280,128]{1,0:T(8,128)} custom-call(f32[1280,128]{1,0:T(8,128)} %copy-done.2), custom_call_target="tpu_custom_call" | custom-call | flops 20000000000 | bytes 40000000 | tf_op jit(solution)/shard_map/pallas_call | solution.py:536
  168.3 1.3 dynamic_slice.19
  169.6 18.1 %shard_map.58.inverse_ref = f32[512,512]{1,0:T(8,128)} custom-call(f32[1280,128]{1,0:T(8,128)} %shard_map.57.block_ref, f32[1,512]{1,0:T(1,128)} %bitcast.23), custom_call_target="tpu_custom_call" | custom-call | flops 30000001024 | bytes 60000000 | tf_op jit(solution)/shard_map/pallas_call | solution.py:262
  187.8 0.0 all-to-all-done.arrived_ref
  187.8 0.0 copy-start.1
  187.8 1.1 copy-done.1
  188.8 3.2 %shard_map.59 = f32[512,160]{1,0:T(8,128)} custom-call(s32[1]{0:T(128)} %bitcast.1.shift_ref, bf16[8,160,512]{2,1,0:T(8,128)(2,1)} %copy-done.1, f32[512,512]{1,0:T(8,128)} %shard_map.58.inverse_ref, f32[1,512]{1,0:T(1,128)} %bitcast.24), custom_call_target="tpu_custom_call" | custom-call | tf_op jit(solution)/shard_map/pallas_call | solution.py:285
  192.1 1.9 %copy.16 = f32[512,160]{0,1:T(8,128)} copy(f32[512,160]{1,0:T(8,128)} %shard_map.59) | data formatting | bytes 655360 | tf_op jit(solution)/shard_map/pallas_call | solution.py:285
  (13 shorter events, 0.1 us)
Async XLA Ops:
  5.9 104.1 %slice-start = ((s8[5242880]{0:T(1024)(128)(4,1)}), s8[4194304]{0:T(1024)(128)(4,1)S(1)}, s32[]{:S(2)}) async-start(s8[5242880]{0:T(1024)(128)(4,1)} %bitcast.21), calls=%async_computation.1 | async-start | bytes 8388608
  81.5 28.6 %slice-start.1 = ((s8[5242880]{0:T(1024)(128)(4,1)}), s8[1048576]{0:T(1024)(128)(4,1)S(1)}, s32[]{:S(2)}) async-start(s8[5242880]{0:T(1024)(128)(4,1)} %bitcast.21), calls=%async_computation.2 | async-start | bytes 2097152
  114.3 7.6 %copy-start = (bf16[2,1024,512]{2,1,0:T(8,128)(2,1)S(1)}, bf16[2,1024,512]{2,1,0:T(8,128)(2,1)}, u32[]{:S(2)}) copy-start(bf16[2,1024,512]{2,1,0:T(8,128)(2,1)} %get-tuple-element.14) | copy-start | bytes 6291460
  114.3 73.4 %all-to-all-start = ((bf16[8,160,512]{2,1,0:T(8,128)(2,1)}), bf16[8,160,512]{2,1,0:T(8,128)(2,1)S(1)}, u32[]{:S(2)}, u32[]{:S(2)}) async-start(bf16[8,160,512]{2,1,0:T(8,128)(2,1)} %bitcast.20), calls=%async_computation | async-start | bytes 2621440 | tf_op jit(solution)/shard_map/all_to_all | solution.py:588
  123.4 0.9 copy-start.2
  187.8 1.1 copy-start.1

commit v3 on v2

--- a/solution.py
+++ b/solution.py
@@ -66,20 +66,39 @@
     return [jnp.concatenate(inv, axis=0) for inv in inverse]
 
 
-def spot_of(arc, row_slab, piece):
-    big = row_slab // 16
-    pair = row_slab + big * (31 - 2 * row_slab)
-    near, far = lax.rem(pair, 4) if not isinstance(pair, int) else pair % 4, pair // 4
+def dot2(a, b, dims=((1,), (0,))):
+    bh, bl = b
+    return dot_by(a, bh, dims) + dot_by(a, bl, dims)
+
+
+def spot_of(arc, slab):
+    big = slab // 16
+    pair = slab + big * (31 - 2 * slab)
+    far = pair // 4
+    near = pair - 4 * far
     place = (1 - arc) * (4 * far + near) + arc * (4 * near + far)
-    return place, piece + big * (far + 1)
+    return place, big, big * far
 
 
 def tile_of(ref, arc, row, column):
-    pieces = [ref[(arc, *spot_of(arc, 4 * row + i, column))] for i in range(4)]
+    pieces = []
+    for i in range(4):
+        place, _, shift = spot_of(arc, 4 * row + i)
+        pieces.append(ref[arc, place, shift + column])
     return jnp.concatenate(pieces, axis=0)
 
 
-def solve_kernel(arcs, factor_ref, rhs_ref, y_ref, qh_ref, ql_ref, inv, fh, fl, wh, wl, yh, yl):
+def diagonal_of(ref, arc, row):
+    pieces = []
+    for i in range(4):
+        place, big, _ = spot_of(arc, 4 * row + i)
+        pieces.append(
+            ref[arc, place, 7 + 2 * big].astype(F32) + ref[arc, place, 8 + 2 * big].astype(F32)
+        )
+    return jnp.concatenate(pieces, axis=0)
+
+
+def solve_kernel(arcs, factor_ref, rhs_ref, block_ref, qh_ref, ql_ref, inv, fh, wh, wl, yh, yl):
     size = rhs_ref.shape[1]
     tiles = size // 128
 
@@ -91,7 +110,7 @@
             arc, tile = at // tiles, lax.rem(at, tiles)
             spot = pl.ds(pl.multiple_of(tile * 128, 128), 128)
             found.append((arc, spot, tile))
-        values = [tile_of(factor_ref, arc, tile, tile) for arc, spot, tile in found]
+        values = [diagonal_of(factor_ref, arc, tile) for arc, spot, tile in found]
         low = lanes((64, 128)) < 64
         for (arc, spot, _), value, done in zip(found, values, invert_tiles(values)):
             first = jnp.where(low, done, 0.0)
@@ -109,7 +128,7 @@
             r = b * OBS_STEP
             one, two = inv[arc, r : r + 128, :], inv[arc, r + 128 : r + 256, :]
             cross = tile_of(factor_ref, arc, 2 * b + 1, 2 * b)
-            corner = -dot3(halves(two), halves(dot3(halves(cross), halves(one))))
+            corner = -dot3(halves(two), halves(dot2(cross, halves(one))))
             zero = jnp.zeros((128, 128), BF)
             for (ref, a, c, d) in zip((wh, wl), halves(one), halves(corner), halves(two)):
                 ref[arc, r : r + 128, 0:128] = a
@@ -118,9 +137,9 @@
                 ref[arc, r + 128 : r + 256, 128:256] = d
             for row in (2 * b, 2 * b + 1):
                 for column in range(2 * b):
-                    high, less = halves(tile_of(factor_ref, arc, row, column))
-                    fh[arc, row * 128 : row * 128 + 128, column * 128 : column * 128 + 128] = high
-                    fl[arc, row * 128 : row * 128 + 128, column * 128 : column * 128 + 128] = less
+                    fh[arc, row * 128 : row * 128 + 128, column * 128 : column * 128 + 128] = tile_of(
+                        factor_ref, arc, row, column
+                    )
 
     for b in range(blocks):
         r = b * OBS_STEP
@@ -128,14 +147,11 @@
         for arc in range(arcs):
             value = rhs_ref[arc, here, :].astype(F32)
             if b:
-                value = value - dot3(
-                    (fh[arc, here, 0:r], fl[arc, here, 0:r]), (yh[arc, 0:r, :], yl[arc, 0:r, :])
-                )
+                value = value - dot2(fh[arc, here, 0:r], (yh[arc, 0:r, :], yl[arc, 0:r, :]))
             value = dot3((wh[arc, here, :], wl[arc, here, :]), halves(value))
             high, less = halves(value)
             yh[arc, here, :] = high
             yl[arc, here, :] = less
-            y_ref[arc, here, :] = high
     flip = ((0,), (0,))
     for b in reversed(range(blocks)):
         r = b * OBS_STEP
@@ -143,27 +159,31 @@
         for arc in range(arcs):
             value = yh[arc, here, :].astype(F32) + yl[arc, here, :].astype(F32)
             if b + 1 < blocks:
-                value = value - dot3(
-                    (fh[arc, after, here], fl[arc, after, here]),
-                    (qh_ref[arc, after, :], ql_ref[arc, after, :]),
-                    flip,
+                value = value - dot2(
+                    fh[arc, after, here], (qh_ref[arc, after, :], ql_ref[arc, after, :]), flip
                 )
             value = dot3((wh[arc, here, :], wl[arc, here, :]), halves(value), flip)
             qh_ref[arc, here, :], ql_ref[arc, here, :] = halves(value)
+    at = 0
+    for i in range(0, rhs_ref.shape[2], 128):
+        strip = sum(dot_by(yh[arc, :, i : i + 128], yh[arc, :, i:], flip) for arc in range(arcs))
+        for j in range(0, strip.shape[1], 128):
+            block_ref[at : at + 128, :] = strip[:, j : j + 128]
+            at += 128
 
 
 def solve_twice(factor, rhs):
     arcs, size, width = rhs.shape
     vm = pltpu.VMEM
     out = jax.ShapeDtypeStruct(rhs.shape, BF)
+    tiles = len(tile_list(width))
     return pl.pallas_call(
         functools.partial(solve_kernel, arcs),
-        out_shape=(out, out, out),
+        out_shape=(jax.ShapeDtypeStruct((tiles * 128, 128), F32), out, out),
         in_specs=[pl.BlockSpec(memory_space=vm)] * 2,
         out_specs=(pl.BlockSpec(memory_space=vm),) * 3,
         scratch_shapes=[
             vm((arcs, size, 128), F32),
-            vm((arcs, size, size), BF),
             vm((arcs, size, size), BF),
             vm((arcs, size, OBS_STEP), BF),
             vm((arcs, size, OBS_STEP), BF),
@@ -241,7 +261,7 @@
     return [(i, j) for i in range(size // 128) for j in range(i, size // 128)]
 
 
-def factor_kernel(block_ref, reg_ref, out_ref, work):
+def factor_kernel(at_ref, block_ref, reg_ref, out_ref, work):
     size = out_ref.shape[0]
     square = (128, 128)
     eye = lanes(square) == rows_of(square)
@@ -249,46 +269,118 @@
     for at, (i, j) in enumerate(tile_list(size)):
         value = block_ref[at * 128 : at * 128 + 128, :]
         if i == j:
-            value = value + jnp.where(eye, reg_ref[:, i * 128 : i * 128 + 128], 0.0)
+            value = value + jnp.where(eye, reg_ref[0, :, i * 128 : i * 128 + 128], 0.0)
             work[i * 128 : i * 128 + 128, size + i * 128 : size + i * 128 + 128] = jnp.where(eye, 1.0, 0.0)
         work[i * 128 : i * 128 + 128, j * 128 : j * 128 + 128] = value
     factor_and_invert(work)
     out_ref[...] = work[:, size:]
 
 
-def factor_inverse(block, reg_panel):
-    size = reg_panel.shape[0]
-    vm = pltpu.VMEM
+def whole(shape):
+    return pl.BlockSpec(shape, lambda i, at: (0,) * len(shape))
+
+
+def factor_inverse(at, block, reg):
+    size = reg.shape[-1]
     return pl.pallas_call(
         factor_kernel,
         out_shape=jax.ShapeDtypeStruct((size, size), F32),
-        in_specs=[pl.BlockSpec(memory_space=vm)] * 2,
-        out_specs=pl.BlockSpec(memory_space=vm),
-        scratch_shapes=[vm((size, 2 * size), F32)],
+        grid_spec=pltpu.PrefetchScalarGridSpec(
+            num_scalar_prefetch=1,
+            grid=(1,),
+            in_specs=[whole(block.shape), pl.BlockSpec((1, 1, size), lambda i, at: (at[0], 0, 0))],
+            out_specs=whole((size, size)),
+            scratch_shapes=[pltpu.VMEM((size, 2 * size), F32)],
+        ),
         compiler_params=pltpu.CompilerParams(vmem_limit_bytes=KERNEL_VMEM),
         cost_estimate=pl.CostEstimate(flops=30_000_000_000, bytes_accessed=60_000_000, transcendentals=0),
-    )(block, reg_panel[None])
-
-
-def apply_kernel(shift_ref, arrived_ref, inverse_ref, reg_ref, out_ref):
-    total = arrived_ref[0].astype(F32)
-    for part in range(1, arrived_ref.shape[0]):
-        total = total + arrived_ref[part].astype(F32)
-    on = rows_of(total.shape) + shift_ref[0] == lanes(total.shape)
-    total = total + jnp.where(on, reg_ref[...], 0.0)
-    out_ref[...] = dot3(halves(inverse_ref[...]), halves(total), ((1,), (1,)))
-
-
-def apply_inverse(shift, arrived, inverse, reg_panel):
-    _, share, size = arrived.shape
-    vm = pltpu.VMEM
+    )(at, block, reg)
+
+
+def apply_kernel(at_ref, arrived_ref, own_ref, inverse_ref, reg_ref, out_ref):
+    total = own_ref[...]
+    for part in range(arrived_ref.shape[0]):
+        total = total + jnp.where(at_ref[2] == part, 0.0, arrived_ref[part].astype(F32))
+    on = rows_of(total.shape) + at_ref[1] == lanes(total.shape)
+    total = total + jnp.where(on, reg_ref[0], 0.0)
+    out_ref[...] = dot3(halves(total), halves(inverse_ref[...]), ((1,), (1,)))
+
+
+def apply_inverse(at, arrived, own, inverse, reg):
+    share, size = own.shape
     return pl.pallas_call(
         apply_kernel,
-        out_shape=jax.ShapeDtypeStruct((size, share), F32),
-        in_specs=[pl.BlockSpec(memory_space=pltpu.SMEM)] + [pl.BlockSpec(memory_space=vm)] * 3,
-        out_specs=pl.BlockSpec(memory_space=vm),
+        out_shape=jax.ShapeDtypeStruct((share, size), F32),
+        grid_spec=pltpu.PrefetchScalarGridSpec(
+            num_scalar_prefetch=1,
+            grid=(1,),
+            in_specs=[
+                whole(arrived.shape),
+                whole(own.shape),
+                whole(inverse.shape),
+                pl.BlockSpec((1, 1, size), lambda i, at: (at[0], 0, 0)),
+            ],
+            out_specs=whole((share, size)),
+        ),
         compiler_params=pltpu.CompilerParams(vmem_limit_bytes=KERNEL_VMEM),
-    )(shift, arrived, inverse, reg_panel[None])
+    )(at, arrived, own, inverse, reg)
+
+
+def window_kernel(at_ref, on_ref, design_ref, out_ref):
+    part = pl.program_id(0)
+    for arc in range(out_ref.shape[0]):
+        on = on_ref[part * out_ref.shape[0] + arc] > 0
+        out_ref[arc] = jnp.where(on, design_ref[arc], jnp.zeros((), BF))
+
+
+def window_of(at, on, design):
+    arcs, observed, _ = design.shape
+    parts = at.shape[0]
+    block = (arcs, observed, BLK)
+    return pl.pallas_call(
+        window_kernel,
+        out_shape=jax.ShapeDtypeStruct((arcs, observed, parts * BLK), BF),
+        grid_spec=pltpu.PrefetchScalarGridSpec(
+            num_scalar_prefetch=2,
+            grid=(parts,),
+            in_specs=[pl.BlockSpec(block, lambda i, at, on: (0, 0, at[i]))],
+            out_specs=pl.BlockSpec(block, lambda i, at, on: (0, 0, i)),
+        ),
+        compiler_params=pltpu.CompilerParams(vmem_limit_bytes=KERNEL_VMEM),
+    )(at, on, design)
+
+
+def gram_kernel(on_ref, design_ref, qh_ref, ql_ref, out_ref):
+    arcs = design_ref.shape[0]
+    out_ref[...] = jnp.zeros_like(out_ref)
+    for arc in range(arcs):
+
+        @pl.when(on_ref[pl.program_id(0) * arcs + arc] > 0)
+        def _():
+            flip = ((0,), (0,))
+            out_ref[...] += dot_by(design_ref[arc], qh_ref[arc], flip) + dot_by(
+                design_ref[arc], ql_ref[arc], flip
+            )
+
+
+def gram_of(on, design, high, less):
+    arcs, observed, columns = design.shape
+    width = high.shape[2]
+    return pl.pallas_call(
+        gram_kernel,
+        out_shape=jax.ShapeDtypeStruct((columns, width), F32),
+        grid_spec=pltpu.PrefetchScalarGridSpec(
+            num_scalar_prefetch=1,
+            grid=(columns // BLK,),
+            in_specs=[
+                pl.BlockSpec((arcs, observed, BLK), lambda i, on: (0, 0, i)),
+                whole(high.shape),
+                whole(less.shape),
+            ],
+            out_specs=pl.BlockSpec((BLK, width), lambda i, on: (i, 0)),
+        ),
+        compiler_params=pltpu.CompilerParams(vmem_limit_bytes=KERNEL_VMEM),
+    )(on, design, high, less)
 
 
 MESH = pl.DeviceIdType.MESH
@@ -343,10 +435,17 @@
     held = small + z * (9 - 2 * small)
 
     def piece(c):
-        spot = pl.ds(pl.multiple_of(c * 128, 128), 128)
-        return remote(cov_ref.at[:, :, spot], slabs.at[z, :, :, spot], ls.at[c], lr.at[c], partner)
-
+        return remote(slabs.at[z, c], slabs.at[z, c], ls.at[c], lr.at[c], partner)
+
+    def came(c):
+        return remote(slabs.at[1 - z, c], slabs.at[1 - z, c], ls.at[c], lr.at[c], partner)
+
+    last = cov_ref[:, :, pl.ds(pl.multiple_of((held - 1) * 128, 128), 128)]
+    slabs[z, 8] = (last - last.astype(BF).astype(F32)).astype(BF)
+    for c in range(8):
+        slabs[z, c] = cov_ref[:, :, c * 128 : c * 128 + 128].astype(BF)
     pl.loop(0, held)(lambda c: piece(c).start())
+    piece(8).start()
     scatter1 = [
         remote(
             win_ref.at[arc, pl.ds(pl.multiple_of(lax.rem(outer[arc][0] + k, 4) * 256, 256), 256)],
@@ -357,24 +456,25 @@
     ]
     for copy in scatter1:
         copy.start()
-    slabs[z] = cov_ref[...]
-    pl.loop(0, 9 - held)(lambda c: piece(c).wait_recv())
-
-    @pl.loop(0, small)
-    def _(c):
-        spot = pl.ds(pl.multiple_of(c * 128, 128), 128)
-        for arc in range(arcs):
-            place = 4 * turned(outer[arc][0]) + turned(inner[arc][0])
-            fac_ref[arc, place, c] = slabs[0, arc, :, spot]
-
-    @pl.loop(0, 9 - small)
-    def _(c):
-        spot = pl.ds(pl.multiple_of(c * 128, 128), 128)
-        for arc in range(arcs):
-            place = 4 * turned(outer[arc][0]) + turned(inner[arc][0])
-            fac_ref[arc, place, small + c] = slabs[1, arc, :, spot]
-
-    def l_unit(arc, cut=slice(0, 9)):
+    pl.loop(0, 9 - held)(lambda c: came(c).wait_recv())
+    came(8).wait_recv()
+    for arc in range(arcs):
+        place = 4 * turned(outer[arc][0]) + turned(inner[arc][0])
+
+        @pl.loop(0, small - 1)
+        def _(c):
+            fac_ref[arc, place, c] = slabs[0, c, arc]
+
+        @pl.loop(0, 8 - small)
+        def _(c):
+            fac_ref[arc, place, small - 1 + c] = slabs[1, c, arc]
+
+        fac_ref[arc, place, 7] = slabs[0, small - 1, arc]
+        fac_ref[arc, place, 8] = slabs[0, 8, arc]
+        fac_ref[arc, place, 9] = slabs[1, 8 - small, arc]
+        fac_ref[arc, place, 10] = slabs[1, 8, arc]
+
+    def l_unit(arc, cut=slice(0, 11)):
         size = cut.stop - cut.start
         return lambda r: fac_ref.at[
             arc, 4 * turned(outer[arc][0]) + turned(r), pl.ds(cut.start, size)
@@ -428,7 +528,7 @@
                 )
             ])
     arrive(l1)
-    l2 = begin(far(lambda a: l_unit(a, slice(0, 5)), lambda a: l_unit(a, slice(5, 9)), inner, 0, gls, glr))
+    l2 = begin(far(lambda a: l_unit(a, slice(0, 6)), lambda a: l_unit(a, slice(6, 11)), inner, 0, gls, glr))
     arrive(scatter2)
     across = []
     for arc in two:
@@ -453,6 +553,7 @@
     arrive(l4)
     arrive(g4)
     pl.loop(0, held)(lambda c: piece(c).wait_send())
+    piece(8).wait_send()
     for copy in sent + scatter2 + across + l1 + l2 + l3 + l4 + g1 + g2 + g3 + g4:
         copy.wait_send()
 
@@ -464,19 +565,19 @@
     return pl.pallas_call(
         spread_kernel,
         out_shape=(
-            jax.ShapeDtypeStruct((arcs, 16, 9, lines, 128), F32),
+            jax.ShapeDtypeStruct((arcs, 16, 11, lines, 128), BF),
             jax.ShapeDtypeStruct(window.shape, BF),
         ),
         in_specs=[pl.BlockSpec(memory_space=vm)] * 2,
         out_specs=(pl.BlockSpec(memory_space=vm),) * 2,
         scratch_shapes=[
-            vm((2, arcs, lines, size), F32),
+            vm((2, 9, arcs, lines, 128), BF),
             vm((arcs, 3, 256, width), BF),
             vm((arcs, 3, 64, width), BF),
             vm((arcs, 64, width), BF),
             vm((arcs, 256, width), BF),
             vm((arcs, 64, width), BF),
-            dma((8,)), dma((8,)),
+            dma((9,)), dma((9,)),
             dma((arcs, 3)), dma((arcs, 3)), dma((arcs, 3)), dma((arcs, 3)),
             dma((arcs,)), dma((arcs,)),
             dma((arcs, 2, 4)), dma((arcs, 2, 4)), dma((arcs, 2, 4)), dma((arcs, 2, 4)),
@@ -487,18 +588,22 @@
     )(cov, window)
 
 
-def total_kernel(part_ref, out_ref, kept, mate, got, ps, pr, rs, rr, gs, gr, fs, fr):
-    me = lax.axis_index("arc")
-    core, chip = lax.rem(me, 2), me // 2
-    other = {"arc": chip * 2 + 1 - core}
+def total_kernel(
+    part_ref, gram_ref, out_ref, sum_ref, own_ref, kept, mate, got, pair,
+    ps, pr, qs, qr, rs, rr, gs, gr, fs, fr,
+):
+    chip, core = lax.axis_index("line"), lax.axis_index("core")
+    other = {"core": 1 - core}
     chips = [lax.rem(chip + k, 4) for k in (1, 2, 3)]
-    peers = [{"arc": c * 2 + core} for c in chips]
+    peers = [{"line": c} for c in chips]
     meet(peers + [other])
     half = part_ref.shape[0] // 2
     quarter = half // 4
     rows = lambda base, n: pl.ds(pl.multiple_of(base, 32), n)
     swap = remote(part_ref.at[rows((1 - core) * half, half)], mate, ps, pr, other)
     swap.start()
+    trade = remote(gram_ref.at[:, 1 - core], pair, qs, qr, other)
+    trade.start()
     swap.wait_recv()
     kept[...] = part_ref[rows(core * half, half), :] + mate[...]
     scatter = [
@@ -507,6 +612,10 @@
     ]
     for copy in scatter:
         copy.start()
+    trade.wait_recv()
+    for c in range(4):
+        sum_ref[c] = (gram_ref[c, core] + pair[c]).astype(BF)
+    own_ref[...] = gram_ref[chip, core] + pair[chip]
     for copy in scatter:
         copy.wait_recv()
     mine = rows(core * half + chip * quarter, quarter)
@@ -526,84 +635,81 @@
         forward.append(copy)
     for copy in forward:
         copy.wait_recv()
-    for copy in [swap] + scatter + gather + forward:
+    for copy in [swap, trade] + scatter + gather + forward:
         copy.wait_send()
 
 
-def total_over_arc(part):
+def total_over_arc(part, gram):
     lines, width = part.shape
+    chips, _, share, size = gram.shape
     vm, dma = pltpu.VMEM, pltpu.SemaphoreType.DMA
     return pl.pallas_call(
         total_kernel,
-        out_shape=jax.ShapeDtypeStruct(part.shape, F32),
-        in_specs=[pl.BlockSpec(memory_space=vm)],
-        out_specs=pl.BlockSpec(memory_space=vm),
+        out_shape=(
+            jax.ShapeDtypeStruct(part.shape, F32),
+            jax.ShapeDtypeStruct((chips, share, size), BF),
+            jax.ShapeDtypeStruct((share, size), F32),
+        ),
+        in_specs=[pl.BlockSpec(memory_space=vm)] * 2,
+        out_specs=(pl.BlockSpec(memory_space=vm),) * 3,
         scratch_shapes=[
             vm((lines // 2, width), F32),
             vm((lines // 2, width), F32),
             vm((3, lines // 8, width), F32),
-            dma, dma, dma((3,)), dma((3,)), dma((3,)), dma((3,)), dma((4,)), dma((4,)),
+            vm((chips, share, size), F32),
+            dma, dma, dma, dma, dma((3,)), dma((3,)), dma((3,)), dma((3,)), dma((4,)), dma((4,)),
         ],
         compiler_params=pltpu.CompilerParams(
             vmem_limit_bytes=KERNEL_VMEM, collective_id=1, has_side_effects=True
         ),
-        cost_estimate=pl.CostEstimate(flops=20_000_000_000, bytes_accessed=40_000_000, transcendentals=0),
-    )(part)
+    )(part, gram)
 
 
 PANEL = 512
 BLK = 256
 PAR = ("par_0", "par_1", "par_2")
-PAR_ARC = ("par_0", "par_1", "par_2", "arc")
 
 
 def on_device(design, cov_factor, active_blocks, panel_index, reg_diag):
     arcs, observed, columns = design.shape
     local_blocks = columns // BLK
     par_id = lax.axis_index(PAR)
-    arc_id = lax.axis_index("arc")
+    chip, core = lax.axis_index("line"), lax.axis_index("core")
     start = panel_index[0] * PANEL
     block_ids = par_id * local_blocks + jnp.arange(local_blocks, dtype=jnp.int32)
     hits = jnp.any(active_blocks[:, :, None] == block_ids[None, None, :], axis=1)
-    wanted = []
-    for part in range(PANEL // BLK):
-        local = start // BLK + part - par_id * local_blocks
-        kept = jnp.clip(local, 0, local_blocks - 1)
-        on = (local == kept) & lax.dynamic_slice_in_dim(hits, kept, 1, 1)
-        piece = lax.dynamic_slice_in_dim(design, kept * BLK, BLK, 2)
-        wanted.append(jnp.where(on[:, :, None], piece, jnp.zeros((), BF)))
-    factor, raw = spread(cov_factor, jnp.concatenate(wanted, axis=2))
-    panel, solved_high, solved_low = solve_twice(factor, raw)
-    col_mask = jnp.repeat(hits, BLK, axis=1).astype(BF)
-    masked = design * col_mask[:, None, :]
-    gram = jnp.einsum(
-        "haop,aoc->cp",
-        jnp.stack([solved_high, solved_low]),
-        masked,
-        preferred_element_type=F32,
+    parts = jnp.arange(PANEL // BLK, dtype=jnp.int32)
+    wanted = panel_index[0] * (PANEL // BLK) + parts
+    local = wanted - par_id * local_blocks
+    inside = (local >= 0) & (local < local_blocks)
+    active = jnp.any(active_blocks[None] == wanted[:, None, None], axis=2)
+    window = window_of(
+        jnp.clip(local, 0, local_blocks - 1),
+        (inside[:, None] & active).astype(jnp.int32).reshape(-1),
+        design,
     )
-    devices = lax.axis_size("arc")
-    share = columns // devices
-    tiles = gram.astype(BF).reshape(devices, share, PANEL)
-    arrived = lax.all_to_all(tiles, "arc", split_axis=0, concat_axis=0, tiled=True)
-    block = jnp.einsum("aop,aoq->pq", panel, panel, preferred_element_type=F32)
-    upper = jnp.concatenate(
-        [block[i * 128 : i * 128 + 128, j * 128 : j * 128 + 128] for i, j in tile_list(PANEL)], axis=0
-    )
-    reg_panel = lax.dynamic_slice_in_dim(reg_diag, start, PANEL)
-    inverse = factor_inverse(total_over_arc(upper), reg_panel)
-    shift = (par_id * columns + arc_id * share - start).astype(jnp.int32)[None]
-    return apply_inverse(shift, arrived, inverse, reg_panel)
+    factor, raw = spread(cov_factor, window)
+    block, high, less = solve_twice(factor, raw)
+    gram = gram_of(hits.T.astype(jnp.int32).reshape(-1), design, high, less)
+    share = columns // (4 * 2)
+    block, sums, own = total_over_arc(block, gram.reshape(4, 2, share, PANEL))
+    arrived = lax.all_to_all(sums, "line", split_axis=0, concat_axis=0, tiled=True)
+    reg = reg_diag.reshape(-1, 1, PANEL)
+    shift = par_id * columns + (chip * 2 + core) * share - start
+    at = jnp.stack([panel_index[0], shift, chip]).astype(jnp.int32)
+    inverse = factor_inverse(at, block, reg)
+    return apply_inverse(at, arrived, own, inverse, reg).T
 
 
 def solution(mesh):
     split = Mesh(
-        mesh.devices.reshape(mesh.shape["arc"], 2, 4, 4), ("arc", "par_0", "par_1", "par_2")
+        mesh.devices.reshape(mesh.shape["arc"] // 2, 2, 2, 4, 4), ("line", "core") + PAR
     )
+    arc = ("line", "core")
     return jax.shard_map(
         on_device,
         mesh=split,
-        in_specs=(P("arc", None, PAR), P("arc", PAR, None), P("arc", None), P(), P()),
-        out_specs=P(None, PAR_ARC),
+        in_specs=(P(arc, None, PAR), P(arc, PAR, None), P(arc, None), P(), P()),
+        out_specs=P(None, PAR + arc),
         check_vma=False,
     )

time: 194 us -> 162 us (0.84)
  Pallas kernels: 167 us -> 150 us
  matrix products: 5.52 us -> 0 us
  other arithmetic: 8.03 us -> 3.04 us
  local copies, waits for them, and re-layouts: 5.42 us -> 2.19 us
  starting transfers between devices: 7.62 us -> 5.45 us
    pallas_call x1, Pallas kernels: 75.5 us -> 65.6 us  [spread(): pl.pallas_call(spread_kernel, out_shape=(jax.ShapeDtypeStruct((arcs, 16,...]
    pallas_call x3 -> x5, Pallas kernels: 72.8 us -> 65.9 us  [the longest x1 26.2 us: total_over_arc(): pl.pallas_call(total_kernel, out_shape=(jax.ShapeDtypeStruct(part.shape,...]
    dot_general x2 -> x0, matrix products: 5.52 us -> none  [the longest x1 4.24 us: on_device(): jnp.einsum('haop,aoc->cp', jnp.stack([solved_high, solved_low]), masked,...]
    reduce_sum x1 -> x0, other arithmetic: 2.94 us -> none  [on_device(): jnp.einsum('haop,aoc->cp', jnp.stack([solved_high, solved_low]), masked,...]
    select_n x1 -> x0, other arithmetic: 2.45 us -> none  [on_device(): wanted.append(jnp.where(on[:, :, None], piece, jnp.zeros((), BF)))]
    all_to_all x1, starting transfers between devices: 7.62 us -> 5.45 us  [on_device(): lax.all_to_all(sums, 'line', split_axis=0, concat_axis=0, tiled=True)]
    pallas_call x1 -> x0, local copies, waits for them, and re-layouts: 1.94 us -> none  [apply_inverse(): pl.pallas_call(apply_kernel, out_shape=jax.ShapeDtypeStruct((size, share)...]
  transfers between devices with their start and end apart: 1 -> 1, of which waited for: 0 -> 0; matrix products, arithmetic and copies ran while one was open for 1% -> 0% of each run, Pallas kernels for 32% -> 12%
where the time goes in v3:
time: 162 us
  Pallas kernels  150 us (93%)
  starting transfers between devices  5.45 us (3%)
  other arithmetic  3.04 us (2%)
  local copies, waits for them, and re-layouts  2.19 us (1%)
    pallas_call x1, Pallas kernels, spread(): pl.pallas_call(spread_kernel, out_shape=(jax.ShapeDtypeStruct((arcs, 16,...  65.6 us
    pallas_call x1, Pallas kernels, total_over_arc(): pl.pallas_call(total_kernel, out_shape=(jax.ShapeDtypeStruct(part.shape,...  26.2 us
    pallas_call x1, Pallas kernels, solve_twice(): pl.pallas_call(functools.partial(solve_kernel, arcs), out_shape=(jax.Shap...  23.9 us
    pallas_call x1, Pallas kernels, factor_inverse(): pl.pallas_call(factor_kernel, out_shape=jax.ShapeDtypeStruct((size, size)...  18.8 us
    pallas_call x1, Pallas kernels, gram_of(): pl.pallas_call(gram_kernel, out_shape=jax.ShapeDtypeStruct((columns, widt...  8.78 us
    all_to_all x1, starting transfers between devices, on_device(): lax.all_to_all(sums, 'line', split_axis=0, concat_axis=0, tiled=True)  5.45 us
    pallas_call x1, Pallas kernels, apply_inverse(): pl.pallas_call(apply_kernel, out_shape=jax.ShapeDtypeStruct((share, size)...  3.65 us
    pallas_call x1, Pallas kernels, window_of(): pl.pallas_call(window_kernel, out_shape=jax.ShapeDtypeStruct((arcs, obser...  3.37 us
  transfers between devices with their start and end apart: 1, of which 0 were waited for; matrix products, arithmetic and copies ran while one was open for 0% of the time, Pallas kernels for 12%

profile of v3, /device:TPU:1, one launch (start us, length us, event | category | flops | bytes accessed | tf_op | source)
XLA Modules:
  0.0 161.7 jit_solution(10632632612095985822)
XLA Ops:
  0.7 0.5 iota_add_fusion.1
  1.2 0.9 compare_reduce_fusion
  2.1 0.9 compare_reduce_fusion.1
  3.0 0.1 and_convert_fusion
  3.1 0.6 reshape.43.on_ref
  3.7 0.1 copy.6
  3.8 0.6 reshape.45.on_ref
  4.4 3.4 %shard_map.55.win_ref = bf16[2,1024,512]{2,1,0:T(8,128)(2,1)} custom-call(s32[2]{0:T(128)} %get-tuple-element.22.at_ref, s32[4]{0:T(128)} %reshape.43.on_ref, bf16[2,1024,1280]{2,1,0:T(8,128)(2,1)} %design_ref.3), custom_call_target="tpu_custom_call" | custom-call | tf_op jit(solution)/shard_map/pallas_call | solution.py:340
  7.8 65.6 %shard_map.56 = (bf16[2,16,11,32,128]{4,3,2,1,0:T(8,128)(2,1)}, bf16[2,1024,512]{2,1,0:T(8,128)(2,1)}) custom-call(f32[2,32,1024]{2,1,0:T(8,128)} %cov_ref.1, bf16[2,1024,512]{2,1,0:T(8,128)(2,1)} %shard_map.55.win_ref), custom_call_target="tpu_custom_call" | custom-call | tf_op jit(solution)/shard_map/pallas_call | solution.py:565
  73.4 23.9 %shard_map.57 = (f32[1280,128]{1,0:T(8,128)}, bf16[2,1024,512]{2,1,0:T(8,128)(2,1)}, bf16[2,1024,512]{2,1,0:T(8,128)(2,1)}) custom-call(bf16[2,16,11,32,128]{4,3,2,1,0:T(8,128)(2,1)} %get-tuple-element.13.factor_ref, bf16[2,1024,512]{2,1,0:T(8,128)(2,1)} %get-tuple-element.14.rhs_ref), custom_call_target="tpu_custom_call" | custom-call | tf_op jit(solution)/shard_map/pallas_call | solution.py:180
  97.3 8.8 %shard_map.58 = f32[1280,512]{1,0:T(8,128)} custom-call(s32[10]{0:T(128)} %reshape.45.on_ref, bf16[2,1024,1280]{2,1,0:T(8,128)(2,1)} %design_ref.3, bf16[2,1024,512]{2,1,0:T(8,128)(2,1)} %get-tuple-element.16.qh_ref, bf16[2,1024,512]{2,1,0:T(8,128)(2,1)} %get-tuple-element.17.ql_ref), custom_call_target="tpu_custom_call" | custom-call | tf_op jit(solution)/shard_map/pallas_call | solution.py:369
  106.1 26.2 %shard_map.59 = (f32[1280,128]{1,0:T(8,128)}, bf16[4,160,512]{2,1,0:T(8,128)(2,1)}, f32[160,512]{1,0:T(8,128)}) custom-call(f32[1280,128]{1,0:T(8,128)} %get-tuple-element.15.part_ref, f32[4,2,160,512]{3,2,1,0:T(8,128)} %bitcast.9), custom_call_target="tpu_custom_call" | custom-call | tf_op jit(solution)/shard_map/pallas_call | solution.py:646
  132.3 5.5 %all-to-all-start = ((bf16[4,160,512]{2,1,0:T(8,128)(2,1)}), bf16[4,160,512]{2,1,0:T(8,128)(2,1)S(1)}, u32[]{:S(2)}, u32[]{:S(2)}) async-start(bf16[4,160,512]{2,1,0:T(8,128)(2,1)} %get-tuple-element.18), calls=%async_computation | async-start | bytes 1310720 | tf_op jit(solution)/shard_map/all_to_all | solution.py:696
  137.7 0.7 pad_add_fusion.at_ref
  138.4 18.8 %shard_map.60.inverse_ref = f32[512,512]{1,0:T(8,128)} custom-call(s32[3]{0:T(128)} %pad_add_fusion.at_ref, f32[1280,128]{1,0:T(8,128)} %get-tuple-element.20.block_ref, f32[80,1,512]{2,1,0:T(1,128)} %bitcast.10), custom_call_target="tpu_custom_call" | custom-call | flops 30000001024 | bytes 60000000 | tf_op jit(solution)/shard_map/pallas_call | solution.py:285
  157.1 0.0 all-to-all-done.arrived_ref
  157.2 0.0 copy-start
  157.2 0.9 copy-done
  158.0 3.6 %shard_map.61 = f32[160,512]{1,0:T(8,128)} custom-call(s32[3]{0:T(128)} %pad_add_fusion.at_ref, bf16[4,160,512]{2,1,0:T(8,128)(2,1)} %copy-done, f32[160,512]{1,0:T(8,128)} %get-tuple-element.19.own_ref, f32[512,512]{1,0:T(8,128)} %shard_map.60.inverse_ref, f32[80,1,512]{2,1,0:T(1,128)} %bitcast.11), custom_call_target="tpu_custom_call" | custom-call | tf_op jit(solution)/shard_map/pallas_call | solution.py:311
  (3 shorter events, 0.0 us)
Async XLA Ops:
  132.3 24.9 %all-to-all-start = ((bf16[4,160,512]{2,1,0:T(8,128)(2,1)}), bf16[4,160,512]{2,1,0:T(8,128)(2,1)S(1)}, u32[]{:S(2)}, u32[]{:S(2)}) async-start(bf16[4,160,512]{2,1,0:T(8,128)(2,1)} %get-tuple-element.18), calls=%async_computation | async-start | bytes 1310720 | tf_op jit(solution)/shard_map/all_to_all | solution.py:696
  157.2 0.9 copy-start

commit v4 on v3

--- a/solution.py
+++ b/solution.py
@@ -8,6 +8,7 @@
 from jax.sharding import PartitionSpec as P
 
 OBS_STEP = 256
+GROUP = 8
 BF = jnp.bfloat16
 F32 = jnp.float32
 KERNEL_VMEM = 56 * 1024 * 1024
@@ -37,33 +38,53 @@
 
 def invert_tiles(tiles):
     lane = lanes((8, 128))
-    low = lane < 64
-    base = jnp.where(low, 0, 64)
-    packed, inverse = [], []
+    row = rows_of((8, 128))
+    base = lane - lax.rem(lane, 32)
+    packed, inverse, scales = [], [], []
     for tile in tiles:
-        packed.append(
-            [jnp.where(low, tile[8 * g : 8 * g + 8], tile[64 + 8 * g : 72 + 8 * g]) for g in range(8)]
-        )
-        inverse.append(
-            [
-                jnp.where(lane - base == rows_of((8, 128)) + 8 * g, 1.0, 0.0).astype(F32)
-                for g in range(8)
-            ]
-        )
-    for j in range(64):
+        pack, inv, scale = [], [], jnp.zeros((8, 128), F32)
+        for g in range(4):
+            piece = tile[96 + 8 * g : 104 + 8 * g]
+            for part in (2, 1, 0):
+                low = 32 * part + 8 * g
+                piece = jnp.where(base == 32 * part, tile[low : low + 8], piece)
+            pivot = 1.0 / jnp.take_along_axis(piece, base + row + 8 * g, axis=1)
+            on = lane - base == row + 8 * g
+            scale = scale + jnp.where(on, pivot, 0.0)
+            pack.append(piece * pivot)
+            inv.append(jnp.where(on, 1.0, 0.0).astype(F32))
+        packed.append(pack)
+        inverse.append(inv)
+        scales.append(jnp.sum(scale, axis=0, keepdims=True))
+    for j in range(31):
         at, sub = j // 8, j % 8
         index = base + j
         for pack, inv in zip(packed, inverse):
-            coef = [jnp.take_along_axis(pack[g], index, axis=1) for g in range(at, 8)]
-            pivot = inv[at][sub : sub + 1] / coef[0][sub : sub + 1]
-            pivot = jnp.broadcast_to(pivot, (8, 128))
-            row = rows_of((8, 128))
-            inv[at] = jnp.where(
-                row == sub, pivot, jnp.where(row > sub, inv[at] - coef[0] * pivot, inv[at])
-            )
-            for g in range(at + 1, 8):
-                inv[g] = inv[g] - coef[g - at] * pivot
-    return [jnp.concatenate(inv, axis=0) for inv in inverse]
+            top = jnp.broadcast_to(inv[at][sub : sub + 1], (8, 128))
+            for g in range(at, 4):
+                coef = jnp.take_along_axis(pack[g], index, axis=1)
+                if g == at:
+                    coef = jnp.where(row > sub, coef, 0.0)
+                inv[g] = inv[g] - coef * top
+    wide = lanes((32, 128)) // 32
+    zero = jnp.zeros((32, 128), F32)
+    results = []
+    for tile, inv, scale in zip(tiles, inverse, scales):
+        value = jnp.concatenate(inv, axis=0) * scale
+        parts = [jnp.where(wide == g, value, 0.0) for g in range(4)]
+        cross = [jnp.where(wide == g - 1, tile[32 * g : 32 * g + 32], 0.0) for g in (1, 3)]
+        left = dot3(halves(jnp.concatenate(cross, axis=0)), halves(jnp.concatenate(parts, axis=0)))
+        left = jnp.concatenate([zero, left[:32], zero, left[32:]], axis=0)
+        odd = jnp.concatenate([parts[1], parts[3]], axis=0)
+        odd = odd - dot3(halves(odd), halves(left))
+        first = jnp.concatenate([parts[0], odd[:32]], axis=0)
+        second = jnp.concatenate([parts[2], odd[32:]], axis=0)
+        half = jnp.concatenate([first, second], axis=0)
+        cross = jnp.where(lanes((64, 128)) < 64, tile[64:], 0.0)
+        left = dot3(halves(cross), halves(half))
+        left = jnp.concatenate([jnp.zeros_like(left), left], axis=0)
+        results.append(jnp.concatenate([first, second - dot3(halves(second), halves(left))], axis=0))
+    return results
 
 
 def dot2(a, b, dims=((1,), (0,))):
@@ -102,25 +123,17 @@
     size = rhs_ref.shape[1]
     tiles = size // 128
 
-    @pl.loop(0, arcs * tiles // 4)
+    @pl.loop(0, arcs * tiles // GROUP)
     def _(step):
         found = []
-        for part in range(4):
-            at = step * 4 + part
+        for part in range(GROUP):
+            at = step * GROUP + part
             arc, tile = at // tiles, lax.rem(at, tiles)
             spot = pl.ds(pl.multiple_of(tile * 128, 128), 128)
             found.append((arc, spot, tile))
-        values = [diagonal_of(factor_ref, arc, tile) for arc, spot, tile in found]
-        low = lanes((64, 128)) < 64
-        for (arc, spot, _), value, done in zip(found, values, invert_tiles(values)):
-            first = jnp.where(low, done, 0.0)
-            second = jnp.where(low, 0.0, done)
-            whole = jnp.concatenate([first, second], axis=0)
-            cross = jnp.where(low, value[64:], 0.0)
-            left = dot3(halves(cross), halves(whole))
-            left = jnp.concatenate([jnp.zeros_like(left), left], axis=0)
-            corner = dot3(halves(second), halves(left))
-            inv[arc, spot, :] = jnp.concatenate([first, second - corner], axis=0)
+        done = invert_tiles([diagonal_of(factor_ref, arc, tile) for arc, spot, tile in found])
+        for (arc, spot, _), value in zip(found, done):
+            inv[arc, spot, :] = value
 
     blocks = size // OBS_STEP
     for arc in range(arcs):
@@ -348,39 +361,6 @@
         ),
         compiler_params=pltpu.CompilerParams(vmem_limit_bytes=KERNEL_VMEM),
     )(at, on, design)
-
-
-def gram_kernel(on_ref, design_ref, qh_ref, ql_ref, out_ref):
-    arcs = design_ref.shape[0]
-    out_ref[...] = jnp.zeros_like(out_ref)
-    for arc in range(arcs):
-
-        @pl.when(on_ref[pl.program_id(0) * arcs + arc] > 0)
-        def _():
-            flip = ((0,), (0,))
-            out_ref[...] += dot_by(design_ref[arc], qh_ref[arc], flip) + dot_by(
-                design_ref[arc], ql_ref[arc], flip
-            )
-
-
-def gram_of(on, design, high, less):
-    arcs, observed, columns = design.shape
-    width = high.shape[2]
-    return pl.pallas_call(
-        gram_kernel,
-        out_shape=jax.ShapeDtypeStruct((columns, width), F32),
-        grid_spec=pltpu.PrefetchScalarGridSpec(
-            num_scalar_prefetch=1,
-            grid=(columns // BLK,),
-            in_specs=[
-                pl.BlockSpec((arcs, observed, BLK), lambda i, on: (0, 0, i)),
-                whole(high.shape),
-                whole(less.shape),
-            ],
-            out_specs=pl.BlockSpec((BLK, width), lambda i, on: (i, 0)),
-        ),
-        compiler_params=pltpu.CompilerParams(vmem_limit_bytes=KERNEL_VMEM),
-    )(on, design, high, less)
 
 
 MESH = pl.DeviceIdType.MESH
@@ -589,7 +569,7 @@
 
 
 def total_kernel(
-    part_ref, gram_ref, out_ref, sum_ref, own_ref, kept, mate, got, pair,
+    on_ref, part_ref, design_ref, high_ref, less_ref, out_ref, sum_ref, own_ref, gram, kept, mate, got, pair,
     ps, pr, qs, qr, rs, rr, gs, gr, fs, fr,
 ):
     chip, core = lax.axis_index("line"), lax.axis_index("core")
@@ -600,10 +580,31 @@
     half = part_ref.shape[0] // 2
     quarter = half // 4
     rows = lambda base, n: pl.ds(pl.multiple_of(base, 32), n)
+    arcs, _, columns = design_ref.shape
+    width = high_ref.shape[2]
+    share = gram.shape[2]
     swap = remote(part_ref.at[rows((1 - core) * half, half)], mate, ps, pr, other)
     swap.start()
-    trade = remote(gram_ref.at[:, 1 - core], pair, qs, qr, other)
-    trade.start()
+
+    def product(block):
+        flip = ((0,), (0,))
+        total = jnp.zeros((BLK, width), F32)
+        for arc in range(arcs):
+            piece = design_ref[arc, :, block * BLK : block * BLK + BLK]
+            on = on_ref[block * arcs + arc].astype(F32)
+            one = dot_by(piece, high_ref[arc], flip) + dot_by(piece, less_ref[arc], flip)
+            total = total + one * on
+        low = block * BLK
+        while low < block * BLK + BLK:
+            at = low // share
+            stop = min((at + 1) * share, block * BLK + BLK)
+            gram[at // 2, at % 2, low - at * share : stop - at * share, :] = total[
+                low - block * BLK : stop - block * BLK
+            ]
+            low = stop
+
+    blocks = columns // BLK
+    product(0)
     swap.wait_recv()
     kept[...] = part_ref[rows(core * half, half), :] + mate[...]
     scatter = [
@@ -612,10 +613,10 @@
     ]
     for copy in scatter:
         copy.start()
-    trade.wait_recv()
-    for c in range(4):
-        sum_ref[c] = (gram_ref[c, core] + pair[c]).astype(BF)
-    own_ref[...] = gram_ref[chip, core] + pair[chip]
+    for block in range(1, blocks):
+        product(block)
+    trade = remote(gram.at[:, 1 - core], pair, qs, qr, other)
+    trade.start()
     for copy in scatter:
         copy.wait_recv()
     mine = rows(core * half + chip * quarter, quarter)
@@ -627,6 +628,10 @@
     forward = [remote(out_ref.at[mine], out_ref.at[mine], fs.at[0], fr.at[0], other)]
     for copy in gather + forward:
         copy.start()
+    trade.wait_recv()
+    for c in range(4):
+        sum_ref[c] = (gram[c, core] + pair[c]).astype(BF)
+    own_ref[...] = gram[chip, core] + pair[chip]
     for k in range(3):
         gather[k].wait_recv()
         came = rows(core * half + lax.rem(chip + 3 - k, 4) * quarter, quarter)
@@ -639,9 +644,11 @@
         copy.wait_send()
 
 
-def total_over_arc(part, gram):
+def total_over_arc(on, part, design, high, less):
     lines, width = part.shape
-    chips, _, share, size = gram.shape
+    size = high.shape[2]
+    chips = 4
+    share = design.shape[2] // (2 * chips)
     vm, dma = pltpu.VMEM, pltpu.SemaphoreType.DMA
     return pl.pallas_call(
         total_kernel,
@@ -650,9 +657,10 @@
             jax.ShapeDtypeStruct((chips, share, size), BF),
             jax.ShapeDtypeStruct((share, size), F32),
         ),
-        in_specs=[pl.BlockSpec(memory_space=vm)] * 2,
+        in_specs=[pl.BlockSpec(memory_space=pltpu.SMEM)] + [pl.BlockSpec(memory_space=vm)] * 4,
         out_specs=(pl.BlockSpec(memory_space=vm),) * 3,
         scratch_shapes=[
+            vm((chips, 2, share, size), F32),
             vm((lines // 2, width), F32),
             vm((lines // 2, width), F32),
             vm((3, lines // 8, width), F32),
@@ -662,7 +670,7 @@
         compiler_params=pltpu.CompilerParams(
             vmem_limit_bytes=KERNEL_VMEM, collective_id=1, has_side_effects=True
         ),
-    )(part, gram)
+    )(on, part, design, high, less)
 
 
 PANEL = 512
@@ -690,9 +698,9 @@
     )
     factor, raw = spread(cov_factor, window)
     block, high, less = solve_twice(factor, raw)
-    gram = gram_of(hits.T.astype(jnp.int32).reshape(-1), design, high, less)
     share = columns // (4 * 2)
-    block, sums, own = total_over_arc(block, gram.reshape(4, 2, share, PANEL))
+    on = hits.T.astype(jnp.int32).reshape(-1)
+    block, sums, own = total_over_arc(on, block, design, high, less)
     arrived = lax.all_to_all(sums, "line", split_axis=0, concat_axis=0, tiled=True)
     reg = reg_diag.reshape(-1, 1, PANEL)
     shift = par_id * columns + (chip * 2 + core) * share - start

time: 162 us -> 153 us (0.944)
  Pallas kernels: 150 us -> 142 us
    pallas_call x1 -> x0, Pallas kernels: 8.78 us -> none  [gram_of(): pl.pallas_call(gram_kernel, out_shape=jax.ShapeDtypeStruct((columns, widt...]
    pallas_call x1, Pallas kernels: 26.2 us -> 28.8 us  [total_over_arc(): pl.pallas_call(total_kernel, out_shape=(jax.ShapeDtypeStruct(part.shape,...]
    pallas_call x1, Pallas kernels: 23.9 us -> 21.5 us  [solve_twice(): pl.pallas_call(functools.partial(solve_kernel, arcs), out_shape=(jax.Shap...]
where the time goes in v4:
time: 153 us
  Pallas kernels  142 us (93%)
  starting transfers between devices  5.04 us (3%)
  other arithmetic  3.04 us (2%)
  local copies, waits for them, and re-layouts  2.22 us (1%)
    pallas_call x1, Pallas kernels, spread(): pl.pallas_call(spread_kernel, out_shape=(jax.ShapeDtypeStruct((arcs, 16,...  65.6 us
    pallas_call x1, Pallas kernels, total_over_arc(): pl.pallas_call(total_kernel, out_shape=(jax.ShapeDtypeStruct(part.shape,...  28.8 us
    pallas_call x1, Pallas kernels, solve_twice(): pl.pallas_call(functools.partial(solve_kernel, arcs), out_shape=(jax.Shap...  21.5 us
    pallas_call x1, Pallas kernels, factor_inverse(): pl.pallas_call(factor_kernel, out_shape=jax.ShapeDtypeStruct((size, size)...  18.8 us
    all_to_all x1, starting transfers between devices, on_device(): lax.all_to_all(sums, 'line', split_axis=0, concat_axis=0, tiled=True)  5.04 us
    pallas_call x1, Pallas kernels, apply_inverse(): pl.pallas_call(apply_kernel, out_shape=jax.ShapeDtypeStruct((share, size)...  3.65 us
    pallas_call x1, Pallas kernels, window_of(): pl.pallas_call(window_kernel, out_shape=jax.ShapeDtypeStruct((arcs, obser...  3.37 us
  transfers between devices with their start and end apart: 1, of which 0 were waited for; matrix products, arithmetic and copies ran while one was open for 0% of the time, Pallas kernels for 12%

profile of v4, /device:TPU:1, one launch (start us, length us, event | category | flops | bytes accessed | tf_op | source)
XLA Modules:
  0.0 152.8 jit_solution(348639329643491287)
XLA Ops:
  0.7 0.5 iota_add_fusion
  1.2 0.9 compare_reduce_fusion
  2.1 0.9 compare_reduce_fusion.1
  3.0 0.1 and_convert_fusion
  3.1 0.7 reshape.41.on_ref
  3.7 0.1 copy.6
  3.8 0.6 reshape.40.on_ref
  4.4 3.4 %shard_map.55.win_ref = bf16[2,1024,512]{2,1,0:T(8,128)(2,1)} custom-call(s32[2]{0:T(128)} %get-tuple-element.22.at_ref, s32[4]{0:T(128)} %reshape.41.on_ref, bf16[2,1024,1280]{2,1,0:T(8,128)(2,1)} %design_ref.3), custom_call_target="tpu_custom_call" | custom-call | tf_op jit(solution)/shard_map/pallas_call | solution.py:353
  7.8 65.6 %shard_map.56 = (bf16[2,16,11,32,128]{4,3,2,1,0:T(8,128)(2,1)}, bf16[2,1024,512]{2,1,0:T(8,128)(2,1)}) custom-call(f32[2,32,1024]{2,1,0:T(8,128)} %cov_ref.1, bf16[2,1024,512]{2,1,0:T(8,128)(2,1)} %shard_map.55.win_ref), custom_call_target="tpu_custom_call" | custom-call | tf_op jit(solution)/shard_map/pallas_call | solution.py:545
  73.4 21.5 %shard_map.57 = (f32[1280,128]{1,0:T(8,128)}, bf16[2,1024,512]{2,1,0:T(8,128)(2,1)}, bf16[2,1024,512]{2,1,0:T(8,128)(2,1)}) custom-call(bf16[2,16,11,32,128]{4,3,2,1,0:T(8,128)(2,1)} %get-tuple-element.13.factor_ref, bf16[2,1024,512]{2,1,0:T(8,128)(2,1)} %get-tuple-element.14.rhs_ref), custom_call_target="tpu_custom_call" | custom-call | tf_op jit(solution)/shard_map/pallas_call | solution.py:193
  95.0 28.8 %shard_map.58 = (f32[1280,128]{1,0:T(8,128)}, bf16[4,160,512]{2,1,0:T(8,128)(2,1)}, f32[160,512]{1,0:T(8,128)}) custom-call(s32[10]{0:T(128)} %reshape.40.on_ref, f32[1280,128]{1,0:T(8,128)} %get-tuple-element.15.part_ref, bf16[2,1024,1280]{2,1,0:T(8,128)(2,1)} %design_ref.3, bf16[2,1024,512]{2,1,0:T(8,128)(2,1)} %get-tuple-element.16.high_ref, ...), custom_call_target="tpu_custom_call" | custom-call | tf_op jit(solution)/shard_map/pallas_call | solution.py:653
  123.8 5.0 %all-to-all-start = ((bf16[4,160,512]{2,1,0:T(8,128)(2,1)}), bf16[4,160,512]{2,1,0:T(8,128)(2,1)S(1)}, u32[]{:S(2)}, u32[]{:S(2)}) async-start(bf16[4,160,512]{2,1,0:T(8,128)(2,1)} %get-tuple-element.18), calls=%async_computation | async-start | bytes 1310720 | tf_op jit(solution)/shard_map/all_to_all | solution.py:704
  128.8 0.7 pad_add_fusion.at_ref
  129.5 18.8 %shard_map.59.inverse_ref = f32[512,512]{1,0:T(8,128)} custom-call(s32[3]{0:T(128)} %pad_add_fusion.at_ref, f32[1280,128]{1,0:T(8,128)} %get-tuple-element.20.block_ref, f32[80,1,512]{2,1,0:T(1,128)} %bitcast.8), custom_call_target="tpu_custom_call" | custom-call | flops 30000001024 | bytes 60000000 | tf_op jit(solution)/shard_map/pallas_call | solution.py:298
  148.2 0.0 all-to-all-done.arrived_ref
  148.2 0.0 copy-start
  148.2 0.9 copy-done
  149.1 3.6 %shard_map.60 = f32[160,512]{1,0:T(8,128)} custom-call(s32[3]{0:T(128)} %pad_add_fusion.at_ref, bf16[4,160,512]{2,1,0:T(8,128)(2,1)} %copy-done, f32[160,512]{1,0:T(8,128)} %get-tuple-element.19.own_ref, f32[512,512]{1,0:T(8,128)} %shard_map.59.inverse_ref, f32[80,1,512]{2,1,0:T(1,128)} %bitcast.9), custom_call_target="tpu_custom_call" | custom-call | tf_op jit(solution)/shard_map/pallas_call | solution.py:324
  (3 shorter events, 0.0 us)
Async XLA Ops:
  123.8 24.5 %all-to-all-start = ((bf16[4,160,512]{2,1,0:T(8,128)(2,1)}), bf16[4,160,512]{2,1,0:T(8,128)(2,1)S(1)}, u32[]{:S(2)}, u32[]{:S(2)}) async-start(bf16[4,160,512]{2,1,0:T(8,128)(2,1)} %get-tuple-element.18), calls=%async_computation | async-start | bytes 1310720 | tf_op jit(solution)/shard_map/all_to_all | solution.py:704
  148.2 0.9 copy-start

commit v5 on v4

--- a/solution.py
+++ b/solution.py
@@ -119,92 +119,71 @@
     return jnp.concatenate(pieces, axis=0)
 
 
-def solve_kernel(arcs, factor_ref, rhs_ref, block_ref, qh_ref, ql_ref, inv, fh, wh, wl, yh, yl):
-    size = rhs_ref.shape[1]
-    tiles = size // 128
-
-    @pl.loop(0, arcs * tiles // GROUP)
-    def _(step):
-        found = []
-        for part in range(GROUP):
-            at = step * GROUP + part
-            arc, tile = at // tiles, lax.rem(at, tiles)
-            spot = pl.ds(pl.multiple_of(tile * 128, 128), 128)
-            found.append((arc, spot, tile))
-        done = invert_tiles([diagonal_of(factor_ref, arc, tile) for arc, spot, tile in found])
-        for (arc, spot, _), value in zip(found, done):
-            inv[arc, spot, :] = value
-
-    blocks = size // OBS_STEP
-    for arc in range(arcs):
-        for b in range(blocks):
-            r = b * OBS_STEP
-            one, two = inv[arc, r : r + 128, :], inv[arc, r + 128 : r + 256, :]
-            cross = tile_of(factor_ref, arc, 2 * b + 1, 2 * b)
-            corner = -dot3(halves(two), halves(dot2(cross, halves(one))))
-            zero = jnp.zeros((128, 128), BF)
-            for (ref, a, c, d) in zip((wh, wl), halves(one), halves(corner), halves(two)):
-                ref[arc, r : r + 128, 0:128] = a
-                ref[arc, r : r + 128, 128:256] = zero
-                ref[arc, r + 128 : r + 256, 0:128] = c
-                ref[arc, r + 128 : r + 256, 128:256] = d
-            for row in (2 * b, 2 * b + 1):
-                for column in range(2 * b):
-                    fh[arc, row * 128 : row * 128 + 128, column * 128 : column * 128 + 128] = tile_of(
-                        factor_ref, arc, row, column
-                    )
-
-    for b in range(blocks):
+def invert_all(step, factor_ref, inv):
+    tiles = inv.shape[1] // 128
+    found = []
+    for part in range(GROUP):
+        at = step * GROUP + part
+        arc, tile = at // tiles, lax.rem(at, tiles)
+        spot = pl.ds(pl.multiple_of(tile * 128, 128), 128)
+        found.append((arc, spot, tile))
+    done = invert_tiles([diagonal_of(factor_ref, arc, tile) for arc, spot, tile in found])
+    for (arc, spot, _), value in zip(found, done):
+        inv[arc, spot, :] = value
+
+
+def join_tiles(arc, factor_ref, inv, fh, wh, wl):
+    for b in range(inv.shape[1] // OBS_STEP):
         r = b * OBS_STEP
-        here = slice(r, r + OBS_STEP)
-        for arc in range(arcs):
-            value = rhs_ref[arc, here, :].astype(F32)
-            if b:
-                value = value - dot2(fh[arc, here, 0:r], (yh[arc, 0:r, :], yl[arc, 0:r, :]))
-            value = dot3((wh[arc, here, :], wl[arc, here, :]), halves(value))
-            high, less = halves(value)
-            yh[arc, here, :] = high
-            yl[arc, here, :] = less
+        one, two = inv[arc, r : r + 128, :], inv[arc, r + 128 : r + 256, :]
+        cross = tile_of(factor_ref, arc, 2 * b + 1, 2 * b)
+        corner = -dot3(halves(two), halves(dot2(cross, halves(one))))
+        zero = jnp.zeros((128, 128), BF)
+        for ref, a, c, d in zip((wh, wl), halves(one), halves(corner), halves(two)):
+            ref[arc, r : r + 128, 0:128] = a
+            ref[arc, r : r + 128, 128:256] = zero
+            ref[arc, r + 128 : r + 256, 0:128] = c
+            ref[arc, r + 128 : r + 256, 128:256] = d
+        for row in (2 * b, 2 * b + 1):
+            for column in range(2 * b):
+                fh[arc, row * 128 : row * 128 + 128, column * 128 : column * 128 + 128] = tile_of(
+                    factor_ref, arc, row, column
+                )
+
+
+def solve_forward(b, rhs_ref, fh, wh, wl, yh, yl):
+    r = b * OBS_STEP
+    here = slice(r, r + OBS_STEP)
+    for arc in range(rhs_ref.shape[0]):
+        value = rhs_ref[arc, here, :].astype(F32)
+        if b:
+            value = value - dot2(fh[arc, here, 0:r], (yh[arc, 0:r, :], yl[arc, 0:r, :]))
+        value = dot3((wh[arc, here, :], wl[arc, here, :]), halves(value))
+        yh[arc, here, :], yl[arc, here, :] = halves(value)
+
+
+def solve_back(b, fh, wh, wl, yh, yl, qh, ql):
     flip = ((0,), (0,))
-    for b in reversed(range(blocks)):
-        r = b * OBS_STEP
-        here, after = slice(r, r + OBS_STEP), slice(r + OBS_STEP, size)
-        for arc in range(arcs):
-            value = yh[arc, here, :].astype(F32) + yl[arc, here, :].astype(F32)
-            if b + 1 < blocks:
-                value = value - dot2(
-                    fh[arc, after, here], (qh_ref[arc, after, :], ql_ref[arc, after, :]), flip
-                )
-            value = dot3((wh[arc, here, :], wl[arc, here, :]), halves(value), flip)
-            qh_ref[arc, here, :], ql_ref[arc, here, :] = halves(value)
+    size = yh.shape[1]
+    r = b * OBS_STEP
+    here, after = slice(r, r + OBS_STEP), slice(r + OBS_STEP, size)
+    for arc in range(yh.shape[0]):
+        value = yh[arc, here, :].astype(F32) + yl[arc, here, :].astype(F32)
+        if r + OBS_STEP < size:
+            value = value - dot2(fh[arc, after, here], (qh[arc, after, :], ql[arc, after, :]), flip)
+        value = dot3((wh[arc, here, :], wl[arc, here, :]), halves(value), flip)
+        qh[arc, here, :], ql[arc, here, :] = halves(value)
+
+
+def block_tiles(yh, block_ref):
     at = 0
-    for i in range(0, rhs_ref.shape[2], 128):
-        strip = sum(dot_by(yh[arc, :, i : i + 128], yh[arc, :, i:], flip) for arc in range(arcs))
+    for i in range(0, yh.shape[2], 128):
+        strip = sum(
+            dot_by(yh[arc, :, i : i + 128], yh[arc, :, i:], ((0,), (0,))) for arc in range(yh.shape[0])
+        )
         for j in range(0, strip.shape[1], 128):
             block_ref[at : at + 128, :] = strip[:, j : j + 128]
             at += 128
-
-
-def solve_twice(factor, rhs):
-    arcs, size, width = rhs.shape
-    vm = pltpu.VMEM
-    out = jax.ShapeDtypeStruct(rhs.shape, BF)
-    tiles = len(tile_list(width))
-    return pl.pallas_call(
-        functools.partial(solve_kernel, arcs),
-        out_shape=(jax.ShapeDtypeStruct((tiles * 128, 128), F32), out, out),
-        in_specs=[pl.BlockSpec(memory_space=vm)] * 2,
-        out_specs=(pl.BlockSpec(memory_space=vm),) * 3,
-        scratch_shapes=[
-            vm((arcs, size, 128), F32),
-            vm((arcs, size, size), BF),
-            vm((arcs, size, OBS_STEP), BF),
-            vm((arcs, size, OBS_STEP), BF),
-            vm((arcs, size, width), BF),
-            vm((arcs, size, width), BF),
-        ],
-        compiler_params=pltpu.CompilerParams(vmem_limit_bytes=KERNEL_VMEM),
-    )(factor, rhs)
 
 
 def split_rows(u):
@@ -396,11 +375,20 @@
     ]
 
 
-def spread_kernel(
-    cov_ref, win_ref, fac_ref, rhs_ref, slabs, got1, got2, gotz, sum1, sum2,
+def main_kernel(
+    on_ref, cov_ref, win_ref, design_hbm, out_ref, sum_ref, own_ref,
+    fac_ref, rhs_ref, slabs, got1, got2, gotz, sum1, sum2, inv, fh, wh, wl, yh, yl, qh, ql, design_ref,
+    part_ref, gram, kept, mate, got, pair,
     ls, lr, m1s, m1r, m2s, m2r, mzs, mzr, gls, glr, gms, gmr,
+    ds, ps, pr, qs, qr, rs, rr, gs, gr, fs, fr,
 ):
     z, x, y = (lax.axis_index(name) for name in ("par_0", "par_1", "par_2"))
+    chip, core = lax.axis_index("line"), lax.axis_index("core")
+    other = {"core": 1 - core}
+    chips = [lax.rem(chip + k, 4) for k in (1, 2, 3)]
+    peers = [{"line": c} for c in chips]
+    load = pltpu.make_async_copy(design_hbm, design_ref, ds)
+    load.start()
     arcs = cov_ref.shape[0]
     turned = lambda v: v + z * (3 - 2 * v)
     outer = [(x, "par_1"), (y, "par_2")]
@@ -409,7 +397,7 @@
     ring = [{"par_1": lax.rem(x + k, 4)} for k in (1, 2, 3)] + [
         {"par_2": lax.rem(y + k, 4)} for k in (1, 2, 3)
     ]
-    meet(ring + [{"par_0": 1 - z}, partner])
+    meet(ring + [{"par_0": 1 - z}, partner] + peers + [other])
 
     small = turned(x) + 1
     held = small + z * (9 - 2 * small)
@@ -528,60 +516,24 @@
     g3 = begin(near(m_group, outer, 1, gms, gmr))
     arrive(l3)
     l4 = begin(far(lambda a: l_group(a, 0, 2), lambda a: l_group(a, 2, 2), outer, 1, gls, glr))
+    arrive(l4)
+    invert_all(0, fac_ref, inv)
     arrive(g3)
     g4 = begin(far(lambda a: m_group(a, 0, 128), lambda a: m_group(a, 128, 128), outer, 1, gms, gmr))
-    arrive(l4)
+    invert_all(1, fac_ref, inv)
+    for arc in two:
+        join_tiles(arc, fac_ref, inv, fh, wh, wl)
     arrive(g4)
-    pl.loop(0, held)(lambda c: piece(c).wait_send())
-    piece(8).wait_send()
-    for copy in sent + scatter2 + across + l1 + l2 + l3 + l4 + g1 + g2 + g3 + g4:
-        copy.wait_send()
-
-
-def spread(cov, window):
-    arcs, lines, size = cov.shape
-    _, observed, width = window.shape
-    vm, dma = pltpu.VMEM, pltpu.SemaphoreType.DMA
-    return pl.pallas_call(
-        spread_kernel,
-        out_shape=(
-            jax.ShapeDtypeStruct((arcs, 16, 11, lines, 128), BF),
-            jax.ShapeDtypeStruct(window.shape, BF),
-        ),
-        in_specs=[pl.BlockSpec(memory_space=vm)] * 2,
-        out_specs=(pl.BlockSpec(memory_space=vm),) * 2,
-        scratch_shapes=[
-            vm((2, 9, arcs, lines, 128), BF),
-            vm((arcs, 3, 256, width), BF),
-            vm((arcs, 3, 64, width), BF),
-            vm((arcs, 64, width), BF),
-            vm((arcs, 256, width), BF),
-            vm((arcs, 64, width), BF),
-            dma((9,)), dma((9,)),
-            dma((arcs, 3)), dma((arcs, 3)), dma((arcs, 3)), dma((arcs, 3)),
-            dma((arcs,)), dma((arcs,)),
-            dma((arcs, 2, 4)), dma((arcs, 2, 4)), dma((arcs, 2, 4)), dma((arcs, 2, 4)),
-        ],
-        compiler_params=pltpu.CompilerParams(
-            vmem_limit_bytes=KERNEL_VMEM, collective_id=0, has_side_effects=True
-        ),
-    )(cov, window)
-
-
-def total_kernel(
-    on_ref, part_ref, design_ref, high_ref, less_ref, out_ref, sum_ref, own_ref, gram, kept, mate, got, pair,
-    ps, pr, qs, qr, rs, rr, gs, gr, fs, fr,
-):
-    chip, core = lax.axis_index("line"), lax.axis_index("core")
-    other = {"core": 1 - core}
-    chips = [lax.rem(chip + k, 4) for k in (1, 2, 3)]
-    peers = [{"line": c} for c in chips]
-    meet(peers + [other])
+    blocks = rhs_ref.shape[1] // OBS_STEP
+    for b in range(blocks):
+        solve_forward(b, rhs_ref, fh, wh, wl, yh, yl)
+    block_tiles(yh, part_ref)
+
     half = part_ref.shape[0] // 2
     quarter = half // 4
     rows = lambda base, n: pl.ds(pl.multiple_of(base, 32), n)
-    arcs, _, columns = design_ref.shape
-    width = high_ref.shape[2]
+    columns = design_ref.shape[2]
+    width = qh.shape[2]
     share = gram.shape[2]
     swap = remote(part_ref.at[rows((1 - core) * half, half)], mate, ps, pr, other)
     swap.start()
@@ -592,7 +544,7 @@
         for arc in range(arcs):
             piece = design_ref[arc, :, block * BLK : block * BLK + BLK]
             on = on_ref[block * arcs + arc].astype(F32)
-            one = dot_by(piece, high_ref[arc], flip) + dot_by(piece, less_ref[arc], flip)
+            one = dot_by(piece, qh[arc], flip) + dot_by(piece, ql[arc], flip)
             total = total + one * on
         low = block * BLK
         while low < block * BLK + BLK:
@@ -603,74 +555,102 @@
             ]
             low = stop
 
-    blocks = columns // BLK
+    for b in reversed(range(1, blocks)):
+        solve_back(b, fh, wh, wl, yh, yl, qh, ql)
+        if b == blocks - 1:
+            swap.wait_recv()
+            kept[...] = part_ref[rows(core * half, half), :] + mate[...]
+            scatter = begin([
+                remote(kept.at[rows(c * quarter, quarter)], got.at[k], rs.at[k], rr.at[k], peer)
+                for k, (c, peer) in enumerate(zip(chips, peers))
+            ])
+    solve_back(0, fh, wh, wl, yh, yl, qh, ql)
+    load.wait()
     product(0)
-    swap.wait_recv()
-    kept[...] = part_ref[rows(core * half, half), :] + mate[...]
-    scatter = [
-        remote(kept.at[rows(c * quarter, quarter)], got.at[k], rs.at[k], rr.at[k], peer)
-        for k, (c, peer) in enumerate(zip(chips, peers))
-    ]
-    for copy in scatter:
-        copy.start()
-    for block in range(1, blocks):
+    product(1)
+    arrive(scatter)
+    mine = rows(core * half + chip * quarter, quarter)
+    out_ref[mine, :] = (kept[rows(chip * quarter, quarter), :] + got[0]) + (got[1] + got[2])
+    gather = begin([
+        remote(out_ref.at[mine], out_ref.at[mine], gs.at[k], gr.at[k], peer)
+        for k, peer in enumerate(peers)
+    ])
+    forward = begin([remote(out_ref.at[mine], out_ref.at[mine], fs.at[0], fr.at[0], other)])
+    for block in range(2, columns // BLK):
         product(block)
     trade = remote(gram.at[:, 1 - core], pair, qs, qr, other)
     trade.start()
-    for copy in scatter:
-        copy.wait_recv()
-    mine = rows(core * half + chip * quarter, quarter)
-    out_ref[mine, :] = (kept[rows(chip * quarter, quarter), :] + got[0]) + (got[1] + got[2])
-    gather = [
-        remote(out_ref.at[mine], out_ref.at[mine], gs.at[k], gr.at[k], peer)
-        for k, peer in enumerate(peers)
-    ]
-    forward = [remote(out_ref.at[mine], out_ref.at[mine], fs.at[0], fr.at[0], other)]
-    for copy in gather + forward:
-        copy.start()
+    for k in range(3):
+        gather[k].wait_recv()
+        from_chip = rows(core * half + lax.rem(chip + 3 - k, 4) * quarter, quarter)
+        forward += begin([
+            remote(out_ref.at[from_chip], out_ref.at[from_chip], fs.at[k + 1], fr.at[k + 1], other)
+        ])
     trade.wait_recv()
     for c in range(4):
         sum_ref[c] = (gram[c, core] + pair[c]).astype(BF)
     own_ref[...] = gram[chip, core] + pair[chip]
-    for k in range(3):
-        gather[k].wait_recv()
-        came = rows(core * half + lax.rem(chip + 3 - k, 4) * quarter, quarter)
-        copy = remote(out_ref.at[came], out_ref.at[came], fs.at[k + 1], fr.at[k + 1], other)
-        copy.start()
-        forward.append(copy)
-    for copy in forward:
-        copy.wait_recv()
+    arrive(forward)
+    pl.loop(0, held)(lambda c: piece(c).wait_send())
+    piece(8).wait_send()
+    for copy in sent + scatter2 + across + l1 + l2 + l3 + l4 + g1 + g2 + g3 + g4:
+        copy.wait_send()
     for copy in [swap, trade] + scatter + gather + forward:
         copy.wait_send()
 
 
-def total_over_arc(on, part, design, high, less):
-    lines, width = part.shape
-    size = high.shape[2]
+def block_and_gram(on, cov, window, design):
+    arcs, lines, size = cov.shape
+    _, observed, width = window.shape
     chips = 4
     share = design.shape[2] // (2 * chips)
+    total = len(tile_list(width)) * 128
     vm, dma = pltpu.VMEM, pltpu.SemaphoreType.DMA
     return pl.pallas_call(
-        total_kernel,
+        main_kernel,
         out_shape=(
-            jax.ShapeDtypeStruct(part.shape, F32),
-            jax.ShapeDtypeStruct((chips, share, size), BF),
-            jax.ShapeDtypeStruct((share, size), F32),
+            jax.ShapeDtypeStruct((total, 128), F32),
+            jax.ShapeDtypeStruct((chips, share, width), BF),
+            jax.ShapeDtypeStruct((share, width), F32),
         ),
-        in_specs=[pl.BlockSpec(memory_space=pltpu.SMEM)] + [pl.BlockSpec(memory_space=vm)] * 4,
+        in_specs=[pl.BlockSpec(memory_space=pltpu.SMEM)]
+        + [pl.BlockSpec(memory_space=vm)] * 2
+        + [pl.BlockSpec(memory_space=pl.ANY)],
         out_specs=(pl.BlockSpec(memory_space=vm),) * 3,
         scratch_shapes=[
-            vm((chips, 2, share, size), F32),
-            vm((lines // 2, width), F32),
-            vm((lines // 2, width), F32),
-            vm((3, lines // 8, width), F32),
-            vm((chips, share, size), F32),
-            dma, dma, dma, dma, dma((3,)), dma((3,)), dma((3,)), dma((3,)), dma((4,)), dma((4,)),
+            vm((arcs, 16, 11, lines, 128), BF),
+            vm((arcs, size, width), BF),
+            vm((2, 9, arcs, lines, 128), BF),
+            vm((arcs, 3, 256, width), BF),
+            vm((arcs, 3, 64, width), BF),
+            vm((arcs, 64, width), BF),
+            vm((arcs, 256, width), BF),
+            vm((arcs, 64, width), BF),
+            vm((arcs, size, 128), F32),
+            vm((arcs, size, size), BF),
+            vm((arcs, size, OBS_STEP), BF),
+            vm((arcs, size, OBS_STEP), BF),
+            vm((arcs, size, width), BF),
+            vm((arcs, size, width), BF),
+            vm((arcs, size, width), BF),
+            vm((arcs, size, width), BF),
+            vm(design.shape, BF),
+            vm((total, 128), F32),
+            vm((chips, 2, share, width), F32),
+            vm((total // 2, 128), F32),
+            vm((total // 2, 128), F32),
+            vm((3, total // 8, 128), F32),
+            vm((chips, share, width), F32),
+            dma((9,)), dma((9,)),
+            dma((arcs, 3)), dma((arcs, 3)), dma((arcs, 3)), dma((arcs, 3)),
+            dma((arcs,)), dma((arcs,)),
+            dma((arcs, 2, 4)), dma((arcs, 2, 4)), dma((arcs, 2, 4)), dma((arcs, 2, 4)),
+            dma, dma, dma, dma, dma, dma((3,)), dma((3,)), dma((3,)), dma((3,)), dma((4,)), dma((4,)),
         ],
         compiler_params=pltpu.CompilerParams(
-            vmem_limit_bytes=KERNEL_VMEM, collective_id=1, has_side_effects=True
+            vmem_limit_bytes=KERNEL_VMEM, collective_id=0, has_side_effects=True
         ),
-    )(on, part, design, high, less)
+    )(on, cov, window, design)
 
 
 PANEL = 512
@@ -696,11 +676,9 @@
         (inside[:, None] & active).astype(jnp.int32).reshape(-1),
         design,
     )
-    factor, raw = spread(cov_factor, window)
-    block, high, less = solve_twice(factor, raw)
     share = columns // (4 * 2)
     on = hits.T.astype(jnp.int32).reshape(-1)
-    block, sums, own = total_over_arc(on, block, design, high, less)
+    block, sums, own = block_and_gram(on, cov_factor, window, design)
     arrived = lax.all_to_all(sums, "line", split_axis=0, concat_axis=0, tiled=True)
     reg = reg_diag.reshape(-1, 1, PANEL)
     shift = par_id * columns + (chip * 2 + core) * share - start

time: 153 us -> 134 us (0.88)
  Pallas kernels: 142 us -> 122 us
  starting transfers between devices: 5.04 us -> 6.68 us
    pallas_call x3 -> x1, Pallas kernels: 116 us -> 95.8 us  [block_and_gram(): pl.pallas_call(main_kernel, out_shape=(jax.ShapeDtypeStruct((total, 128),...]
    all_to_all x1, starting transfers between devices: 5.04 us -> 6.68 us  [on_device(): lax.all_to_all(sums, 'line', split_axis=0, concat_axis=0, tiled=True)]
  transfers between devices with their start and end apart: 1 -> 1, of which waited for: 0 -> 0; matrix products, arithmetic and copies ran while one was open for 0% -> 0% of each run, Pallas kernels for 12% -> 14%
where the time goes in v5:
time: 134 us
  Pallas kernels  122 us (91%)
  starting transfers between devices  6.68 us (5%)
  other arithmetic  2.98 us (2%)
  local copies, waits for them, and re-layouts  2.17 us (2%)
    pallas_call x1, Pallas kernels, block_and_gram(): pl.pallas_call(main_kernel, out_shape=(jax.ShapeDtypeStruct((total, 128),...  95.8 us
    pallas_call x1, Pallas kernels, factor_inverse(): pl.pallas_call(factor_kernel, out_shape=jax.ShapeDtypeStruct((size, size)...  18.8 us
    all_to_all x1, starting transfers between devices, on_device(): lax.all_to_all(sums, 'line', split_axis=0, concat_axis=0, tiled=True)  6.68 us
    pallas_call x1, Pallas kernels, apply_inverse(): pl.pallas_call(apply_kernel, out_shape=jax.ShapeDtypeStruct((share, size)...  3.65 us
    pallas_call x1, Pallas kernels, window_of(): pl.pallas_call(window_kernel, out_shape=jax.ShapeDtypeStruct((arcs, obser...  3.38 us
  transfers between devices with their start and end apart: 1, of which 0 were waited for; matrix products, arithmetic and copies ran while one was open for 0% of the time, Pallas kernels for 14%

profile of v5, /device:TPU:1, one launch (start us, length us, event | category | flops | bytes accessed | tf_op | source)
XLA Modules:
  0.0 134.1 jit_solution(2642514937580093915)
XLA Ops:
  0.7 0.5 iota_add_fusion
  1.2 0.9 compare_reduce_fusion
  2.1 0.9 compare_reduce_fusion.1
  3.0 0.1 and_convert_fusion
  3.0 0.6 reshape.41.on_ref
  3.7 0.1 copy.6
  3.8 0.6 reshape.40.on_ref
  4.4 3.4 %shard_map.55.win_ref = bf16[2,1024,512]{2,1,0:T(8,128)(2,1)} custom-call(s32[2]{0:T(128)} %get-tuple-element.12.at_ref, s32[4]{0:T(128)} %reshape.41.on_ref, bf16[2,1024,1280]{2,1,0:T(8,128)(2,1)} %design_hbm.1), custom_call_target="tpu_custom_call" | custom-call | tf_op jit(solution)/shard_map/pallas_call | solution.py:332
  7.7 95.8 %shard_map.56 = (f32[1280,128]{1,0:T(8,128)}, bf16[4,160,512]{2,1,0:T(8,128)(2,1)}, f32[160,512]{1,0:T(8,128)}) custom-call(s32[10]{0:T(128)} %reshape.40.on_ref, f32[2,32,1024]{2,1,0:T(8,128)} %cov_ref.1, bf16[2,1024,512]{2,1,0:T(8,128)(2,1)} %shard_map.55.win_ref, bf16[2,1024,1280]{2,1,0:T(8,128)(2,1)} %design_hbm.1), custom_call_target="tpu_custom_call" | custom-call | tf_op jit(solution)/shard_map/pallas_call | solution.py:609
  103.5 6.7 %all-to-all-start = ((bf16[4,160,512]{2,1,0:T(8,128)(2,1)}), bf16[4,160,512]{2,1,0:T(8,128)(2,1)S(1)}, u32[]{:S(2)}, u32[]{:S(2)}) async-start(bf16[4,160,512]{2,1,0:T(8,128)(2,1)} %get-tuple-element.8), calls=%async_computation | async-start | bytes 1310720 | tf_op jit(solution)/shard_map/all_to_all | solution.py:682
  110.2 0.6 pad_add_fusion.at_ref
  110.8 18.8 %shard_map.57.inverse_ref = f32[512,512]{1,0:T(8,128)} custom-call(s32[3]{0:T(128)} %pad_add_fusion.at_ref, f32[1280,128]{1,0:T(8,128)} %get-tuple-element.10.block_ref, f32[80,1,512]{2,1,0:T(1,128)} %bitcast.8), custom_call_target="tpu_custom_call" | custom-call | flops 30000001024 | bytes 60000000 | tf_op jit(solution)/shard_map/pallas_call | solution.py:277
  129.6 0.0 all-to-all-done.arrived_ref
  129.6 0.0 copy-start
  129.6 0.9 copy-done
  130.4 3.7 %shard_map.58 = f32[160,512]{1,0:T(8,128)} custom-call(s32[3]{0:T(128)} %pad_add_fusion.at_ref, bf16[4,160,512]{2,1,0:T(8,128)(2,1)} %copy-done, f32[160,512]{1,0:T(8,128)} %get-tuple-element.9.own_ref, f32[512,512]{1,0:T(8,128)} %shard_map.57.inverse_ref, f32[80,1,512]{2,1,0:T(1,128)} %bitcast.9), custom_call_target="tpu_custom_call" | custom-call | tf_op jit(solution)/shard_map/pallas_call | solution.py:303
  (3 shorter events, 0.0 us)
Async XLA Ops:
  103.5 26.1 %all-to-all-start = ((bf16[4,160,512]{2,1,0:T(8,128)(2,1)}), bf16[4,160,512]{2,1,0:T(8,128)(2,1)S(1)}, u32[]{:S(2)}, u32[]{:S(2)}) async-start(bf16[4,160,512]{2,1,0:T(8,128)(2,1)} %get-tuple-element.8), calls=%async_computation | async-start | bytes 1310720 | tf_op jit(solution)/shard_map/all_to_all | solution.py:682
  129.6 0.9 copy-start

commit v6 on v5

--- a/solution.py
+++ b/solution.py
@@ -9,6 +9,9 @@
 
 OBS_STEP = 256
 GROUP = 8
+PARTS = 2
+PART = 512 // PARTS
+ORDER = "lablablablabablabl0ab1ab2"
 BF = jnp.bfloat16
 F32 = jnp.float32
 KERNEL_VMEM = 56 * 1024 * 1024
@@ -401,129 +404,174 @@
 
     small = turned(x) + 1
     held = small + z * (9 - 2 * small)
+    two = range(arcs)
+    sent = []
 
     def piece(c):
         return remote(slabs.at[z, c], slabs.at[z, c], ls.at[c], lr.at[c], partner)
 
     def came(c):
         return remote(slabs.at[1 - z, c], slabs.at[1 - z, c], ls.at[c], lr.at[c], partner)
-
-    last = cov_ref[:, :, pl.ds(pl.multiple_of((held - 1) * 128, 128), 128)]
-    slabs[z, 8] = (last - last.astype(BF).astype(F32)).astype(BF)
-    for c in range(8):
-        slabs[z, c] = cov_ref[:, :, c * 128 : c * 128 + 128].astype(BF)
-    pl.loop(0, held)(lambda c: piece(c).start())
-    piece(8).start()
-    scatter1 = [
-        remote(
-            win_ref.at[arc, pl.ds(pl.multiple_of(lax.rem(outer[arc][0] + k, 4) * 256, 256), 256)],
-            got1.at[arc, k - 1], m1s.at[arc, k - 1], m1r.at[arc, k - 1],
-            {outer[arc][1]: lax.rem(outer[arc][0] + k, 4)},
-        )
-        for k in (1, 3, 2) for arc in range(arcs)
-    ]
-    for copy in scatter1:
-        copy.start()
-    pl.loop(0, 9 - held)(lambda c: came(c).wait_recv())
-    came(8).wait_recv()
-    for arc in range(arcs):
-        place = 4 * turned(outer[arc][0]) + turned(inner[arc][0])
-
-        @pl.loop(0, small - 1)
-        def _(c):
-            fac_ref[arc, place, c] = slabs[0, c, arc]
-
-        @pl.loop(0, 8 - small)
-        def _(c):
-            fac_ref[arc, place, small - 1 + c] = slabs[1, c, arc]
-
-        fac_ref[arc, place, 7] = slabs[0, small - 1, arc]
-        fac_ref[arc, place, 8] = slabs[0, 8, arc]
-        fac_ref[arc, place, 9] = slabs[1, 8 - small, arc]
-        fac_ref[arc, place, 10] = slabs[1, 8, arc]
-
-    def l_unit(arc, cut=slice(0, 11)):
-        size = cut.stop - cut.start
-        return lambda r: fac_ref.at[
-            arc, 4 * turned(outer[arc][0]) + turned(r), pl.ds(cut.start, size)
-        ]
-
-    def l_group(arc, low=0, size=4):
-        return lambda r: fac_ref.at[arc, pl.ds(4 * turned(r) + low, size)]
-
-    def m_rows(arc, unit, base, low, size):
-        return lambda r: rhs_ref.at[arc, pl.ds(pl.multiple_of(base + r * unit + low, 32), size)]
-
-    def m_unit(arc, low=0, size=64):
-        return m_rows(arc, 64, outer[arc][0] * 256, low, size)
-
-    def m_group(arc, low=0, size=256):
-        return m_rows(arc, 256, 0, low, size)
 
     def begin(copies):
         for copy in copies:
             copy.start()
+        sent.extend(copies)
         return copies
 
     def arrive(copies):
         for copy in copies:
             copy.wait_recv()
-        return copies
-
-    two = range(arcs)
-    sent = list(scatter1)
-    near = lambda slot, ax, stage, s, r: [
-        copy for arc in two
-        for copy in ring_pair(slot(arc), *ax[arc], s.at[arc, stage], r.at[arc, stage])
-    ]
-    far = lambda first, second, ax, stage, s, r: [
-        copy for arc in two
-        for copy in ring_far(first(arc), second(arc), *ax[arc], s.at[arc, stage], r.at[arc, stage])
-    ]
-    l1 = begin(near(l_unit, inner, 0, gls, glr))
-    arrive(scatter1)
-    scatter2 = []
-    for arc in two:
-        own = win_ref[arc, pl.ds(pl.multiple_of(outer[arc][0] * 256, 256), 256), :]
-        sum1[arc] = (own + got1[arc, 0]) + (got1[arc, 1] + got1[arc, 2])
-        i, axis = inner[arc]
-        for k in (1, 3, 2):
-            to = lax.rem(i + k, 4)
-            scatter2 += begin([
+
+    def near(slot, ax, s, r):
+        return begin(
+            [copy for arc in two for copy in ring_pair(slot(arc), *ax[arc], s.at[arc], r.at[arc])]
+        )
+
+    def far(first, second, ax, s, r):
+        return begin(
+            [
+                copy for arc in two
+                for copy in ring_far(first(arc), second(arc), *ax[arc], s.at[arc], r.at[arc])
+            ]
+        )
+
+    def l_unit(low, size):
+        return lambda arc: lambda r: fac_ref.at[
+            arc, 4 * turned(outer[arc][0]) + turned(r), pl.ds(low, size)
+        ]
+
+    def l_group(low, size):
+        return lambda arc: lambda r: fac_ref.at[arc, pl.ds(4 * turned(r) + low, size)]
+
+    def factor_stream():
+        last = cov_ref[:, :, pl.ds(pl.multiple_of((held - 1) * 128, 128), 128)]
+        slabs[z, 8] = (last - last.astype(BF).astype(F32)).astype(BF)
+        for c in range(8):
+            slabs[z, c] = cov_ref[:, :, c * 128 : c * 128 + 128].astype(BF)
+        pl.loop(0, held)(lambda c: piece(c).start())
+        piece(8).start()
+        yield
+        pl.loop(0, 9 - held)(lambda c: came(c).wait_recv())
+        came(8).wait_recv()
+        for arc in two:
+            place = 4 * turned(outer[arc][0]) + turned(inner[arc][0])
+
+            @pl.loop(0, small - 1)
+            def _(c):
+                fac_ref[arc, place, c] = slabs[0, c, arc]
+
+            @pl.loop(0, 8 - small)
+            def _(c):
+                fac_ref[arc, place, small - 1 + c] = slabs[1, c, arc]
+
+            fac_ref[arc, place, 7] = slabs[0, small - 1, arc]
+            fac_ref[arc, place, 8] = slabs[0, 8, arc]
+            fac_ref[arc, place, 9] = slabs[1, 8 - small, arc]
+            fac_ref[arc, place, 10] = slabs[1, 8, arc]
+        s, r = gls.at[0], glr.at[0]
+        l1 = near(l_unit(0, 11), inner, s, r)
+        yield
+        arrive(l1)
+        l2 = far(l_unit(0, 6), l_unit(6, 5), inner, s, r)
+        yield
+        arrive(l2)
+        s, r = gls.at[1], glr.at[1]
+        l3 = near(l_group(0, 4), outer, s, r)
+        yield
+        arrive(l3)
+        l4 = far(l_group(0, 2), l_group(2, 2), outer, s, r)
+        yield
+        arrive(l4)
+        yield
+
+    def panel_stream(part):
+        cols = pl.ds(part * PART, PART)
+        lines = lambda base, n: pl.ds(pl.multiple_of(base, 32), n)
+
+        def m_unit(low, size):
+            return lambda arc: lambda r: rhs_ref.at[
+                arc, lines(outer[arc][0] * 256 + r * 64 + low, size), cols
+            ]
+
+        def m_group(low, size):
+            return lambda arc: lambda r: rhs_ref.at[arc, lines(r * 256 + low, size), cols]
+
+        def to_peers(source, target, ax, unit, s, r):
+            copies = []
+            for k in (1, 3, 2):
+                for arc in two:
+                    to = lax.rem(ax[arc][0] + k, 4)
+                    copies.append(
+                        remote(
+                            source.at[arc, lines(to * unit, unit), cols],
+                            target.at[arc, k - 1, :, cols],
+                            s.at[part, arc, k - 1], r.at[part, arc, k - 1], {ax[arc][1]: to},
+                        )
+                    )
+            return begin(copies)
+
+        scatter1 = to_peers(win_ref, got1, outer, 256, m1s, m1r)
+        yield
+        arrive(scatter1)
+        for arc in two:
+            own = win_ref[arc, lines(outer[arc][0] * 256, 256), cols]
+            sum1[arc, :, cols] = (own + got1[arc, 0, :, cols]) + (
+                got1[arc, 1, :, cols] + got1[arc, 2, :, cols]
+            )
+        scatter2 = to_peers(sum1, got2, inner, 64, m2s, m2r)
+        yield
+        arrive(scatter2)
+        for arc in two:
+            own = sum1[arc, lines(inner[arc][0] * 64, 64), cols]
+            sum2[arc, :, cols] = (own + got2[arc, 0, :, cols]) + (
+                got2[arc, 1, :, cols] + got2[arc, 2, :, cols]
+            )
+        across = begin(
+            [
                 remote(
-                    sum1.at[arc, pl.ds(pl.multiple_of(to * 64, 64), 64)],
-                    got2.at[arc, k - 1], m2s.at[arc, k - 1], m2r.at[arc, k - 1], {axis: to},
+                    sum2.at[arc, :, cols], gotz.at[arc, :, cols],
+                    mzs.at[part, arc], mzr.at[part, arc], {"par_0": 1 - z},
                 )
-            ])
-    arrive(l1)
-    l2 = begin(far(lambda a: l_unit(a, slice(0, 6)), lambda a: l_unit(a, slice(6, 11)), inner, 0, gls, glr))
-    arrive(scatter2)
-    across = []
-    for arc in two:
-        own = sum1[arc, pl.ds(pl.multiple_of(inner[arc][0] * 64, 64), 64), :]
-        sum2[arc] = (own + got2[arc, 0]) + (got2[arc, 1] + got2[arc, 2])
-        across += begin([remote(sum2.at[arc], gotz.at[arc], mzs.at[arc], mzr.at[arc], {"par_0": 1 - z})])
-    arrive(l2)
-    l3 = begin(near(l_group, outer, 1, gls, glr))
-    arrive(across)
-    for arc in two:
-        spot = pl.ds(pl.multiple_of(outer[arc][0] * 256 + inner[arc][0] * 64, 64), 64)
-        rhs_ref[arc, spot, :] = sum2[arc] + gotz[arc]
-    g1 = begin(near(m_unit, inner, 0, gms, gmr))
-    arrive(g1)
-    g2 = begin(far(lambda a: m_unit(a, 0, 32), lambda a: m_unit(a, 32, 32), inner, 0, gms, gmr))
-    arrive(g2)
-    g3 = begin(near(m_group, outer, 1, gms, gmr))
-    arrive(l3)
-    l4 = begin(far(lambda a: l_group(a, 0, 2), lambda a: l_group(a, 2, 2), outer, 1, gls, glr))
-    arrive(l4)
-    invert_all(0, fac_ref, inv)
-    arrive(g3)
-    g4 = begin(far(lambda a: m_group(a, 0, 128), lambda a: m_group(a, 128, 128), outer, 1, gms, gmr))
-    invert_all(1, fac_ref, inv)
-    for arc in two:
-        join_tiles(arc, fac_ref, inv, fh, wh, wl)
-    arrive(g4)
+                for arc in two
+            ]
+        )
+        yield
+        arrive(across)
+        for arc in two:
+            spot = lines(outer[arc][0] * 256 + inner[arc][0] * 64, 64)
+            rhs_ref[arc, spot, cols] = sum2[arc, :, cols] + gotz[arc, :, cols]
+        s, r = gms.at[part, 0], gmr.at[part, 0]
+        g1 = near(m_unit(0, 64), inner, s, r)
+        yield
+        arrive(g1)
+        g2 = far(m_unit(0, 32), m_unit(32, 32), inner, s, r)
+        yield
+        arrive(g2)
+        s, r = gms.at[part, 1], gmr.at[part, 1]
+        g3 = near(m_group(0, 256), outer, s, r)
+        yield
+        arrive(g3)
+        g4 = far(m_group(0, 128), m_group(128, 128), outer, s, r)
+        yield
+        arrive(g4)
+        yield
+
+    def prepare(step):
+        if step < 2:
+            invert_all(step, fac_ref, inv)
+        else:
+            for arc in two:
+                join_tiles(arc, fac_ref, inv, fh, wh, wl)
+
+    streams = {"l": factor_stream(), "a": panel_stream(0)}
+    if PARTS > 1:
+        streams["b"] = panel_stream(1)
+    for step in ORDER:
+        if step.isdigit():
+            prepare(int(step))
+        else:
+            next(streams[step])
     blocks = rhs_ref.shape[1] // OBS_STEP
     for b in range(blocks):
         solve_forward(b, rhs_ref, fh, wh, wl, yh, yl)
@@ -593,9 +641,7 @@
     arrive(forward)
     pl.loop(0, held)(lambda c: piece(c).wait_send())
     piece(8).wait_send()
-    for copy in sent + scatter2 + across + l1 + l2 + l3 + l4 + g1 + g2 + g3 + g4:
-        copy.wait_send()
-    for copy in [swap, trade] + scatter + gather + forward:
+    for copy in sent + [swap, trade]:
         copy.wait_send()
 
 
@@ -642,9 +688,9 @@
             vm((3, total // 8, 128), F32),
             vm((chips, share, width), F32),
             dma((9,)), dma((9,)),
-            dma((arcs, 3)), dma((arcs, 3)), dma((arcs, 3)), dma((arcs, 3)),
-            dma((arcs,)), dma((arcs,)),
-            dma((arcs, 2, 4)), dma((arcs, 2, 4)), dma((arcs, 2, 4)), dma((arcs, 2, 4)),
+            dma((PARTS, arcs, 3)), dma((PARTS, arcs, 3)), dma((PARTS, arcs, 3)), dma((PARTS, arcs, 3)),
+            dma((PARTS, arcs)), dma((PARTS, arcs)),
+            dma((2, arcs, 4)), dma((2, arcs, 4)), dma((PARTS, 2, arcs, 4)), dma((PARTS, 2, arcs, 4)),
             dma, dma, dma, dma, dma, dma((3,)), dma((3,)), dma((3,)), dma((3,)), dma((4,)), dma((4,)),
         ],
         compiler_params=pltpu.CompilerParams(

time: 134 us -> 129 us (0.963)
  Pallas kernels: 122 us -> 116 us
    pallas_call x1, Pallas kernels: 95.8 us -> 90.6 us  [block_and_gram(): pl.pallas_call(main_kernel, out_shape=(jax.ShapeDtypeStruct((total, 128),...]
  transfers between devices with their start and end apart: 1 -> 1, of which waited for: 0 -> 0; matrix products, arithmetic and copies ran while one was open for 0% -> 0% of each run, Pallas kernels for 14% -> 15%
where the time goes in v6:
time: 129 us
  Pallas kernels  116 us (90%)
  starting transfers between devices  6.6 us (5%)
  other arithmetic  2.98 us (2%)
  local copies, waits for them, and re-layouts  2.17 us (2%)
    pallas_call x1, Pallas kernels, block_and_gram(): pl.pallas_call(main_kernel, out_shape=(jax.ShapeDtypeStruct((total, 128),...  90.6 us
    pallas_call x1, Pallas kernels, factor_inverse(): pl.pallas_call(factor_kernel, out_shape=jax.ShapeDtypeStruct((size, size)...  18.8 us
    all_to_all x1, starting transfers between devices, on_device(): lax.all_to_all(sums, 'line', split_axis=0, concat_axis=0, tiled=True)  6.6 us
    pallas_call x1, Pallas kernels, apply_inverse(): pl.pallas_call(apply_kernel, out_shape=jax.ShapeDtypeStruct((share, size)...  3.65 us
    pallas_call x1, Pallas kernels, window_of(): pl.pallas_call(window_kernel, out_shape=jax.ShapeDtypeStruct((arcs, obser...  3.38 us
  transfers between devices with their start and end apart: 1, of which 0 were waited for; matrix products, arithmetic and copies ran while one was open for 0% of the time, Pallas kernels for 15%

profile of v6, /device:TPU:1, one launch (start us, length us, event | category | flops | bytes accessed | tf_op | source)
XLA Modules:
  0.0 128.8 jit_solution(11957587465041459400)
XLA Ops:
  0.7 0.5 iota_add_fusion
  1.2 0.9 compare_reduce_fusion
  2.1 0.9 compare_reduce_fusion.1
  3.0 0.1 and_convert_fusion
  3.0 0.6 reshape.41.on_ref
  3.7 0.1 copy.6
  3.8 0.6 reshape.40.on_ref
  4.4 3.4 %shard_map.55.win_ref = bf16[2,1024,512]{2,1,0:T(8,128)(2,1)} custom-call(s32[2]{0:T(128)} %get-tuple-element.12.at_ref, s32[4]{0:T(128)} %reshape.41.on_ref, bf16[2,1024,1280]{2,1,0:T(8,128)(2,1)} %design_hbm.1), custom_call_target="tpu_custom_call" | custom-call | tf_op jit(solution)/shard_map/pallas_call | solution.py:335
  7.7 90.6 %shard_map.56 = (f32[1280,128]{1,0:T(8,128)}, bf16[4,160,512]{2,1,0:T(8,128)(2,1)}, f32[160,512]{1,0:T(8,128)}) custom-call(s32[10]{0:T(128)} %reshape.40.on_ref, f32[2,32,1024]{2,1,0:T(8,128)} %cov_ref.1, bf16[2,1024,512]{2,1,0:T(8,128)(2,1)} %shard_map.55.win_ref, bf16[2,1024,1280]{2,1,0:T(8,128)(2,1)} %design_hbm.1), custom_call_target="tpu_custom_call" | custom-call | tf_op jit(solution)/shard_map/pallas_call | solution.py:655
  98.3 6.6 %all-to-all-start = ((bf16[4,160,512]{2,1,0:T(8,128)(2,1)}), bf16[4,160,512]{2,1,0:T(8,128)(2,1)S(1)}, u32[]{:S(2)}, u32[]{:S(2)}) async-start(bf16[4,160,512]{2,1,0:T(8,128)(2,1)} %get-tuple-element.8), calls=%async_computation | async-start | bytes 1310720 | tf_op jit(solution)/shard_map/all_to_all | solution.py:728
  104.9 0.6 pad_add_fusion.at_ref
  105.5 18.8 %shard_map.57.inverse_ref = f32[512,512]{1,0:T(8,128)} custom-call(s32[3]{0:T(128)} %pad_add_fusion.at_ref, f32[1280,128]{1,0:T(8,128)} %get-tuple-element.10.block_ref, f32[80,1,512]{2,1,0:T(1,128)} %bitcast.8), custom_call_target="tpu_custom_call" | custom-call | flops 30000001024 | bytes 60000000 | tf_op jit(solution)/shard_map/pallas_call | solution.py:280
  124.3 0.0 all-to-all-done.arrived_ref
  124.3 0.0 copy-start
  124.3 0.9 copy-done
  125.2 3.7 %shard_map.58 = f32[160,512]{1,0:T(8,128)} custom-call(s32[3]{0:T(128)} %pad_add_fusion.at_ref, bf16[4,160,512]{2,1,0:T(8,128)(2,1)} %copy-done, f32[160,512]{1,0:T(8,128)} %get-tuple-element.9.own_ref, f32[512,512]{1,0:T(8,128)} %shard_map.57.inverse_ref, f32[80,1,512]{2,1,0:T(1,128)} %bitcast.9), custom_call_target="tpu_custom_call" | custom-call | tf_op jit(solution)/shard_map/pallas_call | solution.py:306
  (3 shorter events, 0.0 us)
Async XLA Ops:
  98.3 26.0 %all-to-all-start = ((bf16[4,160,512]{2,1,0:T(8,128)(2,1)}), bf16[4,160,512]{2,1,0:T(8,128)(2,1)S(1)}, u32[]{:S(2)}, u32[]{:S(2)}) async-start(bf16[4,160,512]{2,1,0:T(8,128)(2,1)} %get-tuple-element.8), calls=%async_computation | async-start | bytes 1310720 | tf_op jit(solution)/shard_map/all_to_all | solution.py:728
  124.3 0.9 copy-start

commit v7 on v6

--- a/solution.py
+++ b/solution.py
@@ -228,97 +228,38 @@
 
 def factor_and_invert(work):
     size = work.shape[0]
+    width = size + 128
     flip = ((0,), (0,))
-    for k in range(size // 128):
+    at = lambda base, n: pl.ds(pl.multiple_of(base, 128), n)
+
+    @pl.loop(0, size // 128)
+    def _(k):
         c0 = k * 128
-        width = size + 128 + c0
+        wide = at(c0, width)
         for q in range(4):
-            r = c0 + q * 32
+            top = lambda g, n: pl.ds(pl.multiple_of(c0 + q * 32 + 8 * g, 8), n)
             panel = [
-                [work[r + 8 * g : r + 8 * g + 8, c : c + 128] for c in range(c0, width, 128)]
-                for g in range(4)
+                [work[top(g, 8), at(c0 + c, 128)] for c in range(0, width, 128)] for g in range(4)
             ]
             done = eliminate(panel, q * 32)
-            work[r : r + 32, c0:width] = done
+            work[top(0, 32), wide] = done
             if q < 3:
                 a, b = split_rows(done)
                 less = dot_by(a[:, 0:128], b, flip)
-                work[r + 32 : c0 + 128, c0:width] -= less[q * 32 + 32 : 128]
-        if c0 + 128 < size:
-            a, b = split_rows(work[c0 : c0 + 128, c0:width])
-            for i in range(c0 + 128, size, 128):
-                work[i : i + 128, i:width] -= dot_by(
-                    a[:, i - c0 : i - c0 + 128], b[:, i - c0 :], flip
-                )
+                work[top(4, 96 - q * 32), wide] -= less[q * 32 + 32 : 128]
+
+        @pl.when(k < size // 128 - 1)
+        def _():
+            _, b = split_rows(work[at(c0, 128), wide])
+
+            @pl.loop(k + 1, size // 128)
+            def _(i):
+                a, _ = split_rows(work[at(c0, 128), at(i * 128, 128)])
+                work[at(i * 128, 128), wide] -= dot_by(a, b, flip)
 
 
 def tile_list(size):
     return [(i, j) for i in range(size // 128) for j in range(i, size // 128)]
-
-
-def factor_kernel(at_ref, block_ref, reg_ref, out_ref, work):
-    size = out_ref.shape[0]
-    square = (128, 128)
-    eye = lanes(square) == rows_of(square)
-    work[:, size:] = jnp.zeros((size, size), F32)
-    for at, (i, j) in enumerate(tile_list(size)):
-        value = block_ref[at * 128 : at * 128 + 128, :]
-        if i == j:
-            value = value + jnp.where(eye, reg_ref[0, :, i * 128 : i * 128 + 128], 0.0)
-            work[i * 128 : i * 128 + 128, size + i * 128 : size + i * 128 + 128] = jnp.where(eye, 1.0, 0.0)
-        work[i * 128 : i * 128 + 128, j * 128 : j * 128 + 128] = value
-    factor_and_invert(work)
-    out_ref[...] = work[:, size:]
-
-
-def whole(shape):
-    return pl.BlockSpec(shape, lambda i, at: (0,) * len(shape))
-
-
-def factor_inverse(at, block, reg):
-    size = reg.shape[-1]
-    return pl.pallas_call(
-        factor_kernel,
-        out_shape=jax.ShapeDtypeStruct((size, size), F32),
-        grid_spec=pltpu.PrefetchScalarGridSpec(
-            num_scalar_prefetch=1,
-            grid=(1,),
-            in_specs=[whole(block.shape), pl.BlockSpec((1, 1, size), lambda i, at: (at[0], 0, 0))],
-            out_specs=whole((size, size)),
-            scratch_shapes=[pltpu.VMEM((size, 2 * size), F32)],
-        ),
-        compiler_params=pltpu.CompilerParams(vmem_limit_bytes=KERNEL_VMEM),
-        cost_estimate=pl.CostEstimate(flops=30_000_000_000, bytes_accessed=60_000_000, transcendentals=0),
-    )(at, block, reg)
-
-
-def apply_kernel(at_ref, arrived_ref, own_ref, inverse_ref, reg_ref, out_ref):
-    total = own_ref[...]
-    for part in range(arrived_ref.shape[0]):
-        total = total + jnp.where(at_ref[2] == part, 0.0, arrived_ref[part].astype(F32))
-    on = rows_of(total.shape) + at_ref[1] == lanes(total.shape)
-    total = total + jnp.where(on, reg_ref[0], 0.0)
-    out_ref[...] = dot3(halves(total), halves(inverse_ref[...]), ((1,), (1,)))
-
-
-def apply_inverse(at, arrived, own, inverse, reg):
-    share, size = own.shape
-    return pl.pallas_call(
-        apply_kernel,
-        out_shape=jax.ShapeDtypeStruct((share, size), F32),
-        grid_spec=pltpu.PrefetchScalarGridSpec(
-            num_scalar_prefetch=1,
-            grid=(1,),
-            in_specs=[
-                whole(arrived.shape),
-                whole(own.shape),
-                whole(inverse.shape),
-                pl.BlockSpec((1, 1, size), lambda i, at: (at[0], 0, 0)),
-            ],
-            out_specs=whole((share, size)),
-        ),
-        compiler_params=pltpu.CompilerParams(vmem_limit_bytes=KERNEL_VMEM),
-    )(at, arrived, own, inverse, reg)
 
 
 def window_kernel(at_ref, on_ref, design_ref, out_ref):
@@ -379,11 +320,11 @@
 
 
 def main_kernel(
-    on_ref, cov_ref, win_ref, design_hbm, out_ref, sum_ref, own_ref,
+    at_ref, on_ref, cov_ref, win_ref, reg_ref, design_hbm, final_ref,
     fac_ref, rhs_ref, slabs, got1, got2, gotz, sum1, sum2, inv, fh, wh, wl, yh, yl, qh, ql, design_ref,
-    part_ref, gram, kept, mate, got, pair,
+    part_ref, gram, kept, mate, got, pair, out_ref, sum_ref, own_ref, arrived, work,
     ls, lr, m1s, m1r, m2s, m2r, mzs, mzr, gls, glr, gms, gmr,
-    ds, ps, pr, qs, qr, rs, rr, gs, gr, fs, fr,
+    ds, ps, pr, qs, qr, rs, rr, gs, gr, fs, fr, es, er,
 ):
     z, x, y = (lax.axis_index(name) for name in ("par_0", "par_1", "par_2"))
     chip, core = lax.axis_index("line"), lax.axis_index("core")
@@ -637,15 +578,39 @@
     trade.wait_recv()
     for c in range(4):
         sum_ref[c] = (gram[c, core] + pair[c]).astype(BF)
+    exchange = begin([
+        remote(sum_ref.at[c], arrived.at[k], es.at[k], er.at[k], peer)
+        for k, (c, peer) in enumerate(zip(chips, peers))
+    ])
     own_ref[...] = gram[chip, core] + pair[chip]
+    reg = reg_ref[at_ref[0]]
+    square = (128, 128)
+    eye = lanes(square) == rows_of(square)
+    work[...] = jnp.zeros_like(work)
     arrive(forward)
+    for at, (i, j) in enumerate(tile_list(width)):
+        value = out_ref[at * 128 : at * 128 + 128, :]
+        if i == j:
+            value = value + jnp.where(eye, reg[:, i * 128 : i * 128 + 128], 0.0)
+            work[i * 128 : i * 128 + 128, width + i * 128 : width + i * 128 + 128] = jnp.where(
+                eye, 1.0, 0.0
+            )
+        work[i * 128 : i * 128 + 128, j * 128 : j * 128 + 128] = value
+    factor_and_invert(work)
+    arrive(exchange)
+    total = own_ref[...]
+    for k in range(3):
+        total = total + arrived[k].astype(F32)
+    first = ((z * 4 + x) * 4 + y) * columns + (chip * 2 + core) * share - at_ref[0] * width
+    total = total + jnp.where(rows_of(total.shape) + first == lanes(total.shape), reg, 0.0)
+    final_ref[...] = dot3(halves(total), halves(work[:, width:]), ((1,), (1,)))
     pl.loop(0, held)(lambda c: piece(c).wait_send())
     piece(8).wait_send()
     for copy in sent + [swap, trade]:
         copy.wait_send()
 
 
-def block_and_gram(on, cov, window, design):
+def solve_panel(at, on, cov, window, reg, design):
     arcs, lines, size = cov.shape
     _, observed, width = window.shape
     chips = 4
@@ -654,15 +619,11 @@
     vm, dma = pltpu.VMEM, pltpu.SemaphoreType.DMA
     return pl.pallas_call(
         main_kernel,
-        out_shape=(
-            jax.ShapeDtypeStruct((total, 128), F32),
-            jax.ShapeDtypeStruct((chips, share, width), BF),
-            jax.ShapeDtypeStruct((share, width), F32),
-        ),
-        in_specs=[pl.BlockSpec(memory_space=pltpu.SMEM)]
-        + [pl.BlockSpec(memory_space=vm)] * 2
+        out_shape=jax.ShapeDtypeStruct((share, width), F32),
+        in_specs=[pl.BlockSpec(memory_space=pltpu.SMEM)] * 2
+        + [pl.BlockSpec(memory_space=vm)] * 3
         + [pl.BlockSpec(memory_space=pl.ANY)],
-        out_specs=(pl.BlockSpec(memory_space=vm),) * 3,
+        out_specs=pl.BlockSpec(memory_space=vm),
         scratch_shapes=[
             vm((arcs, 16, 11, lines, 128), BF),
             vm((arcs, size, width), BF),
@@ -687,16 +648,22 @@
             vm((total // 2, 128), F32),
             vm((3, total // 8, 128), F32),
             vm((chips, share, width), F32),
+            vm((total, 128), F32),
+            vm((chips, share, width), BF),
+            vm((share, width), F32),
+            vm((chips - 1, share, width), BF),
+            vm((width, 2 * width), F32),
             dma((9,)), dma((9,)),
             dma((PARTS, arcs, 3)), dma((PARTS, arcs, 3)), dma((PARTS, arcs, 3)), dma((PARTS, arcs, 3)),
             dma((PARTS, arcs)), dma((PARTS, arcs)),
             dma((2, arcs, 4)), dma((2, arcs, 4)), dma((PARTS, 2, arcs, 4)), dma((PARTS, 2, arcs, 4)),
             dma, dma, dma, dma, dma, dma((3,)), dma((3,)), dma((3,)), dma((3,)), dma((4,)), dma((4,)),
+            dma((3,)), dma((3,)),
         ],
         compiler_params=pltpu.CompilerParams(
             vmem_limit_bytes=KERNEL_VMEM, collective_id=0, has_side_effects=True
         ),
-    )(on, cov, window, design)
+    )(at, on, cov, window, reg, design)
 
 
 PANEL = 512
@@ -708,8 +675,6 @@
     arcs, observed, columns = design.shape
     local_blocks = columns // BLK
     par_id = lax.axis_index(PAR)
-    chip, core = lax.axis_index("line"), lax.axis_index("core")
-    start = panel_index[0] * PANEL
     block_ids = par_id * local_blocks + jnp.arange(local_blocks, dtype=jnp.int32)
     hits = jnp.any(active_blocks[:, :, None] == block_ids[None, None, :], axis=1)
     parts = jnp.arange(PANEL // BLK, dtype=jnp.int32)
@@ -722,15 +687,9 @@
         (inside[:, None] & active).astype(jnp.int32).reshape(-1),
         design,
     )
-    share = columns // (4 * 2)
     on = hits.T.astype(jnp.int32).reshape(-1)
-    block, sums, own = block_and_gram(on, cov_factor, window, design)
-    arrived = lax.all_to_all(sums, "line", split_axis=0, concat_axis=0, tiled=True)
     reg = reg_diag.reshape(-1, 1, PANEL)
-    shift = par_id * columns + (chip * 2 + core) * share - start
-    at = jnp.stack([panel_index[0], shift, chip]).astype(jnp.int32)
-    inverse = factor_inverse(at, block, reg)
-    return apply_inverse(at, arrived, own, inverse, reg).T
+    return solve_panel(panel_index, on, cov_factor, window, reg, design).T
 
 
 def solution(mesh):

time: 129 us -> 118 us (0.915)
  starting transfers between devices: 6.6 us -> 0 us
  Pallas kernels: 116 us -> 112 us
    all_to_all x1 -> x0, starting transfers between devices: 6.6 us -> none  [on_device(): lax.all_to_all(sums, 'line', split_axis=0, concat_axis=0, tiled=True)]
    pallas_call x3 -> x1, Pallas kernels: 113 us -> 108 us  [solve_panel(): pl.pallas_call(main_kernel, out_shape=jax.ShapeDtypeStruct((share, width)...]
  transfers between devices with their start and end apart: 1 -> 0, of which waited for: 0 -> 0; matrix products, arithmetic and copies ran while one was open for 0% -> 0% of each run, Pallas kernels for 15% -> 0%
where the time goes in v7:
time: 118 us
  Pallas kernels  112 us (95%)
  local copies, waits for them, and re-layouts  3.04 us (3%)
  other arithmetic  2.37 us (2%)
    pallas_call x1, Pallas kernels, solve_panel(): pl.pallas_call(main_kernel, out_shape=jax.ShapeDtypeStruct((share, width)...  108 us
    pallas_call x1, Pallas kernels, window_of(): pl.pallas_call(window_kernel, out_shape=jax.ShapeDtypeStruct((arcs, obser...  3.38 us

profile of v7, /device:TPU:1, one launch (start us, length us, event | category | flops | bytes accessed | tf_op | source)
XLA Modules:
  0.0 117.9 jit_solution(691258806799231979)
XLA Ops:
  0.7 0.9 compare_reduce_fusion
  1.5 0.5 iota_add_fusion
  2.1 0.9 compare_reduce_fusion.1
  3.0 0.1 and_convert_fusion
  3.0 0.6 reshape.39.on_ref
  3.7 0.1 copy.6
  3.8 0.6 reshape.38.on_ref
  4.4 3.4 %shard_map.55.win_ref = bf16[2,1024,512]{2,1,0:T(8,128)(2,1)} custom-call(s32[2]{0:T(128)} %get-tuple-element.6.at_ref, s32[4]{0:T(128)} %reshape.39.on_ref, bf16[2,1024,1280]{2,1,0:T(8,128)(2,1)} %design_hbm.1), custom_call_target="tpu_custom_call" | custom-call | tf_op jit(solution)/shard_map/pallas_call | solution.py:276
  7.7 108.4 %shard_map.56 = f32[160,512]{1,0:T(8,128)} custom-call(s32[1]{0:T(128)S(6)} %copy.8.at_ref, s32[10]{0:T(128)} %reshape.38.on_ref, f32[2,32,1024]{2,1,0:T(8,128)} %cov_ref.1, bf16[2,1024,512]{2,1,0:T(8,128)(2,1)} %shard_map.55.win_ref, f32[80,1,512]{2,1,0:T(1,128)} %bitcast.6, bf16[2,1024,1280]{2,1,0:T(8,128)(2,1)} %design_hbm.1), custom_call_target="tpu_custom_call" | custom-call | tf_op jit(solution)/shard_map/pallas_call | solution.py:620
  116.2 1.7 %copy.9 = f32[512,160]{0,1:T(8,128)} copy(f32[512,160]{0,1:T(8,128)} %bitcast.5) | data formatting | bytes 655360
  (3 shorter events, 0.0 us)

commit v8 on v7

--- a/solution.py
+++ b/solution.py
@@ -262,30 +262,6 @@
     return [(i, j) for i in range(size // 128) for j in range(i, size // 128)]
 
 
-def window_kernel(at_ref, on_ref, design_ref, out_ref):
-    part = pl.program_id(0)
-    for arc in range(out_ref.shape[0]):
-        on = on_ref[part * out_ref.shape[0] + arc] > 0
-        out_ref[arc] = jnp.where(on, design_ref[arc], jnp.zeros((), BF))
-
-
-def window_of(at, on, design):
-    arcs, observed, _ = design.shape
-    parts = at.shape[0]
-    block = (arcs, observed, BLK)
-    return pl.pallas_call(
-        window_kernel,
-        out_shape=jax.ShapeDtypeStruct((arcs, observed, parts * BLK), BF),
-        grid_spec=pltpu.PrefetchScalarGridSpec(
-            num_scalar_prefetch=2,
-            grid=(parts,),
-            in_specs=[pl.BlockSpec(block, lambda i, at, on: (0, 0, at[i]))],
-            out_specs=pl.BlockSpec(block, lambda i, at, on: (0, 0, i)),
-        ),
-        compiler_params=pltpu.CompilerParams(vmem_limit_bytes=KERNEL_VMEM),
-    )(at, on, design)
-
-
 MESH = pl.DeviceIdType.MESH
 
 
@@ -320,7 +296,7 @@
 
 
 def main_kernel(
-    at_ref, on_ref, cov_ref, win_ref, reg_ref, design_hbm, final_ref,
+    at_ref, active_ref, cov_ref, reg_ref, design_hbm, final_ref, win_ref,
     fac_ref, rhs_ref, slabs, got1, got2, gotz, sum1, sum2, inv, fh, wh, wl, yh, yl, qh, ql, design_ref,
     part_ref, gram, kept, mate, got, pair, out_ref, sum_ref, own_ref, arrived, work,
     ls, lr, m1s, m1r, m2s, m2r, mzs, mzr, gls, glr, gms, gmr,
@@ -505,10 +481,38 @@
             for arc in two:
                 join_tiles(arc, fac_ref, inv, fh, wh, wl)
 
+    place_of_device = (z * 4 + x) * 4 + y
+
+    def active(*ids):
+        found = jnp.ones(active_ref.shape, F32)
+        for one in ids:
+            found = found * jnp.where(active_ref[...] == one, 1.0, 0.0)
+        return [jnp.sum(found[arc : arc + 1], axis=1, keepdims=True) for arc in two]
+
+    def cut_window():
+        load.wait()
+        many = design_ref.shape[2] // BLK
+        for part in range(win_ref.shape[2] // BLK):
+            wanted = at_ref[0] * (win_ref.shape[2] // BLK) + part
+            marks = [active(wanted, place_of_device * many + block) for block in range(many)]
+            for arc in two:
+                marks_here = [mark[arc].astype(BF) for mark in marks]
+
+                @pl.loop(0, design_ref.shape[1] // 128)
+                def _(step):
+                    spot = pl.ds(pl.multiple_of(step * 128, 128), 128)
+                    total = design_ref[arc, spot, 0:BLK] * marks_here[0]
+                    for block in range(1, many):
+                        low = block * BLK
+                        total = total + design_ref[arc, spot, low : low + BLK] * marks_here[block]
+                    win_ref[arc, spot, part * BLK : part * BLK + BLK] = total
+
     streams = {"l": factor_stream(), "a": panel_stream(0)}
     if PARTS > 1:
         streams["b"] = panel_stream(1)
-    for step in ORDER:
+    for at, step in enumerate(ORDER):
+        if at == 1:
+            cut_window()
         if step.isdigit():
             prepare(int(step))
         else:
@@ -530,9 +534,8 @@
     def product(block):
         flip = ((0,), (0,))
         total = jnp.zeros((BLK, width), F32)
-        for arc in range(arcs):
+        for arc, on in zip(two, active(place_of_device * (columns // BLK) + block)):
             piece = design_ref[arc, :, block * BLK : block * BLK + BLK]
-            on = on_ref[block * arcs + arc].astype(F32)
             one = dot_by(piece, qh[arc], flip) + dot_by(piece, ql[arc], flip)
             total = total + one * on
         low = block * BLK
@@ -554,7 +557,6 @@
                 for k, (c, peer) in enumerate(zip(chips, peers))
             ])
     solve_back(0, fh, wh, wl, yh, yl, qh, ql)
-    load.wait()
     product(0)
     product(1)
     arrive(scatter)
@@ -601,7 +603,7 @@
     total = own_ref[...]
     for k in range(3):
         total = total + arrived[k].astype(F32)
-    first = ((z * 4 + x) * 4 + y) * columns + (chip * 2 + core) * share - at_ref[0] * width
+    first = place_of_device * columns + (chip * 2 + core) * share - at_ref[0] * width
     total = total + jnp.where(rows_of(total.shape) + first == lanes(total.shape), reg, 0.0)
     final_ref[...] = dot3(halves(total), halves(work[:, width:]), ((1,), (1,)))
     pl.loop(0, held)(lambda c: piece(c).wait_send())
@@ -610,9 +612,9 @@
         copy.wait_send()
 
 
-def solve_panel(at, on, cov, window, reg, design):
+def solve_panel(at, active, cov, reg, design):
     arcs, lines, size = cov.shape
-    _, observed, width = window.shape
+    width = reg.shape[2]
     chips = 4
     share = design.shape[2] // (2 * chips)
     total = len(tile_list(width)) * 128
@@ -620,11 +622,12 @@
     return pl.pallas_call(
         main_kernel,
         out_shape=jax.ShapeDtypeStruct((share, width), F32),
-        in_specs=[pl.BlockSpec(memory_space=pltpu.SMEM)] * 2
+        in_specs=[pl.BlockSpec(memory_space=pltpu.SMEM)]
         + [pl.BlockSpec(memory_space=vm)] * 3
         + [pl.BlockSpec(memory_space=pl.ANY)],
         out_specs=pl.BlockSpec(memory_space=vm),
         scratch_shapes=[
+            vm((arcs, size, width), BF),
             vm((arcs, 16, 11, lines, 128), BF),
             vm((arcs, size, width), BF),
             vm((2, 9, arcs, lines, 128), BF),
@@ -663,7 +666,7 @@
         compiler_params=pltpu.CompilerParams(
             vmem_limit_bytes=KERNEL_VMEM, collective_id=0, has_side_effects=True
         ),
-    )(at, on, cov, window, reg, design)
+    )(at, active, cov, reg, design)
 
 
 PANEL = 512
@@ -672,24 +675,8 @@
 
 
 def on_device(design, cov_factor, active_blocks, panel_index, reg_diag):
-    arcs, observed, columns = design.shape
-    local_blocks = columns // BLK
-    par_id = lax.axis_index(PAR)
-    block_ids = par_id * local_blocks + jnp.arange(local_blocks, dtype=jnp.int32)
-    hits = jnp.any(active_blocks[:, :, None] == block_ids[None, None, :], axis=1)
-    parts = jnp.arange(PANEL // BLK, dtype=jnp.int32)
-    wanted = panel_index[0] * (PANEL // BLK) + parts
-    local = wanted - par_id * local_blocks
-    inside = (local >= 0) & (local < local_blocks)
-    active = jnp.any(active_blocks[None] == wanted[:, None, None], axis=2)
-    window = window_of(
-        jnp.clip(local, 0, local_blocks - 1),
-        (inside[:, None] & active).astype(jnp.int32).reshape(-1),
-        design,
-    )
-    on = hits.T.astype(jnp.int32).reshape(-1)
     reg = reg_diag.reshape(-1, 1, PANEL)
-    return solve_panel(panel_index, on, cov_factor, window, reg, design).T
+    return solve_panel(panel_index, active_blocks, cov_factor, reg, design).T
 
 
 def solution(mesh):

time: 118 us -> 111 us (0.941)
  Pallas kernels: 112 us -> 108 us
  other arithmetic: 2.37 us -> 0 us
  local copies, waits for them, and re-layouts: 3.04 us -> 1.72 us
    pallas_call x1 -> x0, Pallas kernels: 3.38 us -> none  [window_of(): pl.pallas_call(window_kernel, out_shape=jax.ShapeDtypeStruct((arcs, obser...]
    reduce_or x2 -> x0, other arithmetic: 1.75 us -> none  [the longest x1 0.89 us: on_device(): active = jnp.any(active_blocks[None] == wanted[:, None, None], axis=2)]
where the time goes in v8:
time: 111 us
  Pallas kernels  108 us (97%)
  local copies, waits for them, and re-layouts  1.72 us (2%)
    pallas_call x1, Pallas kernels, solve_panel(): pl.pallas_call(main_kernel, out_shape=jax.ShapeDtypeStruct((share, width)...  108 us

profile of v8, /device:TPU:1, one launch (start us, length us, event | category | flops | bytes accessed | tf_op | source)
XLA Modules:
  0.0 110.7 jit_solution(16404757999750287662)
XLA Ops:
  0.7 108.3 %shard_map.55 = f32[160,512]{1,0:T(8,128)} custom-call(s32[1]{0:T(128)S(6)} %copy.7.at_ref, s32[2,80]{1,0:T(2,128)} %active_ref.1, f32[2,32,1024]{2,1,0:T(8,128)} %cov_ref.1, f32[80,1,512]{2,1,0:T(1,128)} %bitcast.3, bf16[2,1024,1280]{2,1,0:T(8,128)(2,1)} %design_hbm.1), custom_call_target="tpu_custom_call" | custom-call | tf_op jit(solution)/shard_map/pallas_call | solution.py:622
  109.0 1.7 %copy.8 = f32[512,160]{0,1:T(8,128)} copy(f32[512,160]{0,1:T(8,128)} %bitcast.2) | data formatting | bytes 655360
